TPU v7x, 256 devices: a whole 4x4x8 slice. The times are simulated.
256 devices in a mesh: section: 32 (over y, z_hi, core), tensor: 8 (over x, z_lo).
Axes of the slice: x: 4, y: 4, z: 8 (z_hi: 4, z_lo: 2; z = z_hi * 2 + z_lo), core: 2. Of those that a mesh axis runs over, the one named last changes fastest.
Arguments:
- inflow: float32 [32, 256, 4096], P('section', 'tensor'), may hold values from -6 to 6
- fresh: float32 [256, 4096], P('tensor'), may hold values from -6 to 6
- states: float32 [32, 8, 256, 256], P('section', 'tensor'), may hold values from -1.5 to 1.5
- rates: float32 [32, 8], P('section', 'tensor'), may hold values from 0.00024414062 to 0.03125
- norm_gain: float32 [32, 4096], P('section'), may hold values from 0.1 to 1.9
- w_query: bfloat16 [32, 4096, 2048], P('section', None, 'tensor'), may hold values from -0.09375 to 0.09375
- w_key: bfloat16 [32, 4096, 2048], P('section', None, 'tensor'), may hold values from -0.09375 to 0.09375
- w_value: bfloat16 [32, 4096, 2048], P('section', None, 'tensor'), may hold values from -0.09375 to 0.09375
- w_gate: bfloat16 [32, 4096, 2048], P('section', None, 'tensor'), may hold values from -0.09375 to 0.09375
- w_out: bfloat16 [32, 2048, 4096], P('section', 'tensor'), may hold values from -0.125 to 0.125
Outputs:
- outflow: float32 [32, 256, 4096], P('section', 'tensor')
- final_states: float32 [32, 8, 256, 256], P('section', 'tensor')
All inputs are finite; a program needn't handle non-finite values.
Results may differ from a plain program's by a relative error of at most 0.02.
Values may be sent and summed in bfloat16 or wider, within the bound.
No kernel may reach another device: no remote copies, remote signals or barrier semaphores. Data moves between devices by JAX's collectives and lax.ppermute only.
A program may use at most 128 MiB of HBM per device.

v0:
```python
import jax
import jax.numpy as jnp
from jax import lax
from jax.sharding import PartitionSpec as P

EPSILON = 1e-05


def from_behind(value, axis, steps):
    count = lax.axis_size(axis)
    leading, last = (max(0, -steps), min(count, count - steps))
    return lax.ppermute(value, axis, [(source, source + steps) for source in range(leading, last)])


def layer_norm(token_rows, gain_values):
    centred = token_rows - jnp.mean(token_rows, axis=-1, keepdims=True)
    spread = jnp.mean(centred * centred, axis=-1, keepdims=True)
    return (centred * lax.rsqrt(spread + EPSILON) * gain_values).astype(jnp.bfloat16)


def project(normed, query_weight, key_weight, value_weight, gate_weight):
    return jnp.concatenate(
        [
            jnp.dot(normed, query_weight, preferred_element_type=jnp.float32),
            jnp.dot(normed, key_weight, preferred_element_type=jnp.float32),
            jnp.dot(normed, value_weight, preferred_element_type=jnp.float32),
            jnp.dot(normed, gate_weight, preferred_element_type=jnp.float32),
        ],
        axis=1,
    )


def retain(projected, state_now, rate_values, key_size, value_size):
    head_count = rate_values.shape[0]
    group_len = projected.shape[0]
    key_width = head_count * key_size
    value_width = head_count * value_size
    queries = projected[:, :key_width].astype(jnp.bfloat16).reshape(group_len, head_count, key_size)
    keys = (
        (projected[:, key_width : 2 * key_width] * key_size ** (-0.5))
        .astype(jnp.bfloat16)
        .reshape(group_len, head_count, key_size)
    )
    values = (
        projected[:, 2 * key_width : 2 * key_width + value_width]
        .astype(jnp.bfloat16)
        .reshape(group_len, head_count, value_size)
    )
    gates = projected[:, 2 * key_width + value_width :]
    log_keep = jnp.log1p(-rate_values)
    positions = jnp.arange(group_len).astype(jnp.float32)
    offsets = positions[:, None] - positions[None, :]
    decay_mask = jnp.where(
        offsets[None] >= 0, jnp.exp(jnp.maximum(offsets, 0.0)[None] * log_keep[:, None, None]), 0.0
    )
    scores = jnp.einsum("ihd,jhd->hij", queries, keys, preferred_element_type=jnp.float32)
    weighted = (scores * decay_mask).astype(jnp.bfloat16)
    inner = jnp.einsum("hij,jhe->ihe", weighted, values, preferred_element_type=jnp.float32)
    carried = jnp.einsum(
        "ihd,hde->ihe", queries.astype(jnp.float32), state_now, precision=lax.Precision.HIGHEST
    )
    carried = carried * jnp.exp((positions + 1.0)[:, None] * log_keep[None, :])[:, :, None]
    mixed = inner + carried
    centred = mixed - jnp.mean(mixed, axis=-1, keepdims=True)
    head_out = centred * lax.rsqrt(jnp.mean(centred * centred, axis=-1, keepdims=True) + EPSILON)
    gated = (
        (jax.nn.silu(gates).reshape(group_len, head_count, value_size) * head_out)
        .reshape(group_len, value_width)
        .astype(jnp.bfloat16)
    )
    tail = jnp.exp((group_len - 1.0 - positions)[:, None] * log_keep[None, :])
    new_state = jnp.exp(group_len * log_keep)[:, None, None] * state_now + jnp.einsum(
        "jhd,jhe->hde",
        keys.astype(jnp.float32) * tail[:, :, None],
        values.astype(jnp.float32),
        precision=lax.Precision.HIGHEST,
    )
    return (gated, new_state)


def body(inflow, fresh, states, rates, norm_gain, w_query, w_key, w_value, w_gate, w_out):
    key_size = states.shape[2]
    value_size = states.shape[3]
    slice_rows = fresh.shape[0]
    gain_here = norm_gain[0]
    rate_here = rates[0]
    state_now = states[0]
    out_here = w_out[0]
    first_section = lax.axis_index("section") == 0
    whole_in, whole_fresh = (
        lax.all_gather(inflow[0], "tensor", axis=0, tiled=True),
        lax.all_gather(fresh, "tensor", axis=0, tiled=True),
    )
    entering = whole_in
    token_rows = inflow[0]
    for turn_index in range(2):
        projected = project(
            layer_norm(entering, gain_here), w_query[0], w_key[0], w_value[0], w_gate[0]
        )
        gated, state_now = retain(projected, state_now, rate_here, key_size, value_size)
        own_rows = lax.dynamic_slice_in_dim(
            entering, lax.axis_index("tensor") * slice_rows, slice_rows, 0
        )
        token_rows = own_rows + lax.psum_scatter(
            jnp.dot(gated, out_here, preferred_element_type=jnp.float32).astype(jnp.bfloat16),
            "tensor",
            scatter_dimension=0,
            tiled=True,
        ).astype(jnp.float32)
        if turn_index == 0:
            whole_rows = lax.all_gather(
                token_rows.astype(jnp.bfloat16), "tensor", axis=0, tiled=True
            ).astype(token_rows.dtype)
            arrived = from_behind(whole_rows.astype(jnp.bfloat16), "section", 1).astype(
                whole_rows.dtype
            )
            entering = jnp.where(first_section, whole_fresh, arrived)
    return (token_rows[None], state_now[None])


def solution(mesh):
    in_specs = (
        P("section", "tensor", None),
        P("tensor", None),
        P("section", "tensor", None, None),
        P("section", "tensor"),
        P("section", None),
        P("section", None, "tensor"),
        P("section", None, "tensor"),
        P("section", None, "tensor"),
        P("section", None, "tensor"),
        P("section", "tensor", None),
    )
    out_specs = (P("section", "tensor", None), P("section", "tensor", None, None))
    return jax.shard_map(body, mesh=mesh, in_specs=in_specs, out_specs=out_specs, check_vma=False)
```

profile of v0, /device:TPU:88, one launch (start us, length us, event | category | flops | bytes accessed | tf_op | source)
XLA Modules:
  0.0 445.4 jit_solution(2505309495923296433)
XLA Ops:
  7.2 0.7 all-gather.9.cloned.1.call-update
  8.7 96.5 %all-gather.9.cloned.1.call-done = f32[1,256,4096]{2,1,0:T(8,128)} async-done(((f32[1,32,4096]{2,1,0:T(8,128)}), f32[1,256,4096]{2,1,0:T(8,128)}) %all-gather.9.cloned.1.call-update) | async-done | bytes 4194320 | tf_op jit(solution)/shard_map/all_gather | solution.py:91
  105.1 2.5 reduce_sum.72
  107.6 2.9 multiply_reduce_fusion.1
  111.1 0.8 multiply_convert_fusion.1
  111.8 0.8 copy-done.7
  112.7 0.7 fusion.32
  113.4 1.6 copy-done.9
  115.0 0.7 fusion.37
  115.7 0.9 copy-done.11
  116.6 0.7 fusion.43
  118.3 5.9 %convolution_convert_fusion.1 = bf16[256,4096]{1,0:T(8,128)(2,1)} fusion(bf16[1,256,4096]{2,1,0:T(8,128)(2,1)S(1)} %copy-done, bf16[256,4096]{1,0:T(8,128)(2,1)} %copy-done.4, bf16[1,4096,256]{2,1,0:T(8,128)(2,1)} %param.18, f32[1,256,256]{1,2,0:T(8,128)S(1)} %get-tuple-element.5, f32[256]{0:T(256)S(1)} %add_rsqrt_fusion.2, f32[256]{0:T(256)S(1)} %broadcast_multiply_fusion.1), kind=kOutput, calls=%fused_computation.1 | convolution fusion | flops 1075314688 | bytes 8652800 | tf_op jit(solution)/shard_map/dot_general | solution.py:105
  124.3 55.1 %reduce-scatter.3.cloned.1.call-done = bf16[32,4096]{1,0:T(8,128)(2,1)} async-done(((bf16[256,4096]{1,0:T(8,128)(2,1)}), bf16[32,4096]{1,0:T(8,128)(2,1)}) %reduce-scatter.3.cloned.1.call-update) | async-done | bytes 262160 | tf_op jit(solution)/shard_map/reduce_scatter | solution.py:104
  179.4 1.9 fusion.49
  181.3 0.5 all-gather.5.cloned.1.call-update
  181.9 53.9 %all-gather.7.cloned.1.call-done = bf16[256,4096]{1,0:T(8,128)(2,1)} async-done(((bf16[32,4096]{1,0:T(8,128)(2,1)}), bf16[256,4096]{1,0:T(8,128)(2,1)}) %all-gather.7.cloned.1.call-update) | async-done | bytes 2097168 | tf_op jit(solution)/shard_map/all_gather | solution.py:111
  235.8 2.1 collective-permute-start
  238.4 124.7 %all-gather.5.cloned.1.call-done = f32[256,4096]{1,0:T(8,128)} async-done(((f32[32,4096]{1,0:T(8,128)}), f32[256,4096]{1,0:T(8,128)}) %all-gather.5.cloned.1.call-update) | async-done | bytes 4194320 | tf_op jit(solution)/shard_map/all_gather | solution.py:92
  363.1 2.1 fusion.98
  365.2 0.6 multiply_reduce_fusion
  365.8 1.4 copy-done.2
  367.2 0.8 multiply_convert_fusion
  368.0 0.8 copy-done.8
  368.7 0.7 fusion.29
  369.5 1.6 copy-done.10
  371.1 0.7 fusion.40
  371.8 0.9 copy-done.12
  372.7 0.7 fusion.46
  374.4 5.9 %convolution_convert_fusion = bf16[256,4096]{1,0:T(8,128)(2,1)} fusion(bf16[1,256,4096]{2,1,0:T(8,128)(2,1)S(1)} %copy-done, bf16[256,4096]{1,0:T(8,128)(2,1)} %copy-done.3, bf16[1,4096,256]{2,1,0:T(8,128)(2,1)} %param.18, f32[1,256,256]{1,2,0:T(8,128)S(1)} %get-tuple-element.7, f32[256]{0:T(256)S(1)} %add_rsqrt_fusion, f32[256]{0:T(256)S(1)} %broadcast_multiply_fusion), kind=kOutput, calls=%fused_computation | convolution fusion | flops 1075314688 | bytes 8652800 | tf_op jit(solution)/shard_map/dot_general | solution.py:105
  380.3 1.2 fusion.18
  381.5 55.4 %reduce-scatter.5.cloned.1.call-done = bf16[32,4096]{1,0:T(8,128)(2,1)} async-done(((bf16[256,4096]{1,0:T(8,128)(2,1)}), bf16[32,4096]{1,0:T(8,128)(2,1)}) %reduce-scatter.5.cloned.1.call-update) | async-done | bytes 262160 | tf_op jit(solution)/shard_map/reduce_scatter | solution.py:104
  436.9 2.0 add_bitcast_fusion
  (45 shorter events, 3.2 us)
Async XLA Ops:
  7.2 111.1 %copy-start = (bf16[1,256,4096]{2,1,0:T(8,128)(2,1)S(1)}, bf16[1,256,4096]{2,1,0:T(8,128)(2,1)}, u32[]{:S(2)}) copy-start(bf16[1,256,4096]{2,1,0:T(8,128)(2,1)} %param.19) | copy-start | bytes 6291460
  7.2 98.0 %all-gather.9.cloned.1.call-start = ((), (), s32[]{:S(2)}) async-start(), calls=%async_computation.6 | async-start | bytes 4718592 | tf_op jit(solution)/shard_map/all_gather | solution.py:91
  7.9 171.5 %reduce-scatter.3.cloned.1.call-start = ((), (), s32[]{:S(2)}) async-start(), calls=%async_computation.3 | async-start | bytes 2359296 | tf_op jit(solution)/shard_map/reduce_scatter | solution.py:104
  105.1 5.4 %copy-start.6 = (f32[1,4096]{1,0:T(1,128)S(1)}, f32[1,4096]{1,0:T(1,128)}, u32[]{:S(2)}) copy-start(f32[1,4096]{1,0:T(1,128)} %param.14) | copy-start | bytes 49156
  107.6 3.4 copy-start.1
  111.1 1.6 copy-start.7
  112.7 3.1 copy-start.4
  112.7 2.3 copy-start.9
  115.0 1.6 copy-start.11
  116.6 1.1 copy-start.5
  124.3 111.5 %all-gather.7.cloned.1.call-start = ((), (), s32[]{:S(2)}) async-start(), calls=%async_computation.4 | async-start | bytes 2359296 | tf_op jit(solution)/shard_map/all_gather | solution.py:111
  181.3 181.8 %all-gather.5.cloned.1.call-start = ((), (), s32[]{:S(2)}) async-start(), calls=%async_computation.2 | async-start | bytes 4718592 | tf_op jit(solution)/shard_map/all_gather | solution.py:92
  181.9 255.0 %reduce-scatter.5.cloned.1.call-start = ((), (), s32[]{:S(2)}) async-start(), calls=%async_computation.5 | async-start | bytes 2359296 | tf_op jit(solution)/shard_map/reduce_scatter | solution.py:104
  235.8 127.3 %collective-permute-start = (bf16[256,4096]{1,0:T(8,128)(2,1)}, bf16[256,4096]{1,0:T(8,128)(2,1)}, u32[]{:S(2)}, u32[]{:S(2)}) collective-permute-start(bf16[256,4096]{1,0:T(8,128)(2,1)} %all-gather.7.cloned.1.call-done), channel_id=1, source_target_pairs={{0,8},{8,16},{16,24},{24,32},{32,40},{40,48},{48,56},{56,64},{64,7... | collective-permute-start | bytes 6291464 | tf_op jit(solution)/shard_map/ppermute | solution.py:12
  365.2 1.9 copy-start.2
  367.1 1.6 copy-start.8
  368.7 3.1 copy-start.3
  368.7 2.3 copy-start.10
  371.1 1.6 copy-start.12
Sparse Core Ops, SparseCore 0:
  9.8 95.2 all-gather.8
  124.4 54.9 reduce-scatter.2
  181.8 53.9 all-gather.6
  237.4 125.6 all-gather.4
  380.4 56.3 reduce-scatter.4
where the time goes:
time: 447 us; the launch traced here: 445 us
  waiting for transfers between devices  387 us (87%)
  matrix products  19.3 us (4%)
  between operations  14.7 us (3%)
  other arithmetic  13.9 us (3%)
  local copies, waits for them, and re-layouts  8.46 us (2%)
    all_gather x1, waiting for transfers between devices, body(): lax.all_gather(fresh, 'tensor', axis=0, tiled=True)  125 us
    reduce_scatter x2, waiting for transfers between devices, body(): lax.psum_scatter(jnp.dot(gated, out_here, preferred_element_type=jnp.floa...  110 us
    all_gather x1, waiting for transfers between devices, body(): lax.all_gather(inflow[0], 'tensor', axis=0, tiled=True)  96.5 us
    all_gather x1, waiting for transfers between devices, body(): lax.all_gather(token_rows.astype(jnp.bfloat16), 'tensor', axis=0, tiled=T...  53.9 us
    dot_general x2, matrix products, body(): jnp.dot(gated, out_here, preferred_element_type=jnp.float32)  11.9 us
  transfers between devices with their start and end apart: 6, of which 5 were waited for; matrix products, arithmetic and copies ran while one was open for 0% of the time, Pallas kernels for 0%

commit v1 on v0

--- a/solution.py
+++ b/solution.py
@@ -78,44 +78,37 @@
     return (gated, new_state)
 
 
+def gather_rows(rows):
+    everywhere = jnp.broadcast_to(rows[None], (lax.axis_size("tensor"),) + rows.shape)
+    return lax.all_to_all(everywhere, "tensor", 0, 0, tiled=True).reshape(-1, rows.shape[-1])
+
+
+def scatter_sum(partial):
+    count = lax.axis_size("tensor")
+    parts = partial.reshape(count, partial.shape[0] // count, partial.shape[1])
+    arrived = lax.all_to_all(parts, "tensor", 0, 0, tiled=True)
+    return jnp.sum(arrived.astype(jnp.float32), axis=0)
+
+
 def body(inflow, fresh, states, rates, norm_gain, w_query, w_key, w_value, w_gate, w_out):
     key_size = states.shape[2]
     value_size = states.shape[3]
-    slice_rows = fresh.shape[0]
     gain_here = norm_gain[0]
     rate_here = rates[0]
     state_now = states[0]
     out_here = w_out[0]
     first_section = lax.axis_index("section") == 0
-    whole_in, whole_fresh = (
-        lax.all_gather(inflow[0], "tensor", axis=0, tiled=True),
-        lax.all_gather(fresh, "tensor", axis=0, tiled=True),
-    )
-    entering = whole_in
-    token_rows = inflow[0]
+    own_rows = inflow[0]
     for turn_index in range(2):
-        projected = project(
-            layer_norm(entering, gain_here), w_query[0], w_key[0], w_value[0], w_gate[0]
-        )
+        normed = gather_rows(layer_norm(own_rows, gain_here))
+        projected = project(normed, w_query[0], w_key[0], w_value[0], w_gate[0])
         gated, state_now = retain(projected, state_now, rate_here, key_size, value_size)
-        own_rows = lax.dynamic_slice_in_dim(
-            entering, lax.axis_index("tensor") * slice_rows, slice_rows, 0
-        )
-        token_rows = own_rows + lax.psum_scatter(
-            jnp.dot(gated, out_here, preferred_element_type=jnp.float32).astype(jnp.bfloat16),
-            "tensor",
-            scatter_dimension=0,
-            tiled=True,
-        ).astype(jnp.float32)
+        partial = jnp.dot(gated, out_here, preferred_element_type=jnp.float32).astype(jnp.bfloat16)
+        own_rows = own_rows + scatter_sum(partial)
         if turn_index == 0:
-            whole_rows = lax.all_gather(
-                token_rows.astype(jnp.bfloat16), "tensor", axis=0, tiled=True
-            ).astype(token_rows.dtype)
-            arrived = from_behind(whole_rows.astype(jnp.bfloat16), "section", 1).astype(
-                whole_rows.dtype
-            )
-            entering = jnp.where(first_section, whole_fresh, arrived)
-    return (token_rows[None], state_now[None])
+            arrived = from_behind(own_rows.astype(jnp.bfloat16), "section", 1)
+            own_rows = jnp.where(first_section, fresh, arrived.astype(jnp.float32))
+    return (own_rows[None], state_now[None])
 
 
 def solution(mesh):

time: 447 us -> 182 us (0.41)
  waiting for transfers between devices: 387 us -> 86.4 us
  blocking collectives: 0 us -> 29.8 us
  starting transfers between devices: 2.29 us -> 17.6 us
  matrix products: 19.3 us -> 33.2 us
  between operations: 14.7 us -> 1.69 us
  other arithmetic: 13.9 us -> 7.98 us
    all_gather x3 -> x0, waiting for transfers between devices: 275 us -> none  [the longest x1 125 us: body(): lax.all_gather(fresh, 'tensor', axis=0, tiled=True)]
    reduce_scatter x2 -> x0, waiting for transfers between devices: 110 us -> none  [body(): lax.psum_scatter(jnp.dot(gated, out_here, preferred_element_type=jnp.floa...]
    all_to_all x0 -> x3, waiting for transfers between devices: none -> 79.7 us  [the longest x2 53.3 us: gather_rows(): lax.all_to_all(everywhere, 'tensor', 0, 0, tiled=True)]
    all_to_all x0 -> x1, blocking collectives: none -> 29.8 us  [scatter_sum(): arrived = lax.all_to_all(parts, 'tensor', 0, 0, tiled=True)]
    all_to_all x0 -> x3, starting transfers between devices: none -> 15.7 us  [the longest x2 11.2 us: gather_rows(): lax.all_to_all(everywhere, 'tensor', 0, 0, tiled=True)]
    unnamed x26 -> x36, local copies, waits for them, and re-layouts: 8.46 us -> 1.47 us
    ppermute x1, waiting for transfers between devices: 0.01 us -> 6.76 us  [from_behind(): lax.ppermute(value, axis, [(source, source + steps) for source in range(l...]
    dot_general x2, matrix products: 1.45 us -> 6.16 us  [project(): jnp.dot(normed, key_weight, preferred_element_type=jnp.float32)]
  transfers between devices with their start and end apart: 6 -> 4, of which waited for: 5 -> 4; matrix products, arithmetic and copies ran while one was open for 0% -> 1% of each run, Pallas kernels for 0% -> 0%
where the time goes in v1:
time: 182 us; the launch traced here: 181 us
  waiting for transfers between devices  86.4 us (47%)
  matrix products  33.2 us (18%)
  blocking collectives  29.8 us (16%)
  starting transfers between devices  17.6 us (10%)
  other arithmetic  7.98 us (4%)
  local copies, waits for them, and re-layouts  4.54 us (2%)
    all_to_all x2, waiting for transfers between devices, gather_rows(): lax.all_to_all(everywhere, 'tensor', 0, 0, tiled=True)  53.3 us
    all_to_all x1, blocking collectives, scatter_sum(): arrived = lax.all_to_all(parts, 'tensor', 0, 0, tiled=True)  29.8 us
    all_to_all x1, waiting for transfers between devices, scatter_sum(): arrived = lax.all_to_all(parts, 'tensor', 0, 0, tiled=True)  26.4 us
    dot_general x2, matrix products, body(): jnp.dot(gated, out_here, preferred_element_type=jnp.float32)  11.8 us
    all_to_all x2, starting transfers between devices, gather_rows(): lax.all_to_all(everywhere, 'tensor', 0, 0, tiled=True)  11.2 us
    ppermute x1, waiting for transfers between devices, from_behind(): lax.ppermute(value, axis, [(source, source + steps) for source in range(l...  6.76 us
    dot_general x2, matrix products, project(): jnp.dot(normed, key_weight, preferred_element_type=jnp.float32)  6.16 us
    dot_general x2, matrix products, project(): jnp.dot(normed, query_weight, preferred_element_type=jnp.float32)  4.89 us
  transfers between devices with their start and end apart: 4, of which 4 were waited for; matrix products, arithmetic and copies ran while one was open for 1% of the time, Pallas kernels for 0%

profile of v1, /device:TPU:88, one launch (start us, length us, event | category | flops | bytes accessed | tf_op | source)
XLA Modules:
  0.0 181.2 jit_solution(2244125147211277905)
XLA Ops:
  0.6 1.3 reduce_sum.90
  2.0 1.3 fusion.50
  3.3 1.2 fusion.57
  4.5 1.5 broadcast_in_dim.14
  6.0 5.7 %all-to-all-start = ((bf16[8,32,4096]{2,1,0:T(8,128)(2,1)}), bf16[8,32,4096]{2,1,0:T(8,128)(2,1)}, u32[]{:S(2)}, u32[]{:S(2)}) async-start(bf16[8,32,4096]{2,1,0:T(8,128)(2,1)} %broadcast_in_dim.14), calls=%async_computation | async-start | bytes 4194304 | tf_op jit(solution)/shard_map/all_to_all | solution.py:83
  12.4 26.3 %all-to-all-done = bf16[8,32,4096]{2,1,0:T(8,128)(2,1)} async-done(((bf16[8,32,4096]{2,1,0:T(8,128)(2,1)}), bf16[8,32,4096]{2,1,0:T(8,128)(2,1)}, u32[]{:S(2)}, u32[]{:S(2)}) %all-to-all-start) | async-done | bytes 2097184 | tf_op jit(solution)/shard_map/all_to_all | solution.py:83
  38.7 3.1 %fusion.32 = bf16[256,256]{1,0:T(8,128)(2,1)S(1)} fusion(bf16[256,4096]{1,0:T(8,128)(2,1)} %bitcast.3, bf16[1,4096,256]{2,1,0:T(8,128)(2,1)} %param.16), kind=kOutput, calls=%fused_computation.38 | convolution fusion | flops 537001984 | bytes 4325376 | tf_op jit(solution)/shard_map/dot_general | solution.py:25
  41.8 2.4 %fusion.43 = bf16[256,256]{1,0:T(8,128)(2,1)S(1)} fusion(bf16[256,4096]{1,0:T(8,128)(2,1)} %bitcast.3, bf16[1,4096,256]{2,1,0:T(8,128)(2,1)S(1)} %copy-done.12), kind=kOutput, calls=%fused_computation.43 | convolution fusion | flops 536936448 | bytes 4325376 | tf_op jit(solution)/shard_map/dot_general | solution.py:24
  44.3 2.3 %fusion.37 = bf16[256,256]{1,0:T(8,128)(2,1)S(1)} fusion(bf16[256,4096]{1,0:T(8,128)(2,1)} %bitcast.3, bf16[1,4096,256]{2,1,0:T(8,128)(2,1)S(1)} %copy-done.14), kind=kOutput, calls=%fused_computation.41 | convolution fusion | flops 536936448 | bytes 4325376 | tf_op jit(solution)/shard_map/dot_general | solution.py:26
  46.7 0.4 convolution_bitcast_fusion.3
  47.1 0.4 fusion.102
  47.7 5.9 %convolution_convert_fusion.1 = bf16[256,4096]{1,0:T(8,128)(2,1)} fusion(bf16[1,256,4096]{2,1,0:T(8,128)(2,1)S(1)} %copy-done, bf16[256,4096]{1,0:T(8,128)(2,1)} %bitcast.3, bf16[1,4096,256]{2,1,0:T(8,128)(2,1)} %param.18, f32[1,256,256]{1,2,0:T(8,128)S(1)} %get-tuple-element.3, f32[256]{0:T(256)S(1)} %add_rsqrt_fusion.1, f32[256]{0:T(256)S(1)} %broadcast_multiply_fusion.1), kind=kOutput, calls=%fused_computation.1 | convolution fusion | flops 1075314688 | bytes 8652800 | tf_op jit(solution)/shard_map/dot_general | solution.py:106
  53.6 29.8 %all_to_all.20 = bf16[8,32,4096]{2,1,0:T(8,128)(2,1)S(1)} all-to-all(bf16[8,32,4096]{2,1,0:T(8,128)(2,1)} %bitcast.157), channel_id=1, replica_groups=mesh['section'=32,'tensor'=8] {'tensor'}, dimensions={0} | all-to-all | bytes 4194304 | tf_op jit(solution)/shard_map/all_to_all | solution.py:89
  83.7 0.7 copy-done.1
  84.5 1.9 %collective-permute-start = (bf16[32,4096]{1,0:T(8,128)(2,1)S(1)}, bf16[32,4096]{1,0:T(8,128)(2,1)S(1)}, u32[]{:S(2)}, u32[]{:S(2)}) collective-permute-start(bf16[32,4096]{1,0:T(8,128)(2,1)S(1)} %fusion.51), channel_id=1, source_target_pairs={{0,8},{8,16},{16,24},{24,32},{32,40},{40,48},{48,56},{56,64},{64,7... | collective-permute-start | bytes 786440 | tf_op jit(solution)/shard_map/ppermute | solution.py:12
  86.4 6.8 %collective-permute-done = bf16[32,4096]{1,0:T(8,128)(2,1)S(1)} collective-permute-done((bf16[32,4096]{1,0:T(8,128)(2,1)S(1)}, bf16[32,4096]{1,0:T(8,128)(2,1)S(1)}, u32[]{:S(2)}, u32[]{:S(2)}) %collective-permute-start) | collective-permute-done | bytes 262176 | tf_op jit(solution)/shard_map/ppermute | solution.py:12
  93.8 1.5 broadcast_in_dim.15
  95.3 5.5 %all-to-all-start.2 = ((bf16[8,32,4096]{2,1,0:T(8,128)(2,1)}), bf16[8,32,4096]{2,1,0:T(8,128)(2,1)}, u32[]{:S(2)}, u32[]{:S(2)}) async-start(bf16[8,32,4096]{2,1,0:T(8,128)(2,1)} %broadcast_in_dim.15), calls=%async_computation.2 | async-start | bytes 4194304 | tf_op jit(solution)/shard_map/all_to_all | solution.py:83
  100.9 1.4 convolution_add_fusion.1
  102.3 27.0 %all-to-all-done.2 = bf16[8,32,4096]{2,1,0:T(8,128)(2,1)} async-done(((bf16[8,32,4096]{2,1,0:T(8,128)(2,1)}), bf16[8,32,4096]{2,1,0:T(8,128)(2,1)}, u32[]{:S(2)}, u32[]{:S(2)}) %all-to-all-start.2) | async-done | bytes 2097184 | tf_op jit(solution)/shard_map/all_to_all | solution.py:83
  129.2 3.1 %fusion.29 = bf16[256,256]{1,0:T(8,128)(2,1)S(1)} fusion(bf16[256,4096]{1,0:T(8,128)(2,1)} %bitcast.18, bf16[1,4096,256]{2,1,0:T(8,128)(2,1)} %param.16), kind=kOutput, calls=%fused_computation.37 | convolution fusion | flops 537001984 | bytes 4325376 | tf_op jit(solution)/shard_map/dot_general | solution.py:25
  132.4 2.4 %fusion.46 = bf16[256,256]{1,0:T(8,128)(2,1)S(1)} fusion(bf16[256,4096]{1,0:T(8,128)(2,1)} %bitcast.18, bf16[1,4096,256]{2,1,0:T(8,128)(2,1)S(1)} %copy-done.13), kind=kOutput, calls=%fused_computation.44 | convolution fusion | flops 536936448 | bytes 4325376 | tf_op jit(solution)/shard_map/dot_general | solution.py:24
  134.8 2.3 %fusion.40 = bf16[256,256]{1,0:T(8,128)(2,1)S(1)} fusion(bf16[256,4096]{1,0:T(8,128)(2,1)} %bitcast.18, bf16[1,4096,256]{2,1,0:T(8,128)(2,1)S(1)} %copy-done.15), kind=kOutput, calls=%fused_computation.42 | convolution fusion | flops 536936448 | bytes 4325376 | tf_op jit(solution)/shard_map/dot_general | solution.py:26
  137.2 0.6 copy-done.7
  137.8 1.1 convolution_bitcast_fusion.2
  138.9 1.3 fusion.103
  140.4 5.9 %convolution_convert_fusion = bf16[256,4096]{1,0:T(8,128)(2,1)} fusion(bf16[1,256,4096]{2,1,0:T(8,128)(2,1)S(1)} %copy-done, bf16[256,4096]{1,0:T(8,128)(2,1)} %bitcast.18, bf16[1,4096,256]{2,1,0:T(8,128)(2,1)} %param.18, f32[1,256,256]{1,2,0:T(8,128)S(1)} %get-tuple-element.5, f32[256]{0:T(256)S(1)} %add_rsqrt_fusion, f32[256]{0:T(256)S(1)} %broadcast_multiply_fusion), kind=kOutput, calls=%fused_computation | convolution fusion | flops 1075314688 | bytes 8652800 | tf_op jit(solution)/shard_map/dot_general | solution.py:106
  146.4 4.5 %all-to-all-start.3 = ((bf16[8,32,4096]{2,1,0:T(8,128)(2,1)}), bf16[8,32,4096]{2,1,0:T(8,128)(2,1)}, u32[]{:S(2)}, u32[]{:S(2)}) async-start(bf16[8,32,4096]{2,1,0:T(8,128)(2,1)} %bitcast.156), calls=%async_computation.3 | async-start | bytes 4194304 | tf_op jit(solution)/shard_map/all_to_all | solution.py:89
  150.9 1.2 fusion.18
  152.0 26.4 %all-to-all-done.3 = bf16[8,32,4096]{2,1,0:T(8,128)(2,1)} async-done(((bf16[8,32,4096]{2,1,0:T(8,128)(2,1)}), bf16[8,32,4096]{2,1,0:T(8,128)(2,1)}, u32[]{:S(2)}, u32[]{:S(2)}) %all-to-all-start.3) | async-done | bytes 2097184 | tf_op jit(solution)/shard_map/all_to_all | solution.py:89
  178.4 1.9 %convert_reduce_fusion = f32[32,4096]{1,0:T(8,128)S(1)} fusion(bf16[8,32,4096]{2,1,0:T(8,128)(2,1)} %all-to-all-done.3), kind=kLoop, calls=%fused_computation.2 | loop fusion | flops 1966080 | bytes 2621440 | tf_op jit(solution)/shard_map/reduce_sum | solution.py:90
  180.3 0.9 add_bitcast_fusion
  (52 shorter events, 1.4 us)
Async XLA Ops:
  0.6 47.0 %copy-start = (bf16[1,256,4096]{2,1,0:T(8,128)(2,1)S(1)}, bf16[1,256,4096]{2,1,0:T(8,128)(2,1)}, u32[]{:S(2)}) copy-start(bf16[1,256,4096]{2,1,0:T(8,128)(2,1)} %param.19) | copy-start | bytes 6291460
  6.0 32.7 %all-to-all-start = ((bf16[8,32,4096]{2,1,0:T(8,128)(2,1)}), bf16[8,32,4096]{2,1,0:T(8,128)(2,1)}, u32[]{:S(2)}, u32[]{:S(2)}) async-start(bf16[8,32,4096]{2,1,0:T(8,128)(2,1)} %broadcast_in_dim.14), calls=%async_computation | async-start | bytes 4194304 | tf_op jit(solution)/shard_map/all_to_all | solution.py:83
  12.4 34.3 %copy-start.16 = (f32[256]{0:T(256)}, f32[256]{0:T(256)S(1)}, u32[]{:S(2)}) copy-start(f32[256]{0:T(256)S(1)} %iota_convert_fusion) | copy-start | bytes 3076
  12.4 34.7 %copy-start.10 = (f32[256]{0:T(256)}, f32[256]{0:T(256)S(1)}, u32[]{:S(2)}) copy-start(f32[256]{0:T(256)S(1)} %multiply_exponential_fusion.1) | copy-start | bytes 3076
  38.7 3.1 %copy-start.12 = (bf16[1,4096,256]{2,1,0:T(8,128)(2,1)S(1)}, bf16[1,4096,256]{2,1,0:T(8,128)(2,1)}, u32[]{:S(2)}) copy-start(bf16[1,4096,256]{2,1,0:T(8,128)(2,1)} %param.15) | copy-start | bytes 6291460
  41.8 2.5 %copy-start.14 = (bf16[1,4096,256]{2,1,0:T(8,128)(2,1)S(1)}, bf16[1,4096,256]{2,1,0:T(8,128)(2,1)}, u32[]{:S(2)}) copy-start(bf16[1,4096,256]{2,1,0:T(8,128)(2,1)} %param.17) | copy-start | bytes 6291460
  44.3 2.8 %copy-start.3 = (f32[1,1,256,256]{3,2,1,0:T(8,128)S(1)}, f32[1,1,256,256]{3,2,1,0:T(8,128)}, u32[]{:S(2)}) copy-start(f32[1,1,256,256]{3,2,1,0:T(8,128)} %param.12) | copy-start | bytes 786436
  46.7 6.9 %copy-start.4 = (bf16[256,256]{1,0:T(8,128)(2,1)}, bf16[256,256]{1,0:T(8,128)(2,1)S(1)}, u32[]{:S(2)}) copy-start(bf16[256,256]{1,0:T(8,128)(2,1)S(1)} %fusion.37) | copy-start | bytes 393220
  83.4 1.0 copy-start.1
  83.4 9.8 %copy-start.2 = (f32[32,4096]{1,0:T(8,128)S(1)}, f32[32,4096]{1,0:T(8,128)}, u32[]{:S(2)}) copy-start(f32[32,4096]{1,0:T(8,128)} %param.11) | copy-start | bytes 1572868
  84.4 9.2 %copy-start.9 = (f32[1,4096]{1,0:T(1,128)S(1)}, f32[1,4096]{1,0:T(1,128)}, u32[]{:S(2)}) copy-start(f32[1,4096]{1,0:T(1,128)} %param.14) | copy-start | bytes 49156
  84.5 8.7 %collective-permute-start = (bf16[32,4096]{1,0:T(8,128)(2,1)S(1)}, bf16[32,4096]{1,0:T(8,128)(2,1)S(1)}, u32[]{:S(2)}, u32[]{:S(2)}) collective-permute-start(bf16[32,4096]{1,0:T(8,128)(2,1)S(1)} %fusion.51), channel_id=1, source_target_pairs={{0,8},{8,16},{16,24},{24,32},{32,40},{40,48},{48,56},{56,64},{64,7... | collective-permute-start | bytes 786440 | tf_op jit(solution)/shard_map/ppermute | solution.py:12
  95.3 33.9 %all-to-all-start.2 = ((bf16[8,32,4096]{2,1,0:T(8,128)(2,1)}), bf16[8,32,4096]{2,1,0:T(8,128)(2,1)}, u32[]{:S(2)}, u32[]{:S(2)}) async-start(bf16[8,32,4096]{2,1,0:T(8,128)(2,1)} %broadcast_in_dim.15), calls=%async_computation.2 | async-start | bytes 4194304 | tf_op jit(solution)/shard_map/all_to_all | solution.py:83
  129.2 3.1 %copy-start.13 = (bf16[1,4096,256]{2,1,0:T(8,128)(2,1)S(1)}, bf16[1,4096,256]{2,1,0:T(8,128)(2,1)}, u32[]{:S(2)}) copy-start(bf16[1,4096,256]{2,1,0:T(8,128)(2,1)} %param.15) | copy-start | bytes 6291460
  132.3 4.8 %copy-start.5 = (bf16[256,256]{1,0:T(8,128)(2,1)}, bf16[256,256]{1,0:T(8,128)(2,1)S(1)}, u32[]{:S(2)}) copy-start(bf16[256,256]{1,0:T(8,128)(2,1)S(1)} %fusion.29) | copy-start | bytes 393220
  132.4 2.5 %copy-start.15 = (bf16[1,4096,256]{2,1,0:T(8,128)(2,1)S(1)}, bf16[1,4096,256]{2,1,0:T(8,128)(2,1)}, u32[]{:S(2)}) copy-start(bf16[1,4096,256]{2,1,0:T(8,128)(2,1)} %param.17) | copy-start | bytes 6291460
  134.8 3.0 %copy-start.17 = (f32[256]{0:T(256)S(1)}, f32[256]{0:T(256)}, u32[]{:S(2)}) copy-start(f32[256]{0:T(256)} %copy-done.16) | copy-start | bytes 3076
  134.8 4.1 %copy-start.11 = (f32[256]{0:T(256)S(1)}, f32[256]{0:T(256)}, u32[]{:S(2)}) copy-start(f32[256]{0:T(256)} %copy-done.10) | copy-start | bytes 3076
  137.2 0.7 copy-start.7
  146.4 4.5 %copy-start.6 = (bf16[256,256]{1,0:T(8,128)(2,1)S(1)}, bf16[256,256]{1,0:T(8,128)(2,1)}, u32[]{:S(2)}) copy-start(bf16[256,256]{1,0:T(8,128)(2,1)} %copy-done.5) | copy-start | bytes 393220
  146.4 4.5 %copy-start.8 = (bf16[256,256]{1,0:T(8,128)(2,1)S(1)}, bf16[256,256]{1,0:T(8,128)(2,1)}, u32[]{:S(2)}) copy-start(bf16[256,256]{1,0:T(8,128)(2,1)} %copy-done.7) | copy-start | bytes 393220
  146.4 32.0 %all-to-all-start.3 = ((bf16[8,32,4096]{2,1,0:T(8,128)(2,1)}), bf16[8,32,4096]{2,1,0:T(8,128)(2,1)}, u32[]{:S(2)}, u32[]{:S(2)}) async-start(bf16[8,32,4096]{2,1,0:T(8,128)(2,1)} %bitcast.156), calls=%async_computation.3 | async-start | bytes 4194304 | tf_op jit(solution)/shard_map/all_to_all | solution.py:89

commit v2 on v1

v2 whole, which is shorter than its diff:
```python
import jax
import jax.numpy as jnp
from jax import lax
from jax.experimental import pallas as pl
from jax.experimental.pallas import tpu as pltpu
from jax.sharding import PartitionSpec as P

EPSILON = 1e-05
VMEM = pl.BlockSpec(memory_space=pltpu.VMEM)
SMEM = pl.BlockSpec(memory_space=pltpu.SMEM)
LIMIT = 16 * 1024 * 1024


def shift_x(value, steps):
    return lax.ppermute(value, "tensor", [(t, (t + 2 * steps) % 8) for t in range(8)])


def swap_z(value):
    return lax.ppermute(value, "tensor", [(t, t ^ 1) for t in range(8)])


def next_section(value):
    return lax.ppermute(value, "section", [(s, s + 1) for s in range(lax.axis_size("section") - 1)])


def call(kernel, out_shape, in_specs, flops=0, moved=0, scratch=()):
    return pl.pallas_call(
        kernel,
        out_shape=out_shape,
        in_specs=in_specs,
        out_specs=jax.tree.map(lambda _: VMEM, out_shape),
        scratch_shapes=scratch,
        cost_estimate=pl.CostEstimate(flops=flops, bytes_accessed=moved, transcendentals=0),
        compiler_params=pltpu.CompilerParams(vmem_limit_bytes=LIMIT),
    )


def norm_kernel(rows_ref, gain_ref, out_ref):
    rows = rows_ref[...]
    centred = rows - jnp.mean(rows, axis=-1, keepdims=True)
    spread = jnp.mean(centred * centred, axis=-1, keepdims=True)
    out_ref[...] = (centred * lax.rsqrt(spread + EPSILON) * gain_ref[...]).astype(jnp.bfloat16)


def layer_norm(rows, gain):
    return call(
        norm_kernel, jax.ShapeDtypeStruct(rows.shape, jnp.bfloat16), [VMEM, VMEM], flops=6 * rows.size, moved=6 * rows.size
    )(rows, gain)


def dot(a, b):
    return jnp.dot(a, b, preferred_element_type=jnp.float32)


def project_into(blocks, weights, outs, base):
    rows = jnp.concatenate([block[...] for block in blocks], axis=0)
    count = rows.shape[0]
    w_query, w_key, w_value, w_gate = weights
    queries, keys, values, gates = outs
    where = pl.ds(base, count)
    queries[where] = dot(rows, w_query[0]).astype(jnp.bfloat16)
    keys[where] = (dot(rows, w_key[0]) * 0.0625).astype(jnp.bfloat16)
    values[where] = dot(rows, w_value[0]).astype(jnp.bfloat16)
    gates[where] = dot(rows, w_gate[0])


def early_kernel(b0, b1, b2, b3, wq, wk, wv, wg, queries, keys, values, gates):
    project_into((b0, b1, b2, b3), (wq, wk, wv, wg), (queries, keys, values, gates), 0)


def split(value):
    high = value.astype(jnp.bfloat16)
    return high, (value - high.astype(jnp.float32)).astype(jnp.bfloat16)


def late_kernel(
    b0, b1, b2, b3, wq, wk, wv, wg, early_q, early_k, early_v, early_g, state, decay, lead, tail, keep, w_out,
    over_z, over_x, gated_late, new_state, queries, keys, values, gates,
):
    project_into((b0, b1, b2, b3), (wq, wk, wv, wg), (queries, keys, values, gates), 0)
    half = early_q.shape[0]
    rest = pl.ds(half, half)
    queries[rest] = early_q[...]
    keys[rest] = early_k[...]
    values[rest] = early_v[...]
    gates[rest] = early_g[...]
    q, k, v = queries[...], keys[...], values[...]
    scores = lax.dot_general(q, k, (((1,), (1,)), ((), ())), preferred_element_type=jnp.float32)
    weighted = (scores * decay[...]).astype(jnp.bfloat16)
    before = state[0, 0]
    high, low = split(before)
    mixed = dot(weighted, v) + (dot(q, high) + dot(q, low)) * lead[...]
    centred = mixed - jnp.mean(mixed, axis=-1, keepdims=True)
    head_out = centred * lax.rsqrt(jnp.mean(centred * centred, axis=-1, keepdims=True) + EPSILON)
    gate = gates[...]
    gated = (gate / (1.0 + jnp.exp(-gate)) * head_out).astype(jnp.bfloat16)
    partial = dot(gated[:half], w_out[0]).astype(jnp.bfloat16)
    over_z[...] = partial[: half // 2]
    over_x[...] = partial[half // 2 :]
    gated_late[...] = gated[half:]
    k_high, k_low = split(k.astype(jnp.float32) * tail[...])
    across = (((0,), (0,)), ((), ()))
    added = lax.dot_general(k_high, v, across, preferred_element_type=jnp.float32) + lax.dot_general(
        k_low, v, across, preferred_element_type=jnp.float32
    )
    new_state[0, 0] = keep[0, 0] * before + added


def out_kernel(gated, w_out, up, down, mate, own):
    count = own.shape[0]
    up[...] = dot(gated[:count], w_out[0]).astype(jnp.bfloat16)
    down[...] = dot(gated[count : 2 * count], w_out[0]).astype(jnp.bfloat16)
    mate[...] = dot(gated[2 * count : 3 * count], w_out[0]).astype(jnp.bfloat16)
    own[...] = dot(gated[3 * count :], w_out[0])


def body(inflow, fresh, states, rates, norm_gain, w_query, w_key, w_value, w_gate, w_out):
    count, width = fresh.shape
    key_size, value_size = states.shape[2:]
    group = count * lax.axis_size("tensor")
    half = group // 2
    first_section = lax.axis_index("section") == 0
    steps = jnp.array([2, 6, 4, 4, 2, 6, 0, 0], jnp.int32)
    mates = jnp.array([1, 1, 0, 1, 0, 0, 1, 0], jnp.int32)
    order = ((lax.axis_index("tensor") + steps) & 7) ^ mates
    positions = (order[:, None] * count + jnp.arange(count)[None, :]).reshape(group).astype(jnp.float32)
    log_keep = jnp.log1p(-rates)
    offsets = positions[:, None] - positions[None, :]
    decay = jnp.where(offsets >= 0, jnp.exp(jnp.maximum(offsets, 0.0) * log_keep), 0.0)
    lead = jnp.exp((positions[:, None] + 1.0) * log_keep)
    tail = jnp.exp((group - 1.0 - positions[:, None]) * log_keep)
    keep = jnp.exp(group * log_keep)
    weights = (w_query, w_key, w_value, w_gate)
    bf16, f32 = jnp.bfloat16, jnp.float32
    shape = jax.ShapeDtypeStruct
    state = states
    own_rows = inflow[0]
    for turn_index in range(2):
        own = layer_norm(own_rows, norm_gain)
        below, above, mate = shift_x(own, 1), shift_x(own, -1), swap_z(own)
        below, above, mate, held = lax.optimization_barrier((below, above, mate, own))
        mate_above, mate_below = swap_z(above), swap_z(below)
        far, far_mate = shift_x(held, 2), shift_x(mate, 2)
        early = call(
            early_kernel,
            [shape((half, key_size), bf16)] * 2 + [shape((half, value_size), bf16), shape((half, value_size), f32)],
            [VMEM] * 8,
            flops=2 * half * width * 2 * (key_size + value_size),
            moved=2 * width * 2 * (key_size + value_size),
        )(above, below, mate, own, *weights)
        over_z, over_x, gated_late, state = call(
            late_kernel,
            [shape((half // 2, width), bf16)] * 2 + [shape((half, value_size), bf16), shape(state.shape, f32)],
            [VMEM] * 16 + [SMEM, VMEM],
            flops=2 * half * width * 2 * (key_size + value_size),
            moved=2 * width * 2 * (key_size + value_size),
            scratch=[
                pltpu.VMEM((group, key_size), bf16),
                pltpu.VMEM((group, key_size), bf16),
                pltpu.VMEM((group, value_size), bf16),
                pltpu.VMEM((group, value_size), f32),
            ],
        )(mate_above, mate_below, far, far_mate, *weights, *early, state, decay, lead, tail, keep, w_out)
        via_z, via_x = swap_z(over_z), shift_x(over_x, 2)
        up, down, to_mate, mine = call(
            out_kernel,
            [shape((count, width), bf16)] * 3 + [shape((count, width), f32)],
            [VMEM, VMEM],
            flops=2 * half * value_size * width,
            moved=2 * value_size * width,
        )(gated_late, w_out)

        def add(a, b):
            return (a.astype(f32) + b.astype(f32)).astype(bf16)

        got_up = shift_x(add(up, via_z[:count]), 1)
        got_down = shift_x(add(down, via_z[count:]), -1)
        got_mate = swap_z(add(to_mate, via_x[count:]))
        own_rows = (
            own_rows
            + mine
            + via_x[:count].astype(f32)
            + got_up.astype(f32)
            + got_down.astype(f32)
            + got_mate.astype(f32)
        )
        if turn_index == 0:
            arrived = next_section(own_rows.astype(bf16))
            own_rows = jnp.where(first_section, fresh, arrived.astype(f32))
    return (own_rows[None], state)


def solution(mesh):
    in_specs = (
        P("section", "tensor", None),
        P("tensor", None),
        P("section", "tensor", None, None),
        P("section", "tensor"),
        P("section", None),
        P("section", None, "tensor"),
        P("section", None, "tensor"),
        P("section", None, "tensor"),
        P("section", None, "tensor"),
        P("section", "tensor", None),
    )
    out_specs = (P("section", "tensor", None), P("section", "tensor", None, None))
    return jax.shard_map(body, mesh=mesh, in_specs=in_specs, out_specs=out_specs, check_vma=False)
```

time: 182 us -> 128 us (0.70)
  waiting for transfers between devices: 86.4 us -> 50.7 us
  matrix products: 33.2 us -> 0 us
  blocking collectives: 29.8 us -> 0 us
  starting transfers between devices: 17.6 us -> 41.5 us
  Pallas kernels: 0 us -> 12.3 us
  local copies, waits for them, and re-layouts: 4.54 us -> 16 us
  other arithmetic: 7.98 us -> 4.15 us
    all_to_all x3 -> x0, waiting for transfers between devices: 79.7 us -> none  [the longest x2 53.3 us: gather_rows(): lax.all_to_all(everywhere, 'tensor', 0, 0, tiled=True)]
    ppermute x1 -> x25, waiting for transfers between devices: 6.76 us -> 50.7 us  [the longest x14 33.3 us: shift_x(): lax.ppermute(value, 'tensor', [(t, (t + 2 * steps) % 8) for t in range(8)])]
    ppermute x1 -> x25, starting transfers between devices: 1.92 us -> 41.5 us  [the longest x14 22.9 us: shift_x(): lax.ppermute(value, 'tensor', [(t, (t + 2 * steps) % 8) for t in range(8)])]
    dot_general x14 -> x0, matrix products: 33.2 us -> none  [the longest x2 11.8 us: body(): jnp.dot(gated, out_here, preferred_element_type=jnp.float32)]
    all_to_all x1 -> x0, blocking collectives: 29.8 us -> none  [scatter_sum(): arrived = lax.all_to_all(parts, 'tensor', 0, 0, tiled=True)]
    all_to_all x3 -> x0, starting transfers between devices: 15.7 us -> none  [the longest x2 11.2 us: gather_rows(): lax.all_to_all(everywhere, 'tensor', 0, 0, tiled=True)]
    unnamed x36 -> x40, local copies, waits for them, and re-layouts: 1.47 us -> 15.6 us
    pallas_call x0 -> x8, Pallas kernels: none -> 12.3 us  [the longest x2 4.96 us: body(): call(late_kernel, [shape((half // 2, width), bf16)] * 2 + [shape((half, v...]
  transfers between devices with their start and end apart: 4 -> 25, of which waited for: 4 -> 15; matrix products, arithmetic and copies ran while one was open for 1% -> 1% of each run, Pallas kernels for 0% -> 5%
where the time goes in v2:
time: 128 us; the launch traced here: 126 us
  waiting for transfers between devices  50.7 us (40%)
  starting transfers between devices  41.5 us (32%)
  local copies, waits for them, and re-layouts  16 us (12%)
  Pallas kernels  12.3 us (10%)
  other arithmetic  4.15 us (3%)
  between operations  1.64 us (1%)
    ppermute x14, waiting for transfers between devices, shift_x(): lax.ppermute(value, 'tensor', [(t, (t + 2 * steps) % 8) for t in range(8)])  33.3 us
    ppermute x14, starting transfers between devices, shift_x(): lax.ppermute(value, 'tensor', [(t, (t + 2 * steps) % 8) for t in range(8)])  22.9 us
    ppermute x10, starting transfers between devices, swap_z(): return lax.ppermute(value, 'tensor', [(t, t ^ 1) for t in range(8)])  16.7 us
    unnamed x40, local copies, waits for them, and re-layouts  15.6 us
    ppermute x10, waiting for transfers between devices, swap_z(): return lax.ppermute(value, 'tensor', [(t, t ^ 1) for t in range(8)])  10.4 us
    ppermute x1, waiting for transfers between devices, next_section(): lax.ppermute(value, 'section', [(s, s + 1) for s in range(lax.axis_size('...  7.06 us
    pallas_call x2, Pallas kernels, body(): call(late_kernel, [shape((half // 2, width), bf16)] * 2 + [shape((half, v...  4.96 us
    pallas_call x2, Pallas kernels, body(): call(early_kernel, [shape((half, key_size), bf16)] * 2 + [shape((half, va...  3.62 us
  transfers between devices with their start and end apart: 25, of which 15 were waited for; matrix products, arithmetic and copies ran while one was open for 1% of the time, Pallas kernels for 5%

profile of v2, /device:TPU:88, one launch (start us, length us, event | category | flops | bytes accessed | tf_op | source)
XLA Modules:
  0.0 126.3 jit_solution(14359575872824024234)
XLA Ops:
  2.7 2.0 %collective-permute-start.2 = (bf16[32,4096]{1,0:T(8,128)(2,1)S(1)}, bf16[32,4096]{1,0:T(8,128)(2,1)S(1)}, u32[]{:S(2)}, u32[]{:S(2)}) collective-permute-start(bf16[32,4096]{1,0:T(8,128)(2,1)S(1)} %shard_map.131.b3), channel_id=1, source_target_pairs={{0,1},{1,0},{2,3},{3,2},{4,5},{5,4},{6,7},{7,6},{8,9},{9,8},{10,11... | collective-permute-start | bytes 786440 | tf_op jit(solution)/shard_map/ppermute | solution.py:19
  4.7 2.8 %collective-permute-start.1 = (bf16[32,4096]{1,0:T(8,128)(2,1)S(1)}, bf16[32,4096]{1,0:T(8,128)(2,1)S(1)}, u32[]{:S(2)}, u32[]{:S(2)}) collective-permute-start(bf16[32,4096]{1,0:T(8,128)(2,1)S(1)} %shard_map.131.b3), channel_id=1, source_target_pairs={{0,6},{1,7},{2,0},{3,1},{4,2},{5,3},{6,4},{7,5},{8,14},{9,15},{10,... | collective-permute-start | bytes 786440 | tf_op jit(solution)/shard_map/ppermute | solution.py:15
  9.4 1.6 %collective-permute-done.2.b2 = bf16[32,4096]{1,0:T(8,128)(2,1)S(1)} collective-permute-done((bf16[32,4096]{1,0:T(8,128)(2,1)S(1)}, bf16[32,4096]{1,0:T(8,128)(2,1)S(1)}, u32[]{:S(2)}, u32[]{:S(2)}) %collective-permute-start.2) | collective-permute-done | bytes 262176 | tf_op jit(solution)/shard_map/ppermute | solution.py:19
  11.0 1.7 %collective-permute-done.1.b0 = bf16[32,4096]{1,0:T(8,128)(2,1)S(1)} collective-permute-done((bf16[32,4096]{1,0:T(8,128)(2,1)S(1)}, bf16[32,4096]{1,0:T(8,128)(2,1)S(1)}, u32[]{:S(2)}, u32[]{:S(2)}) %collective-permute-start.1) | collective-permute-done | bytes 262176 | tf_op jit(solution)/shard_map/ppermute | solution.py:15
  12.8 3.5 %collective-permute-done.b1 = bf16[32,4096]{1,0:T(8,128)(2,1)} collective-permute-done((bf16[32,4096]{1,0:T(8,128)(2,1)S(1)}, bf16[32,4096]{1,0:T(8,128)(2,1)}, u32[]{:S(2)}, u32[]{:S(2)}) %collective-permute-start) | collective-permute-done | bytes 262176 | tf_op jit(solution)/shard_map/ppermute | solution.py:15
  16.6 1.7 %collective-permute-start.4 = (bf16[32,4096]{1,0:T(8,128)(2,1)}, bf16[32,4096]{1,0:T(8,128)(2,1)S(1)}, u32[]{:S(2)}, u32[]{:S(2)}) collective-permute-start(bf16[32,4096]{1,0:T(8,128)(2,1)} %collective-permute-done.b1), channel_id=1, source_target_pairs={{0,1},{1,0},{2,3},{3,2},{4,5},{5,4},{6,7},{7,6},{8,9},{9,8},{10,11... | collective-permute-start | bytes 786440 | tf_op jit(solution)/shard_map/ppermute | solution.py:19
  18.3 3.5 %collective-permute-start.6 = (bf16[32,4096]{1,0:T(8,128)(2,1)S(1)}, bf16[32,4096]{1,0:T(8,128)(2,1)S(1)}, u32[]{:S(2)}, u32[]{:S(2)}) collective-permute-start(bf16[32,4096]{1,0:T(8,128)(2,1)S(1)} %collective-permute-done.2.b2), channel_id=1, source_target_pairs={{0,4},{1,5},{2,6},{3,7},{4,0},{5,1},{6,2},{7,3},{8,12},{9,13},{10,... | collective-permute-start | bytes 786440 | tf_op jit(solution)/shard_map/ppermute | solution.py:15
  23.6 1.6 %copy-done.4 = bf16[1,4096,256]{2,1,0:T(8,128)(2,1)S(1)} copy-done((bf16[1,4096,256]{2,1,0:T(8,128)(2,1)S(1)}, bf16[1,4096,256]{2,1,0:T(8,128)(2,1)}, u32[]{:S(2)}) %copy-start.4) | copy-done | bytes 2097176
  28.4 2.4 %shard_map.132 = (bf16[128,256]{1,0:T(8,128)(2,1)S(1)}, bf16[128,256]{1,0:T(8,128)(2,1)S(1)}, bf16[128,256]{1,0:T(8,128)(2,1)S(1)}, f32[128,256]{1,0:T(8,128)S(1)}) custom-call(bf16[32,4096]{1,0:T(8,128)(2,1)S(1)} %collective-permute-done.1.b0, bf16[32,4096]{1,0:T(8,128)(2,1)} %collective-permute-done.b1, bf16[32,4096]{1,0:T(8,128)(2,1)S(1)} %collective-permute-done.2.b2, ...), custom_call_target="tpu_custom_call" | custom-call | flops 1073741824 | bytes 8388608 | tf_op jit(solution)/shard_map/pallas_call | solution.py:144
  31.9 1.6 %copy-done.12 = bf16[1,4096,256]{2,1,0:T(8,128)(2,1)S(1)} copy-done((bf16[1,4096,256]{2,1,0:T(8,128)(2,1)S(1)}, bf16[1,4096,256]{2,1,0:T(8,128)(2,1)}, u32[]{:S(2)}) %copy-start.12) | copy-done | bytes 2097176
  33.5 2.1 %shard_map.133 = (bf16[64,4096]{1,0:T(8,128)(2,1)S(1)}, bf16[64,4096]{1,0:T(8,128)(2,1)S(1)}, bf16[128,256]{1,0:T(8,128)(2,1)S(1)}, f32[1,1,256,256]{3,2,1,0:T(8,128)S(1)}) custom-call(bf16[32,4096]{1,0:T(8,128)(2,1)S(1)} %collective-permute-done.3.b0, bf16[32,4096]{1,0:T(8,128)(2,1)S(1)} %collective-permute-done.4.b1, ...), custom_call_target="tpu_custom_call" | custom-call | flops 1073741824 | bytes 8388608 | tf_op jit(solution)/shard_map/pallas_call | solution.py:151
  37.8 10.5 %collective-permute-done.7 = bf16[64,4096]{1,0:T(8,128)(2,1)S(1)} collective-permute-done((bf16[64,4096]{1,0:T(8,128)(2,1)S(1)}, bf16[64,4096]{1,0:T(8,128)(2,1)S(1)}, u32[]{:S(2)}, u32[]{:S(2)}) %collective-permute-start.7) | collective-permute-done | bytes 524320 | tf_op jit(solution)/shard_map/ppermute | solution.py:15
  49.3 3.2 %collective-permute-start.10 = (bf16[32,4096]{1,0:T(8,128)(2,1)S(1)}, bf16[32,4096]{1,0:T(8,128)(2,1)S(1)}, u32[]{:S(2)}, u32[]{:S(2)}) collective-permute-start(bf16[32,4096]{1,0:T(8,128)(2,1)S(1)} %get-tuple-element.69), channel_id=1, source_target_pairs={{0,6},{1,7},{2,0},{3,1},{4,2},{5,3},{6,4},{7,5},{8,14},{9,15},{10,... | collective-permute-start | bytes 786440 | tf_op jit(solution)/shard_map/ppermute | solution.py:15
  52.5 2.3 %collective-permute-done.11 = bf16[32,4096]{1,0:T(8,128)(2,1)S(1)} collective-permute-done((bf16[32,4096]{1,0:T(8,128)(2,1)S(1)}, bf16[32,4096]{1,0:T(8,128)(2,1)S(1)}, u32[]{:S(2)}, u32[]{:S(2)}) %collective-permute-start.11) | collective-permute-done | bytes 262176 | tf_op jit(solution)/shard_map/ppermute | solution.py:19
  54.8 2.1 %collective-permute-done.9 = bf16[32,4096]{1,0:T(8,128)(2,1)S(1)} collective-permute-done((bf16[32,4096]{1,0:T(8,128)(2,1)S(1)}, bf16[32,4096]{1,0:T(8,128)(2,1)S(1)}, u32[]{:S(2)}, u32[]{:S(2)}) %collective-permute-start.9) | collective-permute-done | bytes 262176 | tf_op jit(solution)/shard_map/ppermute | solution.py:15
  57.7 1.9 %collective-permute-start.12 = (bf16[32,4096]{1,0:T(8,128)(2,1)}, bf16[32,4096]{1,0:T(8,128)(2,1)}, u32[]{:S(2)}, u32[]{:S(2)}) collective-permute-start(bf16[32,4096]{1,0:T(8,128)(2,1)} %add_convert_fusion.3), channel_id=1, source_target_pairs={{0,8},{8,16},{16,24},{24,32},{32,40},{40,48},{48,56},{56,64},{64,7... | collective-permute-start | bytes 786440 | tf_op jit(solution)/shard_map/ppermute | solution.py:23
  59.7 7.1 %collective-permute-done.12 = bf16[32,4096]{1,0:T(8,128)(2,1)} collective-permute-done((bf16[32,4096]{1,0:T(8,128)(2,1)}, bf16[32,4096]{1,0:T(8,128)(2,1)}, u32[]{:S(2)}, u32[]{:S(2)}) %collective-permute-start.12) | collective-permute-done | bytes 262176 | tf_op jit(solution)/shard_map/ppermute | solution.py:23
  68.1 4.3 %collective-permute-start.15 = (bf16[32,4096]{1,0:T(8,128)(2,1)S(1)}, bf16[32,4096]{1,0:T(8,128)(2,1)S(1)}, u32[]{:S(2)}, u32[]{:S(2)}) collective-permute-start(bf16[32,4096]{1,0:T(8,128)(2,1)S(1)} %shard_map.135.b3), channel_id=1, source_target_pairs={{0,1},{1,0},{2,3},{3,2},{4,5},{5,4},{6,7},{7,6},{8,9},{9,8},{10,11... | collective-permute-start | bytes 786440 | tf_op jit(solution)/shard_map/ppermute | solution.py:19
  72.3 3.2 %collective-permute-start.14 = (bf16[32,4096]{1,0:T(8,128)(2,1)S(1)}, bf16[32,4096]{1,0:T(8,128)(2,1)S(1)}, u32[]{:S(2)}, u32[]{:S(2)}) collective-permute-start(bf16[32,4096]{1,0:T(8,128)(2,1)S(1)} %shard_map.135.b3), channel_id=1, source_target_pairs={{0,6},{1,7},{2,0},{3,1},{4,2},{5,3},{6,4},{7,5},{8,14},{9,15},{10,... | collective-permute-start | bytes 786440 | tf_op jit(solution)/shard_map/ppermute | solution.py:15
  75.6 3.8 %collective-permute-done.15.b2 = bf16[32,4096]{1,0:T(8,128)(2,1)S(1)} collective-permute-done((bf16[32,4096]{1,0:T(8,128)(2,1)S(1)}, bf16[32,4096]{1,0:T(8,128)(2,1)S(1)}, u32[]{:S(2)}, u32[]{:S(2)}) %collective-permute-start.15) | collective-permute-done | bytes 262176 | tf_op jit(solution)/shard_map/ppermute | solution.py:19
  80.5 3.4 %collective-permute-done.13.b1 = bf16[32,4096]{1,0:T(8,128)(2,1)S(1)} collective-permute-done((bf16[32,4096]{1,0:T(8,128)(2,1)S(1)}, bf16[32,4096]{1,0:T(8,128)(2,1)S(1)}, u32[]{:S(2)}, u32[]{:S(2)}) %collective-permute-start.13) | collective-permute-done | bytes 262176 | tf_op jit(solution)/shard_map/ppermute | solution.py:15
  83.9 1.7 %collective-permute-start.16 = (bf16[32,4096]{1,0:T(8,128)(2,1)S(1)}, bf16[32,4096]{1,0:T(8,128)(2,1)S(1)}, u32[]{:S(2)}, u32[]{:S(2)}) collective-permute-start(bf16[32,4096]{1,0:T(8,128)(2,1)S(1)} %collective-permute-done.14.b0), channel_id=1, source_target_pairs={{0,1},{1,0},{2,3},{3,2},{4,5},{5,4},{6,7},{7,6},{8,9},{9,8},{10,11... | collective-permute-start | bytes 786440 | tf_op jit(solution)/shard_map/ppermute | solution.py:19
  85.9 3.5 %collective-permute-start.19 = (bf16[32,4096]{1,0:T(8,128)(2,1)S(1)}, bf16[32,4096]{1,0:T(8,128)(2,1)S(1)}, u32[]{:S(2)}, u32[]{:S(2)}) collective-permute-start(bf16[32,4096]{1,0:T(8,128)(2,1)S(1)} %collective-permute-done.15.b2), channel_id=1, source_target_pairs={{0,4},{1,5},{2,6},{3,7},{4,0},{5,1},{6,2},{7,3},{8,12},{9,13},{10,... | collective-permute-start | bytes 786440 | tf_op jit(solution)/shard_map/ppermute | solution.py:15
  89.4 1.6 %copy-done.6 = bf16[1,4096,256]{2,1,0:T(8,128)(2,1)S(1)} copy-done((bf16[1,4096,256]{2,1,0:T(8,128)(2,1)S(1)}, bf16[1,4096,256]{2,1,0:T(8,128)(2,1)}, u32[]{:S(2)}) %copy-start.6) | copy-done | bytes 2097176
  95.5 1.8 %collective-permute-done.17.b1 = bf16[32,4096]{1,0:T(8,128)(2,1)S(1)} collective-permute-done((bf16[32,4096]{1,0:T(8,128)(2,1)S(1)}, bf16[32,4096]{1,0:T(8,128)(2,1)S(1)}, u32[]{:S(2)}, u32[]{:S(2)}) %collective-permute-start.17) | collective-permute-done | bytes 262176 | tf_op jit(solution)/shard_map/ppermute | solution.py:19
  97.4 2.8 %shard_map.137 = (bf16[64,4096]{1,0:T(8,128)(2,1)S(1)}, bf16[64,4096]{1,0:T(8,128)(2,1)S(1)}, bf16[128,256]{1,0:T(8,128)(2,1)S(1)}, f32[1,1,256,256]{3,2,1,0:T(8,128)}) custom-call(bf16[32,4096]{1,0:T(8,128)(2,1)S(1)} %collective-permute-done.16.b0, bf16[32,4096]{1,0:T(8,128)(2,1)S(1)} %collective-permute-done.17.b1, ...), custom_call_target="tpu_custom_call" | custom-call | flops 1073741824 | bytes 8388608 | tf_op jit(solution)/shard_map/pallas_call | solution.py:151
  100.2 3.1 %collective-permute-start.20 = (bf16[64,4096]{1,0:T(8,128)(2,1)S(1)}, bf16[64,4096]{1,0:T(8,128)(2,1)S(1)}, u32[]{:S(2)}, u32[]{:S(2)}) collective-permute-start(bf16[64,4096]{1,0:T(8,128)(2,1)S(1)} %get-tuple-element.60), channel_id=1, source_target_pairs={{0,4},{1,5},{2,6},{3,7},{4,0},{5,1},{6,2},{7,3},{8,12},{9,13},{10,... | collective-permute-start | bytes 1572872 | tf_op jit(solution)/shard_map/ppermute | solution.py:15
  103.3 1.7 %collective-permute-start.21 = (bf16[64,4096]{1,0:T(8,128)(2,1)S(1)}, bf16[64,4096]{1,0:T(8,128)(2,1)S(1)}, u32[]{:S(2)}, u32[]{:S(2)}) collective-permute-start(bf16[64,4096]{1,0:T(8,128)(2,1)S(1)} %get-tuple-element.62), channel_id=1, source_target_pairs={{0,1},{1,0},{2,3},{3,2},{4,5},{5,4},{6,7},{7,6},{8,9},{9,8},{10,11... | collective-permute-start | bytes 1572872 | tf_op jit(solution)/shard_map/ppermute | solution.py:19
  106.7 7.4 %collective-permute-done.20 = bf16[64,4096]{1,0:T(8,128)(2,1)S(1)} collective-permute-done((bf16[64,4096]{1,0:T(8,128)(2,1)S(1)}, bf16[64,4096]{1,0:T(8,128)(2,1)S(1)}, u32[]{:S(2)}, u32[]{:S(2)}) %collective-permute-start.20) | collective-permute-done | bytes 524320 | tf_op jit(solution)/shard_map/ppermute | solution.py:15
  114.2 3.4 %collective-permute-start.24 = (bf16[32,4096]{1,0:T(8,128)(2,1)S(1)}, bf16[32,4096]{1,0:T(8,128)(2,1)S(1)}, u32[]{:S(2)}, u32[]{:S(2)}) collective-permute-start(bf16[32,4096]{1,0:T(8,128)(2,1)S(1)} %add_convert_fusion), channel_id=1, source_target_pairs={{0,1},{1,0},{2,3},{3,2},{4,5},{5,4},{6,7},{7,6},{8,9},{9,8},{10,11... | collective-permute-start | bytes 786440 | tf_op jit(solution)/shard_map/ppermute | solution.py:19
  117.8 3.2 %collective-permute-start.23 = (bf16[32,4096]{1,0:T(8,128)(2,1)S(1)}, bf16[32,4096]{1,0:T(8,128)(2,1)S(1)}, u32[]{:S(2)}, u32[]{:S(2)}) collective-permute-start(bf16[32,4096]{1,0:T(8,128)(2,1)S(1)} %get-tuple-element.67), channel_id=1, source_target_pairs={{0,6},{1,7},{2,0},{3,1},{4,2},{5,3},{6,4},{7,5},{8,14},{9,15},{10,... | collective-permute-start | bytes 786440 | tf_op jit(solution)/shard_map/ppermute | solution.py:15
  121.9 3.4 %collective-permute-done.22 = bf16[32,4096]{1,0:T(8,128)(2,1)S(1)} collective-permute-done((bf16[32,4096]{1,0:T(8,128)(2,1)S(1)}, bf16[32,4096]{1,0:T(8,128)(2,1)S(1)}, u32[]{:S(2)}, u32[]{:S(2)}) %collective-permute-start.22) | collective-permute-done | bytes 262176 | tf_op jit(solution)/shard_map/ppermute | solution.py:15
  (80 shorter events, 24.7 us)
Async XLA Ops:
  2.7 8.3 %collective-permute-start.2 = (bf16[32,4096]{1,0:T(8,128)(2,1)S(1)}, bf16[32,4096]{1,0:T(8,128)(2,1)S(1)}, u32[]{:S(2)}, u32[]{:S(2)}) collective-permute-start(bf16[32,4096]{1,0:T(8,128)(2,1)S(1)} %shard_map.131.b3), channel_id=1, source_target_pairs={{0,1},{1,0},{2,3},{3,2},{4,5},{5,4},{6,7},{7,6},{8,9},{9,8},{10,11... | collective-permute-start | bytes 786440 | tf_op jit(solution)/shard_map/ppermute | solution.py:19
  4.7 8.0 %collective-permute-start.1 = (bf16[32,4096]{1,0:T(8,128)(2,1)S(1)}, bf16[32,4096]{1,0:T(8,128)(2,1)S(1)}, u32[]{:S(2)}, u32[]{:S(2)}) collective-permute-start(bf16[32,4096]{1,0:T(8,128)(2,1)S(1)} %shard_map.131.b3), channel_id=1, source_target_pairs={{0,6},{1,7},{2,0},{3,1},{4,2},{5,3},{6,4},{7,5},{8,14},{9,15},{10,... | collective-permute-start | bytes 786440 | tf_op jit(solution)/shard_map/ppermute | solution.py:15
  7.5 8.8 %collective-permute-start = (bf16[32,4096]{1,0:T(8,128)(2,1)S(1)}, bf16[32,4096]{1,0:T(8,128)(2,1)}, u32[]{:S(2)}, u32[]{:S(2)}) collective-permute-start(bf16[32,4096]{1,0:T(8,128)(2,1)S(1)} %shard_map.131.b3), channel_id=1, source_target_pairs={{0,2},{1,3},{2,4},{3,5},{4,6},{5,7},{6,0},{7,1},{8,10},{9,11},{10,... | collective-permute-start | bytes 786440 | tf_op jit(solution)/shard_map/ppermute | solution.py:15
  16.3 14.5 %collective-permute-start.5 = (bf16[32,4096]{1,0:T(8,128)(2,1)S(1)}, bf16[32,4096]{1,0:T(8,128)(2,1)S(1)}, u32[]{:S(2)}, u32[]{:S(2)}) collective-permute-start(bf16[32,4096]{1,0:T(8,128)(2,1)S(1)} %shard_map.131.b3), channel_id=1, source_target_pairs={{0,4},{1,5},{2,6},{3,7},{4,0},{5,1},{6,2},{7,3},{8,12},{9,13},{10,... | collective-permute-start | bytes 786440 | tf_op jit(solution)/shard_map/ppermute | solution.py:15
  16.3 14.5 %collective-permute-start.3 = (bf16[32,4096]{1,0:T(8,128)(2,1)S(1)}, bf16[32,4096]{1,0:T(8,128)(2,1)S(1)}, u32[]{:S(2)}, u32[]{:S(2)}) collective-permute-start(bf16[32,4096]{1,0:T(8,128)(2,1)S(1)} %collective-permute-done.1.b0), channel_id=1, source_target_pairs={{0,1},{1,0},{2,3},{3,2},{4,5},{5,4},{6,7},{7,6},{8,9},{9,8},{10,11... | collective-permute-start | bytes 786440 | tf_op jit(solution)/shard_map/ppermute | solution.py:19
  16.6 14.1 %collective-permute-start.4 = (bf16[32,4096]{1,0:T(8,128)(2,1)}, bf16[32,4096]{1,0:T(8,128)(2,1)S(1)}, u32[]{:S(2)}, u32[]{:S(2)}) collective-permute-start(bf16[32,4096]{1,0:T(8,128)(2,1)} %collective-permute-done.b1), channel_id=1, source_target_pairs={{0,1},{1,0},{2,3},{3,2},{4,5},{5,4},{6,7},{7,6},{8,9},{9,8},{10,11... | collective-permute-start | bytes 786440 | tf_op jit(solution)/shard_map/ppermute | solution.py:19
  18.3 12.5 %collective-permute-start.6 = (bf16[32,4096]{1,0:T(8,128)(2,1)S(1)}, bf16[32,4096]{1,0:T(8,128)(2,1)S(1)}, u32[]{:S(2)}, u32[]{:S(2)}) collective-permute-start(bf16[32,4096]{1,0:T(8,128)(2,1)S(1)} %collective-permute-done.2.b2), channel_id=1, source_target_pairs={{0,4},{1,5},{2,6},{3,7},{4,0},{5,1},{6,2},{7,3},{8,12},{9,13},{10,... | collective-permute-start | bytes 786440 | tf_op jit(solution)/shard_map/ppermute | solution.py:15
  28.3 3.5 %copy-start.9 = (bf16[1,4096,256]{2,1,0:T(8,128)(2,1)S(1)}, bf16[1,4096,256]{2,1,0:T(8,128)(2,1)}, u32[]{:S(2)}) copy-start(bf16[1,4096,256]{2,1,0:T(8,128)(2,1)} %wv.7) | copy-start | bytes 6291460
  28.3 3.5 %copy-start.16 = (f32[1,1,256,256]{3,2,1,0:T(8,128)S(1)}, f32[1,1,256,256]{3,2,1,0:T(8,128)}, u32[]{:S(2)}) copy-start(f32[1,1,256,256]{3,2,1,0:T(8,128)} %state.1) | copy-start | bytes 786436
  35.6 12.6 %collective-permute-start.7 = (bf16[64,4096]{1,0:T(8,128)(2,1)S(1)}, bf16[64,4096]{1,0:T(8,128)(2,1)S(1)}, u32[]{:S(2)}, u32[]{:S(2)}) collective-permute-start(bf16[64,4096]{1,0:T(8,128)(2,1)S(1)} %get-tuple-element.44), channel_id=1, source_target_pairs={{0,4},{1,5},{2,6},{3,7},{4,0},{5,1},{6,2},{7,3},{8,12},{9,13},{10,... | collective-permute-start | bytes 1572872 | tf_op jit(solution)/shard_map/ppermute | solution.py:15
  35.7 13.4 %collective-permute-start.8 = (bf16[64,4096]{1,0:T(8,128)(2,1)S(1)}, bf16[64,4096]{1,0:T(8,128)(2,1)S(1)}, u32[]{:S(2)}, u32[]{:S(2)}) collective-permute-start(bf16[64,4096]{1,0:T(8,128)(2,1)S(1)} %get-tuple-element.46), channel_id=1, source_target_pairs={{0,1},{1,0},{2,3},{3,2},{4,5},{5,4},{6,7},{7,6},{8,9},{9,8},{10,11... | collective-permute-start | bytes 1572872 | tf_op jit(solution)/shard_map/ppermute | solution.py:19
  36.2 20.7 %copy-start.15 = (f32[1,32,4096]{2,1,0:T(8,128)S(1)}, f32[1,32,4096]{2,1,0:T(8,128)}, u32[]{:S(2)}) copy-start(f32[1,32,4096]{2,1,0:T(8,128)} %param.12) | copy-start | bytes 1572868
  48.3 18.4 %copy-start.19 = (f32[32,4096]{1,0:T(8,128)S(1)}, f32[32,4096]{1,0:T(8,128)}, u32[]{:S(2)}) copy-start(f32[32,4096]{1,0:T(8,128)} %param.13) | copy-start | bytes 1572868
  48.3 6.5 %collective-permute-start.11 = (bf16[32,4096]{1,0:T(8,128)(2,1)S(1)}, bf16[32,4096]{1,0:T(8,128)(2,1)S(1)}, u32[]{:S(2)}, u32[]{:S(2)}) collective-permute-start(bf16[32,4096]{1,0:T(8,128)(2,1)S(1)} %add_convert_fusion.4), channel_id=1, source_target_pairs={{0,1},{1,0},{2,3},{3,2},{4,5},{5,4},{6,7},{7,6},{8,9},{9,8},{10,11... | collective-permute-start | bytes 786440 | tf_op jit(solution)/shard_map/ppermute | solution.py:19
  49.2 18.6 %copy-start.18 = (f32[1,4096]{1,0:T(1,128)S(1)}, f32[1,4096]{1,0:T(1,128)}, u32[]{:S(2)}) copy-start(f32[1,4096]{1,0:T(1,128)} %gain_ref.3) | copy-start | bytes 49156
  49.2 7.7 %collective-permute-start.9 = (bf16[32,4096]{1,0:T(8,128)(2,1)S(1)}, bf16[32,4096]{1,0:T(8,128)(2,1)S(1)}, u32[]{:S(2)}, u32[]{:S(2)}) collective-permute-start(bf16[32,4096]{1,0:T(8,128)(2,1)S(1)} %get-tuple-element.68), channel_id=1, source_target_pairs={{0,2},{1,3},{2,4},{3,5},{4,6},{5,7},{6,0},{7,1},{8,10},{9,11},{10,... | collective-permute-start | bytes 786440 | tf_op jit(solution)/shard_map/ppermute | solution.py:15
  49.3 7.6 %collective-permute-start.10 = (bf16[32,4096]{1,0:T(8,128)(2,1)S(1)}, bf16[32,4096]{1,0:T(8,128)(2,1)S(1)}, u32[]{:S(2)}, u32[]{:S(2)}) collective-permute-start(bf16[32,4096]{1,0:T(8,128)(2,1)S(1)} %get-tuple-element.69), channel_id=1, source_target_pairs={{0,6},{1,7},{2,0},{3,1},{4,2},{5,3},{6,4},{7,5},{8,14},{9,15},{10,... | collective-permute-start | bytes 786440 | tf_op jit(solution)/shard_map/ppermute | solution.py:15
  57.7 9.0 %collective-permute-start.12 = (bf16[32,4096]{1,0:T(8,128)(2,1)}, bf16[32,4096]{1,0:T(8,128)(2,1)}, u32[]{:S(2)}, u32[]{:S(2)}) collective-permute-start(bf16[32,4096]{1,0:T(8,128)(2,1)} %add_convert_fusion.3), channel_id=1, source_target_pairs={{0,8},{8,16},{16,24},{24,32},{32,40},{40,48},{48,56},{56,64},{64,7... | collective-permute-start | bytes 786440 | tf_op jit(solution)/shard_map/ppermute | solution.py:23
  59.7 29.8 %copy-start.3 = (bf16[1,4096,256]{2,1,0:T(8,128)(2,1)S(1)}, bf16[1,4096,256]{2,1,0:T(8,128)(2,1)}, u32[]{:S(2)}) copy-start(bf16[1,4096,256]{2,1,0:T(8,128)(2,1)} %wq.7) | copy-start | bytes 6291460
  68.1 11.3 %collective-permute-start.15 = (bf16[32,4096]{1,0:T(8,128)(2,1)S(1)}, bf16[32,4096]{1,0:T(8,128)(2,1)S(1)}, u32[]{:S(2)}, u32[]{:S(2)}) collective-permute-start(bf16[32,4096]{1,0:T(8,128)(2,1)S(1)} %shard_map.135.b3), channel_id=1, source_target_pairs={{0,1},{1,0},{2,3},{3,2},{4,5},{5,4},{6,7},{7,6},{8,9},{9,8},{10,11... | collective-permute-start | bytes 786440 | tf_op jit(solution)/shard_map/ppermute | solution.py:19
  72.3 8.1 %collective-permute-start.14 = (bf16[32,4096]{1,0:T(8,128)(2,1)S(1)}, bf16[32,4096]{1,0:T(8,128)(2,1)S(1)}, u32[]{:S(2)}, u32[]{:S(2)}) collective-permute-start(bf16[32,4096]{1,0:T(8,128)(2,1)S(1)} %shard_map.135.b3), channel_id=1, source_target_pairs={{0,6},{1,7},{2,0},{3,1},{4,2},{5,3},{6,4},{7,5},{8,14},{9,15},{10,... | collective-permute-start | bytes 786440 | tf_op jit(solution)/shard_map/ppermute | solution.py:15
  75.6 8.3 %collective-permute-start.13 = (bf16[32,4096]{1,0:T(8,128)(2,1)S(1)}, bf16[32,4096]{1,0:T(8,128)(2,1)S(1)}, u32[]{:S(2)}, u32[]{:S(2)}) collective-permute-start(bf16[32,4096]{1,0:T(8,128)(2,1)S(1)} %shard_map.135.b3), channel_id=1, source_target_pairs={{0,2},{1,3},{2,4},{3,5},{4,6},{5,7},{6,0},{7,1},{8,10},{9,11},{10,... | collective-permute-start | bytes 786440 | tf_op jit(solution)/shard_map/ppermute | solution.py:15
  83.9 11.6 %collective-permute-start.18 = (bf16[32,4096]{1,0:T(8,128)(2,1)S(1)}, bf16[32,4096]{1,0:T(8,128)(2,1)S(1)}, u32[]{:S(2)}, u32[]{:S(2)}) collective-permute-start(bf16[32,4096]{1,0:T(8,128)(2,1)S(1)} %shard_map.135.b3), channel_id=1, source_target_pairs={{0,4},{1,5},{2,6},{3,7},{4,0},{5,1},{6,2},{7,3},{8,12},{9,13},{10,... | collective-permute-start | bytes 786440 | tf_op jit(solution)/shard_map/ppermute | solution.py:15
  83.9 11.6 %collective-permute-start.16 = (bf16[32,4096]{1,0:T(8,128)(2,1)S(1)}, bf16[32,4096]{1,0:T(8,128)(2,1)S(1)}, u32[]{:S(2)}, u32[]{:S(2)}) collective-permute-start(bf16[32,4096]{1,0:T(8,128)(2,1)S(1)} %collective-permute-done.14.b0), channel_id=1, source_target_pairs={{0,1},{1,0},{2,3},{3,2},{4,5},{5,4},{6,7},{7,6},{8,9},{9,8},{10,11... | collective-permute-start | bytes 786440 | tf_op jit(solution)/shard_map/ppermute | solution.py:19
  85.5 11.7 %collective-permute-start.17 = (bf16[32,4096]{1,0:T(8,128)(2,1)S(1)}, bf16[32,4096]{1,0:T(8,128)(2,1)S(1)}, u32[]{:S(2)}, u32[]{:S(2)}) collective-permute-start(bf16[32,4096]{1,0:T(8,128)(2,1)S(1)} %collective-permute-done.13.b1), channel_id=1, source_target_pairs={{0,1},{1,0},{2,3},{3,2},{4,5},{5,4},{6,7},{7,6},{8,9},{9,8},{10,11... | collective-permute-start | bytes 786440 | tf_op jit(solution)/shard_map/ppermute | solution.py:19
  85.9 11.5 %collective-permute-start.19 = (bf16[32,4096]{1,0:T(8,128)(2,1)S(1)}, bf16[32,4096]{1,0:T(8,128)(2,1)S(1)}, u32[]{:S(2)}, u32[]{:S(2)}) collective-permute-start(bf16[32,4096]{1,0:T(8,128)(2,1)S(1)} %collective-permute-done.15.b2), channel_id=1, source_target_pairs={{0,4},{1,5},{2,6},{3,7},{4,0},{5,1},{6,2},{7,3},{8,12},{9,13},{10,... | collective-permute-start | bytes 786440 | tf_op jit(solution)/shard_map/ppermute | solution.py:15
  94.2 3.2 %copy-start.7 = (bf16[1,4096,256]{2,1,0:T(8,128)(2,1)S(1)}, bf16[1,4096,256]{2,1,0:T(8,128)(2,1)}, u32[]{:S(2)}) copy-start(bf16[1,4096,256]{2,1,0:T(8,128)(2,1)} %wk.7) | copy-start | bytes 6291460
  100.2 13.9 %collective-permute-start.20 = (bf16[64,4096]{1,0:T(8,128)(2,1)S(1)}, bf16[64,4096]{1,0:T(8,128)(2,1)S(1)}, u32[]{:S(2)}, u32[]{:S(2)}) collective-permute-start(bf16[64,4096]{1,0:T(8,128)(2,1)S(1)} %get-tuple-element.60), channel_id=1, source_target_pairs={{0,4},{1,5},{2,6},{3,7},{4,0},{5,1},{6,2},{7,3},{8,12},{9,13},{10,... | collective-permute-start | bytes 1572872 | tf_op jit(solution)/shard_map/ppermute | solution.py:15
  103.3 14.2 %collective-permute-start.21 = (bf16[64,4096]{1,0:T(8,128)(2,1)S(1)}, bf16[64,4096]{1,0:T(8,128)(2,1)S(1)}, u32[]{:S(2)}, u32[]{:S(2)}) collective-permute-start(bf16[64,4096]{1,0:T(8,128)(2,1)S(1)} %get-tuple-element.62), channel_id=1, source_target_pairs={{0,1},{1,0},{2,3},{3,2},{4,5},{5,4},{6,7},{7,6},{8,9},{9,8},{10,11... | collective-permute-start | bytes 1572872 | tf_op jit(solution)/shard_map/ppermute | solution.py:19
  114.2 7.8 %collective-permute-start.24 = (bf16[32,4096]{1,0:T(8,128)(2,1)S(1)}, bf16[32,4096]{1,0:T(8,128)(2,1)S(1)}, u32[]{:S(2)}, u32[]{:S(2)}) collective-permute-start(bf16[32,4096]{1,0:T(8,128)(2,1)S(1)} %add_convert_fusion), channel_id=1, source_target_pairs={{0,1},{1,0},{2,3},{3,2},{4,5},{5,4},{6,7},{7,6},{8,9},{9,8},{10,11... | collective-permute-start | bytes 786440 | tf_op jit(solution)/shard_map/ppermute | solution.py:19
  117.7 7.7 %collective-permute-start.22 = (bf16[32,4096]{1,0:T(8,128)(2,1)S(1)}, bf16[32,4096]{1,0:T(8,128)(2,1)S(1)}, u32[]{:S(2)}, u32[]{:S(2)}) collective-permute-start(bf16[32,4096]{1,0:T(8,128)(2,1)S(1)} %get-tuple-element.66), channel_id=1, source_target_pairs={{0,2},{1,3},{2,4},{3,5},{4,6},{5,7},{6,0},{7,1},{8,10},{9,11},{10,... | collective-permute-start | bytes 786440 | tf_op jit(solution)/shard_map/ppermute | solution.py:15
  117.8 7.6 %collective-permute-start.23 = (bf16[32,4096]{1,0:T(8,128)(2,1)S(1)}, bf16[32,4096]{1,0:T(8,128)(2,1)S(1)}, u32[]{:S(2)}, u32[]{:S(2)}) collective-permute-start(bf16[32,4096]{1,0:T(8,128)(2,1)S(1)} %get-tuple-element.67), channel_id=1, source_target_pairs={{0,6},{1,7},{2,0},{3,1},{4,2},{5,3},{6,4},{7,5},{8,14},{9,15},{10,... | collective-permute-start | bytes 786440 | tf_op jit(solution)/shard_map/ppermute | solution.py:15
  (13 other events, 22.3 us)

commit v3 on v2

v3 whole, which is shorter than its diff:
```python
import jax
import jax.numpy as jnp
from jax import lax
from jax.experimental import pallas as pl
from jax.experimental.pallas import tpu as pltpu
from jax.sharding import PartitionSpec as P

EPSILON = 1e-05
VMEM = pl.BlockSpec(memory_space=pltpu.VMEM)
SMEM = pl.BlockSpec(memory_space=pltpu.SMEM)
HBM = pl.BlockSpec(memory_space=pltpu.HBM)
MIB = 1024 * 1024
LIMIT = 16 * MIB
ORDER = ((1, 1), (3, 1), (2, 0), (2, 1), (1, 0), (3, 0), (0, 1), (0, 0))


def shift_x(value, steps):
    return lax.ppermute(value, "tensor", [(t, (t + 2 * steps) % 8) for t in range(8)])


def swap_z(value):
    return lax.ppermute(value, "tensor", [(t, t ^ 1) for t in range(8)])


def next_section(value):
    return lax.ppermute(value, "section", [(s, s + 1) for s in range(lax.axis_size("section") - 1)])


def shape(dims, dtype):
    return jax.ShapeDtypeStruct(tuple(dims), dtype)


def call(kernel, out_shape, in_specs, flops=0, moved=0, scratch=(), limit=LIMIT):
    return pl.pallas_call(
        kernel,
        out_shape=out_shape,
        in_specs=in_specs,
        out_specs=jax.tree.map(lambda _: VMEM, out_shape),
        scratch_shapes=scratch,
        cost_estimate=pl.CostEstimate(flops=flops, bytes_accessed=moved, transcendentals=0),
        compiler_params=pltpu.CompilerParams(vmem_limit_bytes=limit),
    )


def normed(rows, gain):
    centred = rows - jnp.mean(rows, axis=-1, keepdims=True)
    spread = jnp.mean(centred * centred, axis=-1, keepdims=True)
    return (centred * lax.rsqrt(spread + EPSILON) * gain).astype(jnp.bfloat16)


def first_norm_kernel(rows_hbm, gain_hbm, state_hbm, out_ref, state_ref, rows_ref, gain_ref, sems):
    pairs = ((rows_hbm, rows_ref), (gain_hbm, gain_ref), (state_hbm, state_ref))
    copies = [pltpu.make_async_copy(source, target, sems.at[i]) for i, (source, target) in enumerate(pairs)]
    for copy in copies:
        copy.start()
    copies[0].wait()
    copies[1].wait()
    out_ref[...] = normed(rows_ref[0], gain_ref[...])
    copies[2].wait()


def second_norm_kernel(arrived_ref, fresh_ref, gain_ref, rows_ref, out_ref):
    rows = jnp.where(lax.axis_index("section") == 0, fresh_ref[...], arrived_ref[...].astype(jnp.float32))
    rows_ref[0] = rows
    out_ref[...] = normed(rows, gain_ref[...])


def setup_kernel(
    log_keep_ref, wq_hbm, wk_hbm, wv_hbm, wg_hbm, wo_hbm, wq, wk, wv, wg, wo, decay, lead, tail, sems
):
    pairs = ((wq_hbm, wq), (wk_hbm, wk), (wv_hbm, wv), (wg_hbm, wg), (wo_hbm, wo))
    copies = [pltpu.make_async_copy(source, target, sems.at[i]) for i, (source, target) in enumerate(pairs)]
    for copy in copies:
        copy.start()
    group = decay.shape[0]
    count = group // len(ORDER)
    log_keep = log_keep_ref[0, 0]
    here = lax.axis_index("tensor")
    row = lax.broadcasted_iota(jnp.int32, (group, group), 0)
    column = lax.broadcasted_iota(jnp.int32, (group, group), 1)

    def position(index):
        block = index // count
        start = jnp.zeros_like(index)
        for place, (steps, mate) in enumerate(ORDER):
            start = jnp.where(block == place, (((here + 2 * steps) & 7) ^ mate) * count, start)
        return (start + index % count).astype(jnp.float32)

    at_row, at_column = position(row), position(column)
    offsets = at_row - at_column
    decay[...] = jnp.where(offsets >= 0, jnp.exp(jnp.maximum(offsets, 0.0) * log_keep), 0.0)
    lead[...] = jnp.exp((at_row[:, :1] + 1.0) * log_keep)
    tail[...] = jnp.exp((group - 1.0 - at_row[:, :1]) * log_keep)
    for copy in copies:
        copy.wait()


def dot(a, b):
    return jnp.dot(a, b, preferred_element_type=jnp.float32)


def dot_over(a, b, axis_a, axis_b):
    return lax.dot_general(a, b, (((axis_a,), (axis_b,)), ((), ())), preferred_element_type=jnp.float32)


def project(blocks, weights):
    rows = jnp.concatenate([block[...] for block in blocks], axis=0)
    w_query, w_key, w_value, w_gate = weights
    scale = w_key.shape[2] ** -0.5
    return (
        dot(rows, w_query[0]).astype(jnp.bfloat16),
        (dot(rows, w_key[0]) * scale).astype(jnp.bfloat16),
        dot(rows, w_value[0]).astype(jnp.bfloat16),
        dot(rows, w_gate[0]),
    )


def early_kernel(b0, b1, b2, b3, wq, wk, wv, wg, queries, keys, values, gates):
    queries[...], keys[...], values[...], gates[...] = project((b0, b1, b2, b3), (wq, wk, wv, wg))


def split(value):
    high = value.astype(jnp.bfloat16)
    return high, (value - high.astype(jnp.float32)).astype(jnp.bfloat16)


def late_kernel(
    b0, b1, b2, b3, wq, wk, wv, wg, early_q, early_k, early_v, early_g, state, decay, lead, w_out,
    over_z, over_x, gated_late, keys, values,
):
    late = project((b0, b1, b2, b3), (wq, wk, wv, wg))
    q, k, v, gate = (
        jnp.concatenate([a, b[...]], axis=0) for a, b in zip(late, (early_q, early_k, early_v, early_g))
    )
    half = early_q.shape[0]
    weighted = (dot_over(q, k, 1, 1) * decay[...]).astype(jnp.bfloat16)
    high, low = split(state[0, 0])
    mixed = dot(weighted, v) + (dot(q, high) + dot(q, low)) * lead[...]
    centred = mixed - jnp.mean(mixed, axis=-1, keepdims=True)
    head_out = centred * lax.rsqrt(jnp.mean(centred * centred, axis=-1, keepdims=True) + EPSILON)
    gated = (gate / (1.0 + jnp.exp(-gate)) * head_out).astype(jnp.bfloat16)
    partial = dot(gated[:half], w_out[0]).astype(jnp.bfloat16)
    over_z[...] = partial[: half // 2]
    over_x[...] = partial[half // 2 :]
    gated_late[...] = gated[half:]
    keys[...] = k
    values[...] = v


def out_kernel(log_keep_ref, gated, w_out, keys, values, tail, state, up, down, mate, own, new_state):
    count = own.shape[0]
    up[...] = dot(gated[:count], w_out[0]).astype(jnp.bfloat16)
    down[...] = dot(gated[count : 2 * count], w_out[0]).astype(jnp.bfloat16)
    mate[...] = dot(gated[2 * count : 3 * count], w_out[0]).astype(jnp.bfloat16)
    own[...] = dot(gated[3 * count :], w_out[0])
    high, low = split(keys[...].astype(jnp.float32) * tail[...])
    added = dot_over(high, values[...], 0, 0) + dot_over(low, values[...], 0, 0)
    keep = jnp.exp(jnp.full((1, 1), keys.shape[0], jnp.float32) * log_keep_ref[0, 0])
    new_state[0, 0] = keep * state[0, 0] + added


def relay_kernel(up, down, to_mate, via_z, via_x, up_sum, down_sum, mate_sum):
    count = up.shape[0]
    f32, bf16 = jnp.float32, jnp.bfloat16
    up_sum[...] = (up[...].astype(f32) + via_z[:count].astype(f32)).astype(bf16)
    down_sum[...] = (down[...].astype(f32) + via_z[count:].astype(f32)).astype(bf16)
    mate_sum[...] = (to_mate[...].astype(f32) + via_x[count:].astype(f32)).astype(bf16)


def sum_kernel(rows, own, via_x, got_up, got_down, got_mate, out):
    total = rows[0] + own[...] + via_x[: own.shape[0]].astype(jnp.float32)
    for part in (got_up, got_down, got_mate):
        total = total + part[...].astype(jnp.float32)
    out[...] = total.astype(out.dtype).reshape(out.shape)


def body(inflow, fresh, states, rates, norm_gain, w_query, w_key, w_value, w_gate, w_out):
    count, width = fresh.shape
    key_size, value_size = states.shape[2:]
    group = count * lax.axis_size("tensor")
    half = group // 2
    bf16, f32 = jnp.bfloat16, jnp.float32
    block = shape((count, width), bf16)
    double = shape((2 * count, width), bf16)
    log_keep = jnp.log1p(-rates)
    heavy = {"flops": 2 * half * width * 2 * (key_size + value_size), "moved": 2 * width * 2 * (key_size + value_size)}
    own, state = call(
        first_norm_kernel,
        [block, shape(states.shape, f32)],
        [HBM] * 3,
        moved=6 * count * width,
        scratch=[pltpu.VMEM(inflow.shape, f32), pltpu.VMEM(norm_gain.shape, f32), pltpu.SemaphoreType.DMA((3,))],
        limit=56 * MIB,
    )(inflow, norm_gain, states)
    rows = inflow
    for turn_index in range(2):
        above, below, mate = shift_x(own, -1), shift_x(own, 1), swap_z(own)
        if turn_index == 0:
            *weights, out_weight, decay, lead, tail = call(
                setup_kernel,
                [shape(a.shape, a.dtype) for a in (w_query, w_key, w_value, w_gate, w_out)]
                + [shape((group, group), f32), shape((group, 1), f32), shape((group, 1), f32)],
                [SMEM] + [HBM] * 5,
                moved=10 * 1024 * 1024,
                scratch=[pltpu.SemaphoreType.DMA((5,))],
                limit=42 * MIB,
                    )(log_keep, w_query, w_key, w_value, w_gate, w_out)
        above, below, mate, held, decay = lax.optimization_barrier((above, below, mate, own, decay))
        mate_above, mate_below = swap_z(above), swap_z(below)
        far, far_mate = shift_x(held, 2), shift_x(mate, 2)
        early = call(
            early_kernel,
            [shape((half, key_size), bf16)] * 2 + [shape((half, value_size), bf16), shape((half, value_size), f32)],
            [VMEM] * 8,
            **heavy,
        )(above, below, mate, own, *weights)
        over_z, over_x, gated_late, keys, values = call(
            late_kernel,
            [double] * 2
            + [shape((half, value_size), bf16), shape((group, key_size), bf16), shape((group, value_size), bf16)],
            [VMEM] * 16,
            **heavy,
        )(mate_above, mate_below, far, far_mate, *weights, *early, state, decay, lead, out_weight)
        via_x, via_z = shift_x(over_x, 2), swap_z(over_z)
        up, down, to_mate, mine, state = call(
            out_kernel,
            [block] * 3 + [shape((count, width), f32), shape(state.shape, f32)],
            [SMEM] + [VMEM] * 6,
            flops=2 * half * value_size * width,
            moved=2 * value_size * width,
        )(log_keep, gated_late, out_weight, keys, values, tail, state)
        up, down, to_mate = call(relay_kernel, [block] * 3, [VMEM] * 5, moved=8 * count * width)(
            up, down, to_mate, via_z, via_x
        )
        got_up, got_down, got_mate = shift_x(up, 1), shift_x(down, -1), swap_z(to_mate)
        parts = (rows, mine, via_x, got_up, got_down, got_mate)
        if turn_index == 0:
            result = call(sum_kernel, block, [VMEM] * 6, moved=16 * count * width)(*parts)
            arrived = next_section(result)
            rows, own = call(
                second_norm_kernel, [shape(inflow.shape, f32), block], [VMEM] * 3, moved=12 * count * width
            )(arrived, fresh, norm_gain)
        else:
            rows = call(sum_kernel, shape(inflow.shape, f32), [VMEM] * 6, moved=16 * count * width)(*parts)
    return (rows, state)


def solution(mesh):
    in_specs = (
        P("section", "tensor", None),
        P("tensor", None),
        P("section", "tensor", None, None),
        P("section", "tensor"),
        P("section", None),
        P("section", None, "tensor"),
        P("section", None, "tensor"),
        P("section", None, "tensor"),
        P("section", None, "tensor"),
        P("section", "tensor", None),
    )
    out_specs = (P("section", "tensor", None), P("section", "tensor", None, None))
    return jax.shard_map(body, mesh=mesh, in_specs=in_specs, out_specs=out_specs, check_vma=False)
```

time: 128 us -> 122 us (0.953)
  the two profiles are of different devices: /device:TPU:88 before, /device:TPU:128 now
where the time goes in v3:
time: 122 us; the launch traced here: 121 us
  waiting for transfers between devices  64.5 us (53%)
  starting transfers between devices  36.3 us (30%)
  Pallas kernels  19.1 us (16%)
  between operations  1.45 us (1%)
    ppermute x14, waiting for transfers between devices, shift_x(): lax.ppermute(value, 'tensor', [(t, (t + 2 * steps) % 8) for t in range(8)])  42.7 us
    ppermute x14, starting transfers between devices, shift_x(): lax.ppermute(value, 'tensor', [(t, (t + 2 * steps) % 8) for t in range(8)])  24.5 us
    ppermute x10, waiting for transfers between devices, swap_z(): return lax.ppermute(value, 'tensor', [(t, t ^ 1) for t in range(8)])  12.5 us
    ppermute x10, starting transfers between devices, swap_z(): return lax.ppermute(value, 'tensor', [(t, t ^ 1) for t in range(8)])  9.95 us
    ppermute x1, waiting for transfers between devices, next_section(): lax.ppermute(value, 'section', [(s, s + 1) for s in range(lax.axis_size('...  9.29 us
    pallas_call x2, Pallas kernels, body(): call(late_kernel, [double] * 2 + [shape((half, value_size), bf16), shape(...  4.2 us
    pallas_call x1, Pallas kernels, body(): call(setup_kernel, [shape(a.shape, a.dtype) for a in (w_query, w_key, w_v...  4.14 us
    pallas_call x2, Pallas kernels, body(): call(out_kernel, [block] * 3 + [shape((count, width), f32), shape(state.s...  4.1 us
  transfers between devices with their start and end apart: 25, of which 17 were waited for; matrix products, arithmetic and copies ran while one was open for 0% of the time, Pallas kernels for 9%

profile of v3, /device:TPU:128, one launch (start us, length us, event | category | flops | bytes accessed | tf_op | source)
XLA Modules:
  0.0 121.4 jit_solution(5900134296030450103)
XLA Ops:
  0.6 2.2 %shard_map.113 = (bf16[32,4096]{1,0:T(8,128)(2,1)}, f32[1,1,256,256]{3,2,1,0:T(8,128)}) custom-call(f32[1,32,4096]{2,1,0:T(8,128)} %rows.1, f32[1,4096]{1,0:T(1,128)} %gain_ref.1, f32[1,1,256,256]{3,2,1,0:T(8,128)} %state_hbm.1), custom_call_target="tpu_custom_call" | custom-call | bytes 786432 | tf_op jit(solution)/shard_map/pallas_call | solution.py:187
  3.9 1.5 %collective-permute-start.1 = (bf16[32,4096]{1,0:T(8,128)(2,1)}, bf16[32,4096]{1,0:T(8,128)(2,1)S(1)}, u32[]{:S(2)}, u32[]{:S(2)}) collective-permute-start(bf16[32,4096]{1,0:T(8,128)(2,1)} %get-tuple-element.62.b3), channel_id=1, source_target_pairs={{0,2},{1,3},{2,4},{3,5},{4,6},{5,7},{6,0},{7,1},{8,10},{9,11},{10,... | collective-permute-start | bytes 786440 | tf_op jit(solution)/shard_map/ppermute | solution.py:18
  5.4 1.7 %collective-permute-start = (bf16[32,4096]{1,0:T(8,128)(2,1)}, bf16[32,4096]{1,0:T(8,128)(2,1)S(1)}, u32[]{:S(2)}, u32[]{:S(2)}) collective-permute-start(bf16[32,4096]{1,0:T(8,128)(2,1)} %get-tuple-element.62.b3), channel_id=1, source_target_pairs={{0,6},{1,7},{2,0},{3,1},{4,2},{5,3},{6,4},{7,5},{8,14},{9,15},{10,... | collective-permute-start | bytes 786440 | tf_op jit(solution)/shard_map/ppermute | solution.py:18
  7.8 4.1 %shard_map.114 = (bf16[1,4096,256]{2,1,0:T(8,128)(2,1)S(1)}, bf16[1,4096,256]{2,1,0:T(8,128)(2,1)S(1)}, bf16[1,4096,256]{2,1,0:T(8,128)(2,1)S(1)}, bf16[1,4096,2...) custom-call(f32[1,1]{1,0:T(1,128)S(6)} %log1p.3.log_keep_ref, ...), custom_call_target="tpu_custom_call" | custom-call | bytes 10485760 | tf_op jit(solution)/shard_map/pallas_call | solution.py:199
  13.1 2.7 %collective-permute-start.5 = (bf16[32,4096]{1,0:T(8,128)(2,1)S(1)}, bf16[32,4096]{1,0:T(8,128)(2,1)S(1)}, u32[]{:S(2)}, u32[]{:S(2)}) collective-permute-start(bf16[32,4096]{1,0:T(8,128)(2,1)S(1)} %copy-done.3), channel_id=1, source_target_pairs={{0,4},{1,5},{2,6},{3,7},{4,0},{5,1},{6,2},{7,3},{8,12},{9,13},{10,... | collective-permute-start | bytes 786440 | tf_op jit(solution)/shard_map/ppermute | solution.py:18
  20.0 3.5 %collective-permute-done.5.b2 = bf16[32,4096]{1,0:T(8,128)(2,1)S(1)} collective-permute-done((bf16[32,4096]{1,0:T(8,128)(2,1)S(1)}, bf16[32,4096]{1,0:T(8,128)(2,1)S(1)}, u32[]{:S(2)}, u32[]{:S(2)}) %collective-permute-start.5) | collective-permute-done | bytes 262176 | tf_op jit(solution)/shard_map/ppermute | solution.py:18
  23.4 1.5 %collective-permute-done.3.b0 = bf16[32,4096]{1,0:T(8,128)(2,1)S(1)} collective-permute-done((bf16[32,4096]{1,0:T(8,128)(2,1)S(1)}, bf16[32,4096]{1,0:T(8,128)(2,1)S(1)}, u32[]{:S(2)}, u32[]{:S(2)}) %collective-permute-start.3) | collective-permute-done | bytes 262176 | tf_op jit(solution)/shard_map/ppermute | solution.py:22
  24.9 2.8 %collective-permute-done.4.b1 = bf16[32,4096]{1,0:T(8,128)(2,1)S(1)} collective-permute-done((bf16[32,4096]{1,0:T(8,128)(2,1)S(1)}, bf16[32,4096]{1,0:T(8,128)(2,1)S(1)}, u32[]{:S(2)}, u32[]{:S(2)}) %collective-permute-start.4) | collective-permute-done | bytes 262176 | tf_op jit(solution)/shard_map/ppermute | solution.py:22
  27.7 2.1 %shard_map.116 = (bf16[64,4096]{1,0:T(8,128)(2,1)S(1)}, bf16[64,4096]{1,0:T(8,128)(2,1)S(1)}, bf16[128,256]{1,0:T(8,128)(2,1)S(1)}, bf16[256,256]{1,0:T(8,128)(2,1)S(1)}, bf16[256,256]{1,0:T(8,128)(2,1)S(1)}) custom-call(bf16[32,4096]{1,0:T(8,128)(2,1)S(1)} %collective-permute-done.3.b0, bf16[32,4096]{1,0:T(8,128)(2,1)S(1)} %collective-permute-done.4.b1, ...), custom_call_target="tpu_custom_call" | custom-call | flops 1073741824 | bytes 8388608 | tf_op jit(solution)/shard_map/pallas_call | solution.py:217
  29.8 1.9 %collective-permute-start.7 = (bf16[64,4096]{1,0:T(8,128)(2,1)S(1)}, bf16[64,4096]{1,0:T(8,128)(2,1)S(1)}, u32[]{:S(2)}, u32[]{:S(2)}) collective-permute-start(bf16[64,4096]{1,0:T(8,128)(2,1)S(1)} %get-tuple-element.81), channel_id=1, source_target_pairs={{0,4},{1,5},{2,6},{3,7},{4,0},{5,1},{6,2},{7,3},{8,12},{9,13},{10,... | collective-permute-start | bytes 1572872 | tf_op jit(solution)/shard_map/ppermute | solution.py:18
  32.7 1.7 %shard_map.117 = (bf16[32,4096]{1,0:T(8,128)(2,1)S(1)}, bf16[32,4096]{1,0:T(8,128)(2,1)S(1)}, bf16[32,4096]{1,0:T(8,128)(2,1)S(1)}, f32[32,4096]{1,0:T(8,128)S(1)}, f32[1,1,256,256]{3,2,1,0:T(8,128)S(1)}) custom-call(f32[1,1]{1,0:T(1,128)S(6)} %log1p.3.log_keep_ref, bf16[128,256]{1,0:T(8,128)(2,1)S(1)} %get-tuple-element.76.gated, ...), custom_call_target="tpu_custom_call" | custom-call | flops 268435456 | bytes 2097152 | tf_op jit(solution)/shard_map/pallas_call | solution.py:225
  34.4 8.3 %collective-permute-done.7.via_x = bf16[64,4096]{1,0:T(8,128)(2,1)S(1)} collective-permute-done((bf16[64,4096]{1,0:T(8,128)(2,1)S(1)}, bf16[64,4096]{1,0:T(8,128)(2,1)S(1)}, u32[]{:S(2)}, u32[]{:S(2)}) %collective-permute-start.7) | collective-permute-done | bytes 524320 | tf_op jit(solution)/shard_map/ppermute | solution.py:18
  44.1 2.2 %collective-permute-start.10 = (bf16[32,4096]{1,0:T(8,128)(2,1)S(1)}, bf16[32,4096]{1,0:T(8,128)(2,1)S(1)}, u32[]{:S(2)}, u32[]{:S(2)}) collective-permute-start(bf16[32,4096]{1,0:T(8,128)(2,1)S(1)} %get-tuple-element.87), channel_id=1, source_target_pairs={{0,6},{1,7},{2,0},{3,1},{4,2},{5,3},{6,4},{7,5},{8,14},{9,15},{10,... | collective-permute-start | bytes 786440 | tf_op jit(solution)/shard_map/ppermute | solution.py:18
  47.3 3.3 %collective-permute-done.9.got_up = bf16[32,4096]{1,0:T(8,128)(2,1)S(1)} collective-permute-done((bf16[32,4096]{1,0:T(8,128)(2,1)S(1)}, bf16[32,4096]{1,0:T(8,128)(2,1)S(1)}, u32[]{:S(2)}, u32[]{:S(2)}) %collective-permute-start.9) | collective-permute-done | bytes 262176 | tf_op jit(solution)/shard_map/ppermute | solution.py:18
  50.6 2.0 %collective-permute-done.11.got_mate = bf16[32,4096]{1,0:T(8,128)(2,1)S(1)} collective-permute-done((bf16[32,4096]{1,0:T(8,128)(2,1)S(1)}, bf16[32,4096]{1,0:T(8,128)(2,1)S(1)}, u32[]{:S(2)}, u32[]{:S(2)}) %collective-permute-start.11) | collective-permute-done | bytes 262176 | tf_op jit(solution)/shard_map/ppermute | solution.py:22
  52.8 1.9 %collective-permute-start.12 = (bf16[32,4096]{1,0:T(8,128)(2,1)S(1)}, bf16[32,4096]{1,0:T(8,128)(2,1)S(1)}, u32[]{:S(2)}, u32[]{:S(2)}) collective-permute-start(bf16[32,4096]{1,0:T(8,128)(2,1)S(1)} %shard_map.119), channel_id=1, source_target_pairs={{0,8},{8,16},{16,24},{24,32},{32,40},{40,48},{48,56},{56,64},{64,7... | collective-permute-start | bytes 786440 | tf_op jit(solution)/shard_map/ppermute | solution.py:26
  54.8 9.3 %collective-permute-done.12.arrived_ref = bf16[32,4096]{1,0:T(8,128)(2,1)S(1)} collective-permute-done((bf16[32,4096]{1,0:T(8,128)(2,1)S(1)}, bf16[32,4096]{1,0:T(8,128)(2,1)S(1)}, u32[]{:S(2)}, u32[]{:S(2)}) %collective-permute-start.12) | collective-permute-done | bytes 262176 | tf_op jit(solution)/shard_map/ppermute | solution.py:26
  64.4 2.5 %collective-permute-start.15 = (bf16[32,4096]{1,0:T(8,128)(2,1)S(1)}, bf16[32,4096]{1,0:T(8,128)(2,1)S(1)}, u32[]{:S(2)}, u32[]{:S(2)}) collective-permute-start(bf16[32,4096]{1,0:T(8,128)(2,1)S(1)} %get-tuple-element.93.b3), channel_id=1, source_target_pairs={{0,1},{1,0},{2,3},{3,2},{4,5},{5,4},{6,7},{7,6},{8,9},{9,8},{10,11... | collective-permute-start | bytes 786440 | tf_op jit(solution)/shard_map/ppermute | solution.py:22
  66.9 3.2 %collective-permute-start.13 = (bf16[32,4096]{1,0:T(8,128)(2,1)S(1)}, bf16[32,4096]{1,0:T(8,128)(2,1)S(1)}, u32[]{:S(2)}, u32[]{:S(2)}) collective-permute-start(bf16[32,4096]{1,0:T(8,128)(2,1)S(1)} %get-tuple-element.93.b3), channel_id=1, source_target_pairs={{0,6},{1,7},{2,0},{3,1},{4,2},{5,3},{6,4},{7,5},{8,14},{9,15},{10,... | collective-permute-start | bytes 786440 | tf_op jit(solution)/shard_map/ppermute | solution.py:18
  71.2 8.8 %collective-permute-done.14.b1 = bf16[32,4096]{1,0:T(8,128)(2,1)S(1)} collective-permute-done((bf16[32,4096]{1,0:T(8,128)(2,1)S(1)}, bf16[32,4096]{1,0:T(8,128)(2,1)S(1)}, u32[]{:S(2)}, u32[]{:S(2)}) %collective-permute-start.14) | collective-permute-done | bytes 262176 | tf_op jit(solution)/shard_map/ppermute | solution.py:18
  80.1 2.0 %collective-permute-start.17 = (bf16[32,4096]{1,0:T(8,128)(2,1)S(1)}, bf16[32,4096]{1,0:T(8,128)(2,1)S(1)}, u32[]{:S(2)}, u32[]{:S(2)}) collective-permute-start(bf16[32,4096]{1,0:T(8,128)(2,1)S(1)} %collective-permute-done.14.b1), channel_id=1, source_target_pairs={{0,1},{1,0},{2,3},{3,2},{4,5},{5,4},{6,7},{7,6},{8,9},{9,8},{10,11... | collective-permute-start | bytes 786440 | tf_op jit(solution)/shard_map/ppermute | solution.py:22
  82.1 3.5 %collective-permute-start.19 = (bf16[32,4096]{1,0:T(8,128)(2,1)S(1)}, bf16[32,4096]{1,0:T(8,128)(2,1)S(1)}, u32[]{:S(2)}, u32[]{:S(2)}) collective-permute-start(bf16[32,4096]{1,0:T(8,128)(2,1)S(1)} %collective-permute-done.15.b2), channel_id=1, source_target_pairs={{0,4},{1,5},{2,6},{3,7},{4,0},{5,1},{6,2},{7,3},{8,12},{9,13},{10,... | collective-permute-start | bytes 786440 | tf_op jit(solution)/shard_map/ppermute | solution.py:18
  87.0 2.8 %collective-permute-done.18.b2 = bf16[32,4096]{1,0:T(8,128)(2,1)S(1)} collective-permute-done((bf16[32,4096]{1,0:T(8,128)(2,1)S(1)}, bf16[32,4096]{1,0:T(8,128)(2,1)S(1)}, u32[]{:S(2)}, u32[]{:S(2)}) %collective-permute-start.18) | collective-permute-done | bytes 262176 | tf_op jit(solution)/shard_map/ppermute | solution.py:18
  89.8 2.7 %collective-permute-done.17.b1 = bf16[32,4096]{1,0:T(8,128)(2,1)S(1)} collective-permute-done((bf16[32,4096]{1,0:T(8,128)(2,1)S(1)}, bf16[32,4096]{1,0:T(8,128)(2,1)S(1)}, u32[]{:S(2)}, u32[]{:S(2)}) %collective-permute-start.17) | collective-permute-done | bytes 262176 | tf_op jit(solution)/shard_map/ppermute | solution.py:22
  92.5 2.9 %collective-permute-done.19.b3 = bf16[32,4096]{1,0:T(8,128)(2,1)S(1)} collective-permute-done((bf16[32,4096]{1,0:T(8,128)(2,1)S(1)}, bf16[32,4096]{1,0:T(8,128)(2,1)S(1)}, u32[]{:S(2)}, u32[]{:S(2)}) %collective-permute-start.19) | collective-permute-done | bytes 262176 | tf_op jit(solution)/shard_map/ppermute | solution.py:18
  95.4 2.1 %shard_map.122 = (bf16[64,4096]{1,0:T(8,128)(2,1)S(1)}, bf16[64,4096]{1,0:T(8,128)(2,1)S(1)}, bf16[128,256]{1,0:T(8,128)(2,1)S(1)}, bf16[256,256]{1,0:T(8,128)(2,1)S(1)}, bf16[256,256]{1,0:T(8,128)(2,1)S(1)}) custom-call(bf16[32,4096]{1,0:T(8,128)(2,1)S(1)} %collective-permute-done.16.b0, bf16[32,4096]{1,0:T(8,128)(2,1)S(1)} %collective-permute-done.17.b1, ...), custom_call_target="tpu_custom_call" | custom-call | flops 1073741824 | bytes 8388608 | tf_op jit(solution)/shard_map/pallas_call | solution.py:217
  97.5 2.4 %collective-permute-start.20 = (bf16[64,4096]{1,0:T(8,128)(2,1)S(1)}, bf16[64,4096]{1,0:T(8,128)(2,1)S(1)}, u32[]{:S(2)}, u32[]{:S(2)}) collective-permute-start(bf16[64,4096]{1,0:T(8,128)(2,1)S(1)} %get-tuple-element.105), channel_id=1, source_target_pairs={{0,4},{1,5},{2,6},{3,7},{4,0},{5,1},{6,2},{7,3},{8,12},{9,13},{10,... | collective-permute-start | bytes 1572872 | tf_op jit(solution)/shard_map/ppermute | solution.py:18
  100.0 2.4 %shard_map.123 = (bf16[32,4096]{1,0:T(8,128)(2,1)S(1)}, bf16[32,4096]{1,0:T(8,128)(2,1)S(1)}, bf16[32,4096]{1,0:T(8,128)(2,1)S(1)}, f32[32,4096]{1,0:T(8,128)S(1)}, f32[1,1,256,256]{3,2,1,0:T(8,128)}) custom-call(f32[1,1]{1,0:T(1,128)S(6)} %log1p.3.log_keep_ref, bf16[128,256]{1,0:T(8,128)(2,1)S(1)} %get-tuple-element.101.gated, ...), custom_call_target="tpu_custom_call" | custom-call | flops 268435456 | bytes 2097152 | tf_op jit(solution)/shard_map/pallas_call | solution.py:225
  102.4 7.8 %collective-permute-done.20.via_x = bf16[64,4096]{1,0:T(8,128)(2,1)S(1)} collective-permute-done((bf16[64,4096]{1,0:T(8,128)(2,1)S(1)}, bf16[64,4096]{1,0:T(8,128)(2,1)S(1)}, u32[]{:S(2)}, u32[]{:S(2)}) %collective-permute-start.20) | collective-permute-done | bytes 524320 | tf_op jit(solution)/shard_map/ppermute | solution.py:18
  111.9 2.2 %collective-permute-start.23 = (bf16[32,4096]{1,0:T(8,128)(2,1)S(1)}, bf16[32,4096]{1,0:T(8,128)(2,1)S(1)}, u32[]{:S(2)}, u32[]{:S(2)}) collective-permute-start(bf16[32,4096]{1,0:T(8,128)(2,1)S(1)} %get-tuple-element.111), channel_id=1, source_target_pairs={{0,6},{1,7},{2,0},{3,1},{4,2},{5,3},{6,4},{7,5},{8,14},{9,15},{10,... | collective-permute-start | bytes 786440 | tf_op jit(solution)/shard_map/ppermute | solution.py:18
  114.3 4.1 %collective-permute-done.22.got_up = bf16[32,4096]{1,0:T(8,128)(2,1)S(1)} collective-permute-done((bf16[32,4096]{1,0:T(8,128)(2,1)S(1)}, bf16[32,4096]{1,0:T(8,128)(2,1)S(1)}, u32[]{:S(2)}, u32[]{:S(2)}) %collective-permute-start.22) | collective-permute-done | bytes 262176 | tf_op jit(solution)/shard_map/ppermute | solution.py:18
  118.4 2.0 %collective-permute-done.24.got_mate = bf16[32,4096]{1,0:T(8,128)(2,1)S(1)} collective-permute-done((bf16[32,4096]{1,0:T(8,128)(2,1)S(1)}, bf16[32,4096]{1,0:T(8,128)(2,1)S(1)}, u32[]{:S(2)}, u32[]{:S(2)}) %collective-permute-start.24) | collective-permute-done | bytes 262176 | tf_op jit(solution)/shard_map/ppermute | solution.py:22
  (41 shorter events, 15.6 us)
Async XLA Ops:
  2.8 9.2 %collective-permute-start.2 = (bf16[32,4096]{1,0:T(8,128)(2,1)}, bf16[32,4096]{1,0:T(8,128)(2,1)S(1)}, u32[]{:S(2)}, u32[]{:S(2)}) collective-permute-start(bf16[32,4096]{1,0:T(8,128)(2,1)} %get-tuple-element.62.b3), channel_id=1, source_target_pairs={{0,1},{1,0},{2,3},{3,2},{4,5},{5,4},{6,7},{7,6},{8,9},{9,8},{10,11... | collective-permute-start | bytes 786440 | tf_op jit(solution)/shard_map/ppermute | solution.py:22
  3.9 9.2 %collective-permute-start.1 = (bf16[32,4096]{1,0:T(8,128)(2,1)}, bf16[32,4096]{1,0:T(8,128)(2,1)S(1)}, u32[]{:S(2)}, u32[]{:S(2)}) collective-permute-start(bf16[32,4096]{1,0:T(8,128)(2,1)} %get-tuple-element.62.b3), channel_id=1, source_target_pairs={{0,2},{1,3},{2,4},{3,5},{4,6},{5,7},{6,0},{7,1},{8,10},{9,11},{10,... | collective-permute-start | bytes 786440 | tf_op jit(solution)/shard_map/ppermute | solution.py:18
  5.4 7.7 %collective-permute-start = (bf16[32,4096]{1,0:T(8,128)(2,1)}, bf16[32,4096]{1,0:T(8,128)(2,1)S(1)}, u32[]{:S(2)}, u32[]{:S(2)}) collective-permute-start(bf16[32,4096]{1,0:T(8,128)(2,1)} %get-tuple-element.62.b3), channel_id=1, source_target_pairs={{0,6},{1,7},{2,0},{3,1},{4,2},{5,3},{6,4},{7,5},{8,14},{9,15},{10,... | collective-permute-start | bytes 786440 | tf_op jit(solution)/shard_map/ppermute | solution.py:18
  7.8 5.3 %copy-start.3 = (bf16[32,4096]{1,0:T(8,128)(2,1)S(1)}, bf16[32,4096]{1,0:T(8,128)(2,1)}, u32[]{:S(2)}) copy-start(bf16[32,4096]{1,0:T(8,128)(2,1)} %get-tuple-element.62.b3) | copy-start | bytes 786436
  13.1 10.3 %collective-permute-start.5 = (bf16[32,4096]{1,0:T(8,128)(2,1)S(1)}, bf16[32,4096]{1,0:T(8,128)(2,1)S(1)}, u32[]{:S(2)}, u32[]{:S(2)}) collective-permute-start(bf16[32,4096]{1,0:T(8,128)(2,1)S(1)} %copy-done.3), channel_id=1, source_target_pairs={{0,4},{1,5},{2,6},{3,7},{4,0},{5,1},{6,2},{7,3},{8,12},{9,13},{10,... | collective-permute-start | bytes 786440 | tf_op jit(solution)/shard_map/ppermute | solution.py:18
  15.8 9.1 %collective-permute-start.3 = (bf16[32,4096]{1,0:T(8,128)(2,1)S(1)}, bf16[32,4096]{1,0:T(8,128)(2,1)S(1)}, u32[]{:S(2)}, u32[]{:S(2)}) collective-permute-start(bf16[32,4096]{1,0:T(8,128)(2,1)S(1)} %collective-permute-done.b0), channel_id=1, source_target_pairs={{0,1},{1,0},{2,3},{3,2},{4,5},{5,4},{6,7},{7,6},{8,9},{9,8},{10,11... | collective-permute-start | bytes 786440 | tf_op jit(solution)/shard_map/ppermute | solution.py:22
  16.8 10.9 %collective-permute-start.4 = (bf16[32,4096]{1,0:T(8,128)(2,1)S(1)}, bf16[32,4096]{1,0:T(8,128)(2,1)S(1)}, u32[]{:S(2)}, u32[]{:S(2)}) collective-permute-start(bf16[32,4096]{1,0:T(8,128)(2,1)S(1)} %collective-permute-done.1.b1), channel_id=1, source_target_pairs={{0,1},{1,0},{2,3},{3,2},{4,5},{5,4},{6,7},{7,6},{8,9},{9,8},{10,11... | collective-permute-start | bytes 786440 | tf_op jit(solution)/shard_map/ppermute | solution.py:22
  17.9 9.9 %collective-permute-start.6 = (bf16[32,4096]{1,0:T(8,128)(2,1)S(1)}, bf16[32,4096]{1,0:T(8,128)(2,1)S(1)}, u32[]{:S(2)}, u32[]{:S(2)}) collective-permute-start(bf16[32,4096]{1,0:T(8,128)(2,1)S(1)} %collective-permute-done.2.b2), channel_id=1, source_target_pairs={{0,4},{1,5},{2,6},{3,7},{4,0},{5,1},{6,2},{7,3},{8,12},{9,13},{10,... | collective-permute-start | bytes 786440 | tf_op jit(solution)/shard_map/ppermute | solution.py:18
  18.7 9.1 %copy-start.1 = (f32[1,1,256,256]{3,2,1,0:T(8,128)S(1)}, f32[1,1,256,256]{3,2,1,0:T(8,128)}, u32[]{:S(2)}) copy-start(f32[1,1,256,256]{3,2,1,0:T(8,128)} %get-tuple-element.72.state) | copy-start | bytes 786436
  29.8 12.9 %collective-permute-start.7 = (bf16[64,4096]{1,0:T(8,128)(2,1)S(1)}, bf16[64,4096]{1,0:T(8,128)(2,1)S(1)}, u32[]{:S(2)}, u32[]{:S(2)}) collective-permute-start(bf16[64,4096]{1,0:T(8,128)(2,1)S(1)} %get-tuple-element.81), channel_id=1, source_target_pairs={{0,4},{1,5},{2,6},{3,7},{4,0},{5,1},{6,2},{7,3},{8,12},{9,13},{10,... | collective-permute-start | bytes 1572872 | tf_op jit(solution)/shard_map/ppermute | solution.py:18
  31.7 11.1 %collective-permute-start.8 = (bf16[64,4096]{1,0:T(8,128)(2,1)S(1)}, bf16[64,4096]{1,0:T(8,128)(2,1)S(1)}, u32[]{:S(2)}, u32[]{:S(2)}) collective-permute-start(bf16[64,4096]{1,0:T(8,128)(2,1)S(1)} %get-tuple-element.85), channel_id=1, source_target_pairs={{0,1},{1,0},{2,3},{3,2},{4,5},{5,4},{6,7},{7,6},{8,9},{9,8},{10,11... | collective-permute-start | bytes 1572872 | tf_op jit(solution)/shard_map/ppermute | solution.py:22
  32.7 19.9 %copy-start = (f32[1,32,4096]{2,1,0:T(8,128)S(1)}, f32[1,32,4096]{2,1,0:T(8,128)}, u32[]{:S(2)}) copy-start(f32[1,32,4096]{2,1,0:T(8,128)} %rows.1) | copy-start | bytes 1572868
  42.8 21.3 %copy-start.2 = (f32[32,4096]{1,0:T(8,128)S(1)}, f32[32,4096]{1,0:T(8,128)}, u32[]{:S(2)}) copy-start(f32[32,4096]{1,0:T(8,128)} %fresh_ref.1) | copy-start | bytes 1572868
  42.8 21.3 %copy-start.4 = (f32[1,4096]{1,0:T(1,128)S(1)}, f32[1,4096]{1,0:T(1,128)}, u32[]{:S(2)}) copy-start(f32[1,4096]{1,0:T(1,128)} %gain_ref.1) | copy-start | bytes 49156
  43.0 7.7 %collective-permute-start.9 = (bf16[32,4096]{1,0:T(8,128)(2,1)S(1)}, bf16[32,4096]{1,0:T(8,128)(2,1)S(1)}, u32[]{:S(2)}, u32[]{:S(2)}) collective-permute-start(bf16[32,4096]{1,0:T(8,128)(2,1)S(1)} %get-tuple-element.86), channel_id=1, source_target_pairs={{0,2},{1,3},{2,4},{3,5},{4,6},{5,7},{6,0},{7,1},{8,10},{9,11},{10,... | collective-permute-start | bytes 786440 | tf_op jit(solution)/shard_map/ppermute | solution.py:18
  44.1 6.5 %collective-permute-start.10 = (bf16[32,4096]{1,0:T(8,128)(2,1)S(1)}, bf16[32,4096]{1,0:T(8,128)(2,1)S(1)}, u32[]{:S(2)}, u32[]{:S(2)}) collective-permute-start(bf16[32,4096]{1,0:T(8,128)(2,1)S(1)} %get-tuple-element.87), channel_id=1, source_target_pairs={{0,6},{1,7},{2,0},{3,1},{4,2},{5,3},{6,4},{7,5},{8,14},{9,15},{10,... | collective-permute-start | bytes 786440 | tf_op jit(solution)/shard_map/ppermute | solution.py:18
  46.3 6.4 %collective-permute-start.11 = (bf16[32,4096]{1,0:T(8,128)(2,1)S(1)}, bf16[32,4096]{1,0:T(8,128)(2,1)S(1)}, u32[]{:S(2)}, u32[]{:S(2)}) collective-permute-start(bf16[32,4096]{1,0:T(8,128)(2,1)S(1)} %get-tuple-element.88), channel_id=1, source_target_pairs={{0,1},{1,0},{2,3},{3,2},{4,5},{5,4},{6,7},{7,6},{8,9},{9,8},{10,11... | collective-permute-start | bytes 786440 | tf_op jit(solution)/shard_map/ppermute | solution.py:22
  52.8 11.2 %collective-permute-start.12 = (bf16[32,4096]{1,0:T(8,128)(2,1)S(1)}, bf16[32,4096]{1,0:T(8,128)(2,1)S(1)}, u32[]{:S(2)}, u32[]{:S(2)}) collective-permute-start(bf16[32,4096]{1,0:T(8,128)(2,1)S(1)} %shard_map.119), channel_id=1, source_target_pairs={{0,8},{8,16},{16,24},{24,32},{32,40},{40,48},{48,56},{56,64},{64,7... | collective-permute-start | bytes 786440 | tf_op jit(solution)/shard_map/ppermute | solution.py:26
  64.4 6.8 %collective-permute-start.15 = (bf16[32,4096]{1,0:T(8,128)(2,1)S(1)}, bf16[32,4096]{1,0:T(8,128)(2,1)S(1)}, u32[]{:S(2)}, u32[]{:S(2)}) collective-permute-start(bf16[32,4096]{1,0:T(8,128)(2,1)S(1)} %get-tuple-element.93.b3), channel_id=1, source_target_pairs={{0,1},{1,0},{2,3},{3,2},{4,5},{5,4},{6,7},{7,6},{8,9},{9,8},{10,11... | collective-permute-start | bytes 786440 | tf_op jit(solution)/shard_map/ppermute | solution.py:22
  66.9 13.2 %collective-permute-start.14 = (bf16[32,4096]{1,0:T(8,128)(2,1)S(1)}, bf16[32,4096]{1,0:T(8,128)(2,1)S(1)}, u32[]{:S(2)}, u32[]{:S(2)}) collective-permute-start(bf16[32,4096]{1,0:T(8,128)(2,1)S(1)} %get-tuple-element.93.b3), channel_id=1, source_target_pairs={{0,2},{1,3},{2,4},{3,5},{4,6},{5,7},{6,0},{7,1},{8,10},{9,11},{10,... | collective-permute-start | bytes 786440 | tf_op jit(solution)/shard_map/ppermute | solution.py:18
  66.9 13.2 %collective-permute-start.13 = (bf16[32,4096]{1,0:T(8,128)(2,1)S(1)}, bf16[32,4096]{1,0:T(8,128)(2,1)S(1)}, u32[]{:S(2)}, u32[]{:S(2)}) collective-permute-start(bf16[32,4096]{1,0:T(8,128)(2,1)S(1)} %get-tuple-element.93.b3), channel_id=1, source_target_pairs={{0,6},{1,7},{2,0},{3,1},{4,2},{5,3},{6,4},{7,5},{8,14},{9,15},{10,... | collective-permute-start | bytes 786440 | tf_op jit(solution)/shard_map/ppermute | solution.py:18
  80.1 9.7 %collective-permute-start.18 = (bf16[32,4096]{1,0:T(8,128)(2,1)S(1)}, bf16[32,4096]{1,0:T(8,128)(2,1)S(1)}, u32[]{:S(2)}, u32[]{:S(2)}) collective-permute-start(bf16[32,4096]{1,0:T(8,128)(2,1)S(1)} %get-tuple-element.93.b3), channel_id=1, source_target_pairs={{0,4},{1,5},{2,6},{3,7},{4,0},{5,1},{6,2},{7,3},{8,12},{9,13},{10,... | collective-permute-start | bytes 786440 | tf_op jit(solution)/shard_map/ppermute | solution.py:18
  80.1 9.7 %collective-permute-start.16 = (bf16[32,4096]{1,0:T(8,128)(2,1)S(1)}, bf16[32,4096]{1,0:T(8,128)(2,1)S(1)}, u32[]{:S(2)}, u32[]{:S(2)}) collective-permute-start(bf16[32,4096]{1,0:T(8,128)(2,1)S(1)} %collective-permute-done.13.b0), channel_id=1, source_target_pairs={{0,1},{1,0},{2,3},{3,2},{4,5},{5,4},{6,7},{7,6},{8,9},{9,8},{10,11... | collective-permute-start | bytes 786440 | tf_op jit(solution)/shard_map/ppermute | solution.py:22
  80.1 12.4 %collective-permute-start.17 = (bf16[32,4096]{1,0:T(8,128)(2,1)S(1)}, bf16[32,4096]{1,0:T(8,128)(2,1)S(1)}, u32[]{:S(2)}, u32[]{:S(2)}) collective-permute-start(bf16[32,4096]{1,0:T(8,128)(2,1)S(1)} %collective-permute-done.14.b1), channel_id=1, source_target_pairs={{0,1},{1,0},{2,3},{3,2},{4,5},{5,4},{6,7},{7,6},{8,9},{9,8},{10,11... | collective-permute-start | bytes 786440 | tf_op jit(solution)/shard_map/ppermute | solution.py:22
  82.1 13.3 %collective-permute-start.19 = (bf16[32,4096]{1,0:T(8,128)(2,1)S(1)}, bf16[32,4096]{1,0:T(8,128)(2,1)S(1)}, u32[]{:S(2)}, u32[]{:S(2)}) collective-permute-start(bf16[32,4096]{1,0:T(8,128)(2,1)S(1)} %collective-permute-done.15.b2), channel_id=1, source_target_pairs={{0,4},{1,5},{2,6},{3,7},{4,0},{5,1},{6,2},{7,3},{8,12},{9,13},{10,... | collective-permute-start | bytes 786440 | tf_op jit(solution)/shard_map/ppermute | solution.py:18
  97.5 12.6 %collective-permute-start.20 = (bf16[64,4096]{1,0:T(8,128)(2,1)S(1)}, bf16[64,4096]{1,0:T(8,128)(2,1)S(1)}, u32[]{:S(2)}, u32[]{:S(2)}) collective-permute-start(bf16[64,4096]{1,0:T(8,128)(2,1)S(1)} %get-tuple-element.105), channel_id=1, source_target_pairs={{0,4},{1,5},{2,6},{3,7},{4,0},{5,1},{6,2},{7,3},{8,12},{9,13},{10,... | collective-permute-start | bytes 1572872 | tf_op jit(solution)/shard_map/ppermute | solution.py:18
  100.0 10.6 %collective-permute-start.21 = (bf16[64,4096]{1,0:T(8,128)(2,1)S(1)}, bf16[64,4096]{1,0:T(8,128)(2,1)S(1)}, u32[]{:S(2)}, u32[]{:S(2)}) collective-permute-start(bf16[64,4096]{1,0:T(8,128)(2,1)S(1)} %get-tuple-element.109), channel_id=1, source_target_pairs={{0,1},{1,0},{2,3},{3,2},{4,5},{5,4},{6,7},{7,6},{8,9},{9,8},{10,11... | collective-permute-start | bytes 1572872 | tf_op jit(solution)/shard_map/ppermute | solution.py:22
  110.7 7.7 %collective-permute-start.22 = (bf16[32,4096]{1,0:T(8,128)(2,1)S(1)}, bf16[32,4096]{1,0:T(8,128)(2,1)S(1)}, u32[]{:S(2)}, u32[]{:S(2)}) collective-permute-start(bf16[32,4096]{1,0:T(8,128)(2,1)S(1)} %get-tuple-element.110), channel_id=1, source_target_pairs={{0,2},{1,3},{2,4},{3,5},{4,6},{5,7},{6,0},{7,1},{8,10},{9,11},{10,... | collective-permute-start | bytes 786440 | tf_op jit(solution)/shard_map/ppermute | solution.py:18
  111.9 6.5 %collective-permute-start.23 = (bf16[32,4096]{1,0:T(8,128)(2,1)S(1)}, bf16[32,4096]{1,0:T(8,128)(2,1)S(1)}, u32[]{:S(2)}, u32[]{:S(2)}) collective-permute-start(bf16[32,4096]{1,0:T(8,128)(2,1)S(1)} %get-tuple-element.111), channel_id=1, source_target_pairs={{0,6},{1,7},{2,0},{3,1},{4,2},{5,3},{6,4},{7,5},{8,14},{9,15},{10,... | collective-permute-start | bytes 786440 | tf_op jit(solution)/shard_map/ppermute | solution.py:18
  114.0 6.4 %collective-permute-start.24 = (bf16[32,4096]{1,0:T(8,128)(2,1)S(1)}, bf16[32,4096]{1,0:T(8,128)(2,1)S(1)}, u32[]{:S(2)}, u32[]{:S(2)}) collective-permute-start(bf16[32,4096]{1,0:T(8,128)(2,1)S(1)} %get-tuple-element.112), channel_id=1, source_target_pairs={{0,1},{1,0},{2,3},{3,2},{4,5},{5,4},{6,7},{7,6},{8,9},{9,8},{10,11... | collective-permute-start | bytes 786440 | tf_op jit(solution)/shard_map/ppermute | solution.py:22

commit v4 on v3

--- a/solution.py
+++ b/solution.py
@@ -24,6 +24,11 @@
 
 def next_section(value):
     return lax.ppermute(value, "section", [(s, s + 1) for s in range(lax.axis_size("section") - 1)])
+
+
+def other_core(value):
+    count = lax.axis_size("section")
+    return lax.ppermute(value[:16, :128], "section", [(s, s ^ 1) for s in range(count)])
 
 
 def shape(dims, dtype):
@@ -59,7 +64,7 @@
     copies[2].wait()
 
 
-def second_norm_kernel(arrived_ref, fresh_ref, gain_ref, rows_ref, out_ref):
+def second_norm_kernel(arrived_ref, in_step_ref, fresh_ref, gain_ref, rows_ref, out_ref):
     rows = jnp.where(lax.axis_index("section") == 0, fresh_ref[...], arrived_ref[...].astype(jnp.float32))
     rows_ref[0] = rows
     out_ref[...] = normed(rows, gain_ref[...])
@@ -95,6 +100,12 @@
         copy.wait()
 
 
+def halves_kernel(above, below, left, right):
+    width = left.shape[1]
+    left[...] = above[:, :width]
+    right[...] = below[:, width:]
+
+
 def dot(a, b):
     return jnp.dot(a, b, preferred_element_type=jnp.float32)
 
@@ -125,9 +136,10 @@
 
 
 def late_kernel(
-    b0, b1, b2, b3, wq, wk, wv, wg, early_q, early_k, early_v, early_g, state, decay, lead, w_out,
-    over_z, over_x, gated_late, keys, values,
+    b0, b1, b2_left, b2_right, b3, wq, wk, wv, wg, early_q, early_k, early_v, early_g, state, decay, lead, w_out,
+    over_z, over_x, half_up, half_down, gated_late, keys, values,
 ):
+    b2 = jnp.concatenate([b2_left[...], b2_right[...]], axis=1)
     late = project((b0, b1, b2, b3), (wq, wk, wv, wg))
     q, k, v, gate = (
         jnp.concatenate([a, b[...]], axis=0) for a, b in zip(late, (early_q, early_k, early_v, early_g))
@@ -141,7 +153,10 @@
     gated = (gate / (1.0 + jnp.exp(-gate)) * head_out).astype(jnp.bfloat16)
     partial = dot(gated[:half], w_out[0]).astype(jnp.bfloat16)
     over_z[...] = partial[: half // 2]
-    over_x[...] = partial[half // 2 :]
+    count, width = half_up.shape
+    over_x[...] = partial[3 * count :]
+    half_up[...] = partial[2 * count : 3 * count, :width]
+    half_down[...] = partial[2 * count : 3 * count, width:]
     gated_late[...] = gated[half:]
     keys[...] = k
     values[...] = v
@@ -159,16 +174,20 @@
     new_state[0, 0] = keep * state[0, 0] + added
 
 
-def relay_kernel(up, down, to_mate, via_z, via_x, up_sum, down_sum, mate_sum):
-    count = up.shape[0]
-    f32, bf16 = jnp.float32, jnp.bfloat16
-    up_sum[...] = (up[...].astype(f32) + via_z[:count].astype(f32)).astype(bf16)
-    down_sum[...] = (down[...].astype(f32) + via_z[count:].astype(f32)).astype(bf16)
-    mate_sum[...] = (to_mate[...].astype(f32) + via_x[count:].astype(f32)).astype(bf16)
-
-
-def sum_kernel(rows, own, via_x, got_up, got_down, got_mate, out):
-    total = rows[0] + own[...] + via_x[: own.shape[0]].astype(jnp.float32)
+def relay_kernel(up, down, to_mate, via_z, via_x, via_up, via_down, up_sum, down_sum, mate_sum):
+    f32 = jnp.float32
+    count, width = via_up.shape
+    up_total = up[...].astype(f32) + via_z[:count].astype(f32)
+    down_total = down[...].astype(f32) + via_z[count:].astype(f32)
+    up_sum[:, :width] = (up_total[:, :width] + via_up[...].astype(f32)).astype(up_sum.dtype)
+    up_sum[:, width:] = up_total[:, width:].astype(up_sum.dtype)
+    down_sum[:, :width] = down_total[:, :width].astype(down_sum.dtype)
+    down_sum[:, width:] = (down_total[:, width:] + via_down[...].astype(f32)).astype(down_sum.dtype)
+    mate_sum[...] = (to_mate[...].astype(f32) + via_x[...].astype(f32)).astype(mate_sum.dtype)
+
+
+def sum_kernel(rows, own, got_up, got_down, got_mate, out):
+    total = rows[0] + own[...]
     for part in (got_up, got_down, got_mate):
         total = total + part[...].astype(jnp.float32)
     out[...] = total.astype(out.dtype).reshape(out.shape)
@@ -182,6 +201,7 @@
     bf16, f32 = jnp.bfloat16, jnp.float32
     block = shape((count, width), bf16)
     double = shape((2 * count, width), bf16)
+    half_block = shape((count, width // 2), bf16)
     log_keep = jnp.log1p(-rates)
     heavy = {"flops": 2 * half * width * 2 * (key_size + value_size), "moved": 2 * width * 2 * (key_size + value_size)}
     own, state = call(
@@ -205,23 +225,26 @@
                 scratch=[pltpu.SemaphoreType.DMA((5,))],
                 limit=42 * MIB,
                     )(log_keep, w_query, w_key, w_value, w_gate, w_out)
-        above, below, mate, held, decay = lax.optimization_barrier((above, below, mate, own, decay))
+        above, below, mate, decay = lax.optimization_barrier((above, below, mate, decay))
         mate_above, mate_below = swap_z(above), swap_z(below)
-        far, far_mate = shift_x(held, 2), shift_x(mate, 2)
+        far_mate = shift_x(mate, 2)
+        left, right = call(halves_kernel, [half_block] * 2, [VMEM] * 2, moved=4 * count * width)(above, below)
+        far = (shift_x(left, -1), shift_x(right, 1))
         early = call(
             early_kernel,
             [shape((half, key_size), bf16)] * 2 + [shape((half, value_size), bf16), shape((half, value_size), f32)],
             [VMEM] * 8,
             **heavy,
         )(above, below, mate, own, *weights)
-        over_z, over_x, gated_late, keys, values = call(
+        over_z, over_x, half_up, half_down, gated_late, keys, values = call(
             late_kernel,
-            [double] * 2
+            [double, block, half_block, half_block]
             + [shape((half, value_size), bf16), shape((group, key_size), bf16), shape((group, value_size), bf16)],
-            [VMEM] * 16,
+            [VMEM] * 17,
             **heavy,
-        )(mate_above, mate_below, far, far_mate, *weights, *early, state, decay, lead, out_weight)
-        via_x, via_z = shift_x(over_x, 2), swap_z(over_z)
+        )(mate_above, mate_below, *far, far_mate, *weights, *early, state, decay, lead, out_weight)
+        via_z, via_x = swap_z(over_z), shift_x(over_x, 2)
+        via_up, via_down = shift_x(half_up, 1), shift_x(half_down, -1)
         up, down, to_mate, mine, state = call(
             out_kernel,
             [block] * 3 + [shape((count, width), f32), shape(state.shape, f32)],
@@ -229,19 +252,19 @@
             flops=2 * half * value_size * width,
             moved=2 * value_size * width,
         )(log_keep, gated_late, out_weight, keys, values, tail, state)
-        up, down, to_mate = call(relay_kernel, [block] * 3, [VMEM] * 5, moved=8 * count * width)(
-            up, down, to_mate, via_z, via_x
+        up, down, to_mate = call(relay_kernel, [block] * 3, [VMEM] * 7, moved=8 * count * width)(
+            up, down, to_mate, via_z, via_x, via_up, via_down
         )
         got_up, got_down, got_mate = shift_x(up, 1), shift_x(down, -1), swap_z(to_mate)
-        parts = (rows, mine, via_x, got_up, got_down, got_mate)
+        parts = (rows, mine, got_up, got_down, got_mate)
         if turn_index == 0:
-            result = call(sum_kernel, block, [VMEM] * 6, moved=16 * count * width)(*parts)
+            result = call(sum_kernel, block, [VMEM] * 5, moved=16 * count * width)(*parts)
             arrived = next_section(result)
             rows, own = call(
-                second_norm_kernel, [shape(inflow.shape, f32), block], [VMEM] * 3, moved=12 * count * width
-            )(arrived, fresh, norm_gain)
+                second_norm_kernel, [shape(inflow.shape, f32), block], [VMEM] * 4, moved=12 * count * width
+            )(arrived, other_core(arrived), fresh, norm_gain)
         else:
-            rows = call(sum_kernel, shape(inflow.shape, f32), [VMEM] * 6, moved=16 * count * width)(*parts)
+            rows = call(sum_kernel, shape(inflow.shape, f32), [VMEM] * 5, moved=16 * count * width)(*parts)
     return (rows, state)
 
 

time: 122 us -> 116 us (0.951)
  the two profiles are of different devices: /device:TPU:128 before, /device:TPU:88 now
where the time goes in v4:
time: 116 us; the launch traced here: 114 us
  starting transfers between devices  47.3 us (41%)
  waiting for transfers between devices  45.9 us (40%)
  Pallas kernels  19.2 us (17%)
  between operations  1.47 us (1%)
    ppermute x20, starting transfers between devices, shift_x(): lax.ppermute(value, 'tensor', [(t, (t + 2 * steps) % 8) for t in range(8)])  31.8 us
    ppermute x20, waiting for transfers between devices, shift_x(): lax.ppermute(value, 'tensor', [(t, (t + 2 * steps) % 8) for t in range(8)])  25.3 us
    ppermute x10, waiting for transfers between devices, swap_z(): return lax.ppermute(value, 'tensor', [(t, t ^ 1) for t in range(8)])  13.1 us
    ppermute x10, starting transfers between devices, swap_z(): return lax.ppermute(value, 'tensor', [(t, t ^ 1) for t in range(8)])  11.2 us
    ppermute x1, waiting for transfers between devices, next_section(): lax.ppermute(value, 'section', [(s, s + 1) for s in range(lax.axis_size('...  6.76 us
    pallas_call x2, Pallas kernels, body(): call(late_kernel, [double, block, half_block, half_block] + [shape((half,...  4.2 us
    pallas_call x1, Pallas kernels, body(): call(setup_kernel, [shape(a.shape, a.dtype) for a in (w_query, w_key, w_v...  4.14 us
    pallas_call x2, Pallas kernels, body(): call(out_kernel, [block] * 3 + [shape((count, width), f32), shape(state.s...  4.1 us
  transfers between devices with their start and end apart: 32, of which 19 were waited for; matrix products, arithmetic and copies ran while one was open for 0% of the time, Pallas kernels for 10%

profile of v4, /device:TPU:88, one launch (start us, length us, event | category | flops | bytes accessed | tf_op | source)
XLA Modules:
  0.0 113.9 jit_solution(11454972947524277835)
XLA Ops:
  0.6 2.2 %shard_map.113 = (bf16[32,4096]{1,0:T(8,128)(2,1)}, f32[1,1,256,256]{3,2,1,0:T(8,128)}) custom-call(f32[1,32,4096]{2,1,0:T(8,128)} %rows.1, f32[1,4096]{1,0:T(1,128)} %gain_ref.1, f32[1,1,256,256]{3,2,1,0:T(8,128)} %state_hbm.1), custom_call_target="tpu_custom_call" | custom-call | bytes 786432 | tf_op jit(solution)/shard_map/pallas_call | solution.py:207
  2.8 2.0 %collective-permute-start.2 = (bf16[32,4096]{1,0:T(8,128)(2,1)}, bf16[32,4096]{1,0:T(8,128)(2,1)S(1)}, u32[]{:S(2)}, u32[]{:S(2)}) collective-permute-start(bf16[32,4096]{1,0:T(8,128)(2,1)} %get-tuple-element.64.b3), channel_id=1, source_target_pairs={{0,1},{1,0},{2,3},{3,2},{4,5},{5,4},{6,7},{7,6},{8,9},{9,8},{10,11... | collective-permute-start | bytes 786440 | tf_op jit(solution)/shard_map/ppermute | solution.py:22
  6.3 1.7 %collective-permute-start = (bf16[32,4096]{1,0:T(8,128)(2,1)}, bf16[32,4096]{1,0:T(8,128)(2,1)S(1)}, u32[]{:S(2)}, u32[]{:S(2)}) collective-permute-start(bf16[32,4096]{1,0:T(8,128)(2,1)} %get-tuple-element.64.b3), channel_id=1, source_target_pairs={{0,6},{1,7},{2,0},{3,1},{4,2},{5,3},{6,4},{7,5},{8,14},{9,15},{10,... | collective-permute-start | bytes 786440 | tf_op jit(solution)/shard_map/ppermute | solution.py:18
  8.7 4.1 %shard_map.114 = (bf16[1,4096,256]{2,1,0:T(8,128)(2,1)S(1)}, bf16[1,4096,256]{2,1,0:T(8,128)(2,1)S(1)}, bf16[1,4096,256]{2,1,0:T(8,128)(2,1)S(1)}, bf16[1,4096,2...) custom-call(f32[1,1]{1,0:T(1,128)S(6)} %log1p.3.log_keep_ref, ...), custom_call_target="tpu_custom_call" | custom-call | bytes 10485760 | tf_op jit(solution)/shard_map/pallas_call | solution.py:219
  14.0 2.7 %collective-permute-start.7 = (bf16[32,4096]{1,0:T(8,128)(2,1)S(1)}, bf16[32,4096]{1,0:T(8,128)(2,1)S(1)}, u32[]{:S(2)}, u32[]{:S(2)}) collective-permute-start(bf16[32,4096]{1,0:T(8,128)(2,1)S(1)} %collective-permute-done.2.b2), channel_id=1, source_target_pairs={{0,4},{1,5},{2,6},{3,7},{4,0},{5,1},{6,2},{7,3},{8,12},{9,13},{10,... | collective-permute-start | bytes 786440 | tf_op jit(solution)/shard_map/ppermute | solution.py:18
  17.1 1.7 %collective-permute-start.4 = (bf16[32,4096]{1,0:T(8,128)(2,1)S(1)}, bf16[32,4096]{1,0:T(8,128)(2,1)S(1)}, u32[]{:S(2)}, u32[]{:S(2)}) collective-permute-start(bf16[32,4096]{1,0:T(8,128)(2,1)S(1)} %collective-permute-done.1.below.b1), channel_id=1, source_target_pairs={{0,1},{1,0},{2,3},{3,2},{4,5},{5,4},{6,7},{7,6},{8,9},{9,8},{10,11... | collective-permute-start | bytes 786440 | tf_op jit(solution)/shard_map/ppermute | solution.py:22
  22.2 3.0 %collective-permute-done.5.b2_left = bf16[32,2048]{1,0:T(8,128)(2,1)S(1)} collective-permute-done((bf16[32,2048]{1,0:T(8,128)(2,1)S(1)}, bf16[32,2048]{1,0:T(8,128)(2,1)S(1)}, u32[]{:S(2)}, u32[]{:S(2)}) %collective-permute-start.5) | collective-permute-done | bytes 131104 | tf_op jit(solution)/shard_map/ppermute | solution.py:18
  26.5 2.2 %collective-permute-done.4.b1 = bf16[32,4096]{1,0:T(8,128)(2,1)S(1)} collective-permute-done((bf16[32,4096]{1,0:T(8,128)(2,1)S(1)}, bf16[32,4096]{1,0:T(8,128)(2,1)S(1)}, u32[]{:S(2)}, u32[]{:S(2)}) %collective-permute-start.4) | collective-permute-done | bytes 262176 | tf_op jit(solution)/shard_map/ppermute | solution.py:22
  28.6 2.1 %shard_map.117 = (bf16[64,4096]{1,0:T(8,128)(2,1)S(1)}, bf16[32,4096]{1,0:T(8,128)(2,1)S(1)}, bf16[32,2048]{1,0:T(8,128)(2,1)S(1)}, bf16[32,2048]{1,0:T(8,128)(2...) custom-call(bf16[32,4096]{1,0:T(8,128)(2,1)S(1)} %collective-permute-done.3.b0, ...), custom_call_target="tpu_custom_call" | custom-call | flops 1073741824 | bytes 8388608 | tf_op jit(solution)/shard_map/pallas_call | solution.py:239
  33.7 2.1 %collective-permute-start.11 = (bf16[32,2048]{1,0:T(8,128)(2,1)S(1)}, bf16[32,2048]{1,0:T(8,128)(2,1)S(1)}, u32[]{:S(2)}, u32[]{:S(2)}) collective-permute-start(bf16[32,2048]{1,0:T(8,128)(2,1)S(1)} %get-tuple-element.94), channel_id=1, source_target_pairs={{0,6},{1,7},{2,0},{3,1},{4,2},{5,3},{6,4},{7,5},{8,14},{9,15},{10,... | collective-permute-start | bytes 393224 | tf_op jit(solution)/shard_map/ppermute | solution.py:18
  35.8 1.7 %shard_map.118 = (bf16[32,4096]{1,0:T(8,128)(2,1)S(1)}, bf16[32,4096]{1,0:T(8,128)(2,1)S(1)}, bf16[32,4096]{1,0:T(8,128)(2,1)S(1)}, f32[32,4096]{1,0:T(8,128)S(1)}, f32[1,1,256,256]{3,2,1,0:T(8,128)S(1)}) custom-call(f32[1,1]{1,0:T(1,128)S(6)} %log1p.3.log_keep_ref, bf16[128,256]{1,0:T(8,128)(2,1)S(1)} %get-tuple-element.83.gated, ...), custom_call_target="tpu_custom_call" | custom-call | flops 268435456 | bytes 2097152 | tf_op jit(solution)/shard_map/pallas_call | solution.py:248
  37.5 3.6 %collective-permute-done.10.via_up = bf16[32,2048]{1,0:T(8,128)(2,1)S(1)} collective-permute-done((bf16[32,2048]{1,0:T(8,128)(2,1)S(1)}, bf16[32,2048]{1,0:T(8,128)(2,1)S(1)}, u32[]{:S(2)}, u32[]{:S(2)}) %collective-permute-start.10) | collective-permute-done | bytes 131104 | tf_op jit(solution)/shard_map/ppermute | solution.py:18
  43.2 2.2 %collective-permute-start.13 = (bf16[32,4096]{1,0:T(8,128)(2,1)S(1)}, bf16[32,4096]{1,0:T(8,128)(2,1)S(1)}, u32[]{:S(2)}, u32[]{:S(2)}) collective-permute-start(bf16[32,4096]{1,0:T(8,128)(2,1)S(1)} %get-tuple-element.96), channel_id=1, source_target_pairs={{0,6},{1,7},{2,0},{3,1},{4,2},{5,3},{6,4},{7,5},{8,14},{9,15},{10,... | collective-permute-start | bytes 786440 | tf_op jit(solution)/shard_map/ppermute | solution.py:18
  46.2 3.4 %collective-permute-done.12.got_up = bf16[32,4096]{1,0:T(8,128)(2,1)S(1)} collective-permute-done((bf16[32,4096]{1,0:T(8,128)(2,1)S(1)}, bf16[32,4096]{1,0:T(8,128)(2,1)S(1)}, u32[]{:S(2)}, u32[]{:S(2)}) %collective-permute-start.12) | collective-permute-done | bytes 262176 | tf_op jit(solution)/shard_map/ppermute | solution.py:18
  49.7 2.0 %collective-permute-done.14.got_mate = bf16[32,4096]{1,0:T(8,128)(2,1)S(1)} collective-permute-done((bf16[32,4096]{1,0:T(8,128)(2,1)S(1)}, bf16[32,4096]{1,0:T(8,128)(2,1)S(1)}, u32[]{:S(2)}, u32[]{:S(2)}) %collective-permute-start.14) | collective-permute-done | bytes 262176 | tf_op jit(solution)/shard_map/ppermute | solution.py:22
  51.9 1.9 %collective-permute-start.15 = (bf16[32,4096]{1,0:T(8,128)(2,1)S(1)}, bf16[32,4096]{1,0:T(8,128)(2,1)S(1)}, u32[]{:S(2)}, u32[]{:S(2)}) collective-permute-start(bf16[32,4096]{1,0:T(8,128)(2,1)S(1)} %shard_map.120), channel_id=1, source_target_pairs={{0,8},{8,16},{16,24},{24,32},{32,40},{40,48},{48,56},{56,64},{64,7... | collective-permute-start | bytes 786440 | tf_op jit(solution)/shard_map/ppermute | solution.py:26
  53.8 6.8 %collective-permute-done.15.arrived_ref = bf16[32,4096]{1,0:T(8,128)(2,1)S(1)} collective-permute-done((bf16[32,4096]{1,0:T(8,128)(2,1)S(1)}, bf16[32,4096]{1,0:T(8,128)(2,1)S(1)}, u32[]{:S(2)}, u32[]{:S(2)}) %collective-permute-start.15) | collective-permute-done | bytes 262176 | tf_op jit(solution)/shard_map/ppermute | solution.py:26
  60.6 2.4 %collective-permute-start.16 = (bf16[16,128]{1,0:T(8,128)(2,1)S(1)}, bf16[16,128]{1,0:T(8,128)(2,1)S(1)}, u32[]{:S(2)}, u32[]{:S(2)}) collective-permute-start(bf16[16,128]{1,0:T(8,128)(2,1)S(1)} %slice.4), channel_id=1, source_target_pairs={{0,8},{8,0},{16,24},{24,16},{32,40},{40,32},{48,56},{56,48},{64,72... | collective-permute-start | bytes 12296 | tf_op jit(solution)/shard_map/ppermute | solution.py:31
  64.2 1.7 %collective-permute-start.19 = (bf16[32,4096]{1,0:T(8,128)(2,1)S(1)}, bf16[32,4096]{1,0:T(8,128)(2,1)S(1)}, u32[]{:S(2)}, u32[]{:S(2)}) collective-permute-start(bf16[32,4096]{1,0:T(8,128)(2,1)S(1)} %get-tuple-element.99.b3), channel_id=1, source_target_pairs={{0,1},{1,0},{2,3},{3,2},{4,5},{5,4},{6,7},{7,6},{8,9},{9,8},{10,11... | collective-permute-start | bytes 786440 | tf_op jit(solution)/shard_map/ppermute | solution.py:22
  65.9 3.2 %collective-permute-start.17 = (bf16[32,4096]{1,0:T(8,128)(2,1)S(1)}, bf16[32,4096]{1,0:T(8,128)(2,1)S(1)}, u32[]{:S(2)}, u32[]{:S(2)}) collective-permute-start(bf16[32,4096]{1,0:T(8,128)(2,1)S(1)} %get-tuple-element.99.b3), channel_id=1, source_target_pairs={{0,6},{1,7},{2,0},{3,1},{4,2},{5,3},{6,4},{7,5},{8,14},{9,15},{10,... | collective-permute-start | bytes 786440 | tf_op jit(solution)/shard_map/ppermute | solution.py:18
  69.1 3.7 %collective-permute-done.19.b2 = bf16[32,4096]{1,0:T(8,128)(2,1)S(1)} collective-permute-done((bf16[32,4096]{1,0:T(8,128)(2,1)S(1)}, bf16[32,4096]{1,0:T(8,128)(2,1)S(1)}, u32[]{:S(2)}, u32[]{:S(2)}) %collective-permute-start.19) | collective-permute-done | bytes 262176 | tf_op jit(solution)/shard_map/ppermute | solution.py:22
  72.8 2.4 %collective-permute-done.18.below.b1 = bf16[32,4096]{1,0:T(8,128)(2,1)S(1)} collective-permute-done((bf16[32,4096]{1,0:T(8,128)(2,1)S(1)}, bf16[32,4096]{1,0:T(8,128)(2,1)S(1)}, u32[]{:S(2)}, u32[]{:S(2)}) %collective-permute-start.18) | collective-permute-done | bytes 262176 | tf_op jit(solution)/shard_map/ppermute | solution.py:18
  78.7 1.6 %collective-permute-start.22 = (bf16[32,2048]{1,0:T(8,128)(2,1)S(1)}, bf16[32,2048]{1,0:T(8,128)(2,1)S(1)}, u32[]{:S(2)}, u32[]{:S(2)}) collective-permute-start(bf16[32,2048]{1,0:T(8,128)(2,1)S(1)} %get-tuple-element.102), channel_id=1, source_target_pairs={{0,6},{1,7},{2,0},{3,1},{4,2},{5,3},{6,4},{7,5},{8,14},{9,15},{10,... | collective-permute-start | bytes 393224 | tf_op jit(solution)/shard_map/ppermute | solution.py:18
  82.8 4.0 %collective-permute-done.22.b2_left = bf16[32,2048]{1,0:T(8,128)(2,1)S(1)} collective-permute-done((bf16[32,2048]{1,0:T(8,128)(2,1)S(1)}, bf16[32,2048]{1,0:T(8,128)(2,1)S(1)}, u32[]{:S(2)}, u32[]{:S(2)}) %collective-permute-start.22) | collective-permute-done | bytes 131104 | tf_op jit(solution)/shard_map/ppermute | solution.py:18
  86.8 2.5 %collective-permute-done.21.b1 = bf16[32,4096]{1,0:T(8,128)(2,1)S(1)} collective-permute-done((bf16[32,4096]{1,0:T(8,128)(2,1)S(1)}, bf16[32,4096]{1,0:T(8,128)(2,1)S(1)}, u32[]{:S(2)}, u32[]{:S(2)}) %collective-permute-start.21) | collective-permute-done | bytes 262176 | tf_op jit(solution)/shard_map/ppermute | solution.py:22
  89.2 2.1 %shard_map.124 = (bf16[64,4096]{1,0:T(8,128)(2,1)S(1)}, bf16[32,4096]{1,0:T(8,128)(2,1)S(1)}, bf16[32,2048]{1,0:T(8,128)(2,1)S(1)}, bf16[32,2048]{1,0:T(8,128)(2...) custom-call(bf16[32,4096]{1,0:T(8,128)(2,1)S(1)} %collective-permute-done.20.b0, ...), custom_call_target="tpu_custom_call" | custom-call | flops 1073741824 | bytes 8388608 | tf_op jit(solution)/shard_map/pallas_call | solution.py:239
  92.2 2.1 %collective-permute-start.26 = (bf16[32,4096]{1,0:T(8,128)(2,1)S(1)}, bf16[32,4096]{1,0:T(8,128)(2,1)S(1)}, u32[]{:S(2)}, u32[]{:S(2)}) collective-permute-start(bf16[32,4096]{1,0:T(8,128)(2,1)S(1)} %get-tuple-element.119), channel_id=1, source_target_pairs={{0,4},{1,5},{2,6},{3,7},{4,0},{5,1},{6,2},{7,3},{8,12},{9,13},{10,... | collective-permute-start | bytes 786440 | tf_op jit(solution)/shard_map/ppermute | solution.py:18
  94.5 3.0 %collective-permute-start.28 = (bf16[32,2048]{1,0:T(8,128)(2,1)S(1)}, bf16[32,2048]{1,0:T(8,128)(2,1)S(1)}, u32[]{:S(2)}, u32[]{:S(2)}) collective-permute-start(bf16[32,2048]{1,0:T(8,128)(2,1)S(1)} %get-tuple-element.121), channel_id=1, source_target_pairs={{0,6},{1,7},{2,0},{3,1},{4,2},{5,3},{6,4},{7,5},{8,14},{9,15},{10,... | collective-permute-start | bytes 393224 | tf_op jit(solution)/shard_map/ppermute | solution.py:18
  97.5 2.4 %shard_map.125 = (bf16[32,4096]{1,0:T(8,128)(2,1)S(1)}, bf16[32,4096]{1,0:T(8,128)(2,1)S(1)}, bf16[32,4096]{1,0:T(8,128)(2,1)S(1)}, f32[32,4096]{1,0:T(8,128)S(1)}, f32[1,1,256,256]{3,2,1,0:T(8,128)}) custom-call(f32[1,1]{1,0:T(1,128)S(6)} %log1p.3.log_keep_ref, bf16[128,256]{1,0:T(8,128)(2,1)S(1)} %get-tuple-element.111.gated, ...), custom_call_target="tpu_custom_call" | custom-call | flops 268435456 | bytes 2097152 | tf_op jit(solution)/shard_map/pallas_call | solution.py:248
  99.9 2.6 %collective-permute-done.27.via_up = bf16[32,2048]{1,0:T(8,128)(2,1)S(1)} collective-permute-done((bf16[32,2048]{1,0:T(8,128)(2,1)S(1)}, bf16[32,2048]{1,0:T(8,128)(2,1)S(1)}, u32[]{:S(2)}, u32[]{:S(2)}) %collective-permute-start.27) | collective-permute-done | bytes 131104 | tf_op jit(solution)/shard_map/ppermute | solution.py:18
  103.3 1.8 %collective-permute-start.29 = (bf16[32,4096]{1,0:T(8,128)(2,1)S(1)}, bf16[32,4096]{1,0:T(8,128)(2,1)S(1)}, u32[]{:S(2)}, u32[]{:S(2)}) collective-permute-start(bf16[32,4096]{1,0:T(8,128)(2,1)S(1)} %get-tuple-element.122), channel_id=1, source_target_pairs={{0,2},{1,3},{2,4},{3,5},{4,6},{5,7},{6,0},{7,1},{8,10},{9,11},{10,... | collective-permute-start | bytes 786440 | tf_op jit(solution)/shard_map/ppermute | solution.py:18
  107.6 3.4 %collective-permute-done.29.got_up = bf16[32,4096]{1,0:T(8,128)(2,1)S(1)} collective-permute-done((bf16[32,4096]{1,0:T(8,128)(2,1)S(1)}, bf16[32,4096]{1,0:T(8,128)(2,1)S(1)}, u32[]{:S(2)}, u32[]{:S(2)}) %collective-permute-start.29) | collective-permute-done | bytes 262176 | tf_op jit(solution)/shard_map/ppermute | solution.py:18
  (58 shorter events, 28.4 us)
Async XLA Ops:
  2.8 10.1 %collective-permute-start.2 = (bf16[32,4096]{1,0:T(8,128)(2,1)}, bf16[32,4096]{1,0:T(8,128)(2,1)S(1)}, u32[]{:S(2)}, u32[]{:S(2)}) collective-permute-start(bf16[32,4096]{1,0:T(8,128)(2,1)} %get-tuple-element.64.b3), channel_id=1, source_target_pairs={{0,1},{1,0},{2,3},{3,2},{4,5},{5,4},{6,7},{7,6},{8,9},{9,8},{10,11... | collective-permute-start | bytes 786440 | tf_op jit(solution)/shard_map/ppermute | solution.py:22
  4.8 9.2 %collective-permute-start.1 = (bf16[32,4096]{1,0:T(8,128)(2,1)}, bf16[32,4096]{1,0:T(8,128)(2,1)S(1)}, u32[]{:S(2)}, u32[]{:S(2)}) collective-permute-start(bf16[32,4096]{1,0:T(8,128)(2,1)} %get-tuple-element.64.b3), channel_id=1, source_target_pairs={{0,2},{1,3},{2,4},{3,5},{4,6},{5,7},{6,0},{7,1},{8,10},{9,11},{10,... | collective-permute-start | bytes 786440 | tf_op jit(solution)/shard_map/ppermute | solution.py:18
  6.3 7.7 %collective-permute-start = (bf16[32,4096]{1,0:T(8,128)(2,1)}, bf16[32,4096]{1,0:T(8,128)(2,1)S(1)}, u32[]{:S(2)}, u32[]{:S(2)}) collective-permute-start(bf16[32,4096]{1,0:T(8,128)(2,1)} %get-tuple-element.64.b3), channel_id=1, source_target_pairs={{0,6},{1,7},{2,0},{3,1},{4,2},{5,3},{6,4},{7,5},{8,14},{9,15},{10,... | collective-permute-start | bytes 786440 | tf_op jit(solution)/shard_map/ppermute | solution.py:18
  14.0 12.5 %collective-permute-start.7 = (bf16[32,4096]{1,0:T(8,128)(2,1)S(1)}, bf16[32,4096]{1,0:T(8,128)(2,1)S(1)}, u32[]{:S(2)}, u32[]{:S(2)}) collective-permute-start(bf16[32,4096]{1,0:T(8,128)(2,1)S(1)} %collective-permute-done.2.b2), channel_id=1, source_target_pairs={{0,4},{1,5},{2,6},{3,7},{4,0},{5,1},{6,2},{7,3},{8,12},{9,13},{10,... | collective-permute-start | bytes 786440 | tf_op jit(solution)/shard_map/ppermute | solution.py:18
  16.7 9.7 %collective-permute-start.3 = (bf16[32,4096]{1,0:T(8,128)(2,1)S(1)}, bf16[32,4096]{1,0:T(8,128)(2,1)S(1)}, u32[]{:S(2)}, u32[]{:S(2)}) collective-permute-start(bf16[32,4096]{1,0:T(8,128)(2,1)S(1)} %collective-permute-done.above.b0), channel_id=1, source_target_pairs={{0,1},{1,0},{2,3},{3,2},{4,5},{5,4},{6,7},{7,6},{8,9},{9,8},{10,11... | collective-permute-start | bytes 786440 | tf_op jit(solution)/shard_map/ppermute | solution.py:22
  17.1 11.5 %collective-permute-start.4 = (bf16[32,4096]{1,0:T(8,128)(2,1)S(1)}, bf16[32,4096]{1,0:T(8,128)(2,1)S(1)}, u32[]{:S(2)}, u32[]{:S(2)}) collective-permute-start(bf16[32,4096]{1,0:T(8,128)(2,1)S(1)} %collective-permute-done.1.below.b1), channel_id=1, source_target_pairs={{0,1},{1,0},{2,3},{3,2},{4,5},{5,4},{6,7},{7,6},{8,9},{9,8},{10,11... | collective-permute-start | bytes 786440 | tf_op jit(solution)/shard_map/ppermute | solution.py:22
  18.8 6.4 %collective-permute-start.5 = (bf16[32,2048]{1,0:T(8,128)(2,1)S(1)}, bf16[32,2048]{1,0:T(8,128)(2,1)S(1)}, u32[]{:S(2)}, u32[]{:S(2)}) collective-permute-start(bf16[32,2048]{1,0:T(8,128)(2,1)S(1)} %get-tuple-element.68), channel_id=1, source_target_pairs={{0,6},{1,7},{2,0},{3,1},{4,2},{5,3},{6,4},{7,5},{8,14},{9,15},{10,... | collective-permute-start | bytes 393224 | tf_op jit(solution)/shard_map/ppermute | solution.py:18
  20.3 6.2 %collective-permute-start.6 = (bf16[32,2048]{1,0:T(8,128)(2,1)S(1)}, bf16[32,2048]{1,0:T(8,128)(2,1)S(1)}, u32[]{:S(2)}, u32[]{:S(2)}) collective-permute-start(bf16[32,2048]{1,0:T(8,128)(2,1)S(1)} %get-tuple-element.69), channel_id=1, source_target_pairs={{0,2},{1,3},{2,4},{3,5},{4,6},{5,7},{6,0},{7,1},{8,10},{9,11},{10,... | collective-permute-start | bytes 393224 | tf_op jit(solution)/shard_map/ppermute | solution.py:18
  30.7 11.1 %collective-permute-start.8 = (bf16[64,4096]{1,0:T(8,128)(2,1)S(1)}, bf16[64,4096]{1,0:T(8,128)(2,1)S(1)}, u32[]{:S(2)}, u32[]{:S(2)}) collective-permute-start(bf16[64,4096]{1,0:T(8,128)(2,1)S(1)} %get-tuple-element.91), channel_id=1, source_target_pairs={{0,1},{1,0},{2,3},{3,2},{4,5},{5,4},{6,7},{7,6},{8,9},{9,8},{10,11... | collective-permute-start | bytes 1572872 | tf_op jit(solution)/shard_map/ppermute | solution.py:22
  31.5 9.7 %collective-permute-start.9 = (bf16[32,4096]{1,0:T(8,128)(2,1)S(1)}, bf16[32,4096]{1,0:T(8,128)(2,1)S(1)}, u32[]{:S(2)}, u32[]{:S(2)}) collective-permute-start(bf16[32,4096]{1,0:T(8,128)(2,1)S(1)} %get-tuple-element.92), channel_id=1, source_target_pairs={{0,4},{1,5},{2,6},{3,7},{4,0},{5,1},{6,2},{7,3},{8,12},{9,13},{10,... | collective-permute-start | bytes 786440 | tf_op jit(solution)/shard_map/ppermute | solution.py:18
  32.6 8.6 %collective-permute-start.10 = (bf16[32,2048]{1,0:T(8,128)(2,1)S(1)}, bf16[32,2048]{1,0:T(8,128)(2,1)S(1)}, u32[]{:S(2)}, u32[]{:S(2)}) collective-permute-start(bf16[32,2048]{1,0:T(8,128)(2,1)S(1)} %get-tuple-element.93), channel_id=1, source_target_pairs={{0,2},{1,3},{2,4},{3,5},{4,6},{5,7},{6,0},{7,1},{8,10},{9,11},{10,... | collective-permute-start | bytes 393224 | tf_op jit(solution)/shard_map/ppermute | solution.py:18
  33.7 7.4 %collective-permute-start.11 = (bf16[32,2048]{1,0:T(8,128)(2,1)S(1)}, bf16[32,2048]{1,0:T(8,128)(2,1)S(1)}, u32[]{:S(2)}, u32[]{:S(2)}) collective-permute-start(bf16[32,2048]{1,0:T(8,128)(2,1)S(1)} %get-tuple-element.94), channel_id=1, source_target_pairs={{0,6},{1,7},{2,0},{3,1},{4,2},{5,3},{6,4},{7,5},{8,14},{9,15},{10,... | collective-permute-start | bytes 393224 | tf_op jit(solution)/shard_map/ppermute | solution.py:18
  42.0 7.7 %collective-permute-start.12 = (bf16[32,4096]{1,0:T(8,128)(2,1)S(1)}, bf16[32,4096]{1,0:T(8,128)(2,1)S(1)}, u32[]{:S(2)}, u32[]{:S(2)}) collective-permute-start(bf16[32,4096]{1,0:T(8,128)(2,1)S(1)} %get-tuple-element.95), channel_id=1, source_target_pairs={{0,2},{1,3},{2,4},{3,5},{4,6},{5,7},{6,0},{7,1},{8,10},{9,11},{10,... | collective-permute-start | bytes 786440 | tf_op jit(solution)/shard_map/ppermute | solution.py:18
  43.2 6.5 %collective-permute-start.13 = (bf16[32,4096]{1,0:T(8,128)(2,1)S(1)}, bf16[32,4096]{1,0:T(8,128)(2,1)S(1)}, u32[]{:S(2)}, u32[]{:S(2)}) collective-permute-start(bf16[32,4096]{1,0:T(8,128)(2,1)S(1)} %get-tuple-element.96), channel_id=1, source_target_pairs={{0,6},{1,7},{2,0},{3,1},{4,2},{5,3},{6,4},{7,5},{8,14},{9,15},{10,... | collective-permute-start | bytes 786440 | tf_op jit(solution)/shard_map/ppermute | solution.py:18
  45.3 6.4 %collective-permute-start.14 = (bf16[32,4096]{1,0:T(8,128)(2,1)S(1)}, bf16[32,4096]{1,0:T(8,128)(2,1)S(1)}, u32[]{:S(2)}, u32[]{:S(2)}) collective-permute-start(bf16[32,4096]{1,0:T(8,128)(2,1)S(1)} %get-tuple-element.97), channel_id=1, source_target_pairs={{0,1},{1,0},{2,3},{3,2},{4,5},{5,4},{6,7},{7,6},{8,9},{9,8},{10,11... | collective-permute-start | bytes 786440 | tf_op jit(solution)/shard_map/ppermute | solution.py:22
  51.9 8.7 %collective-permute-start.15 = (bf16[32,4096]{1,0:T(8,128)(2,1)S(1)}, bf16[32,4096]{1,0:T(8,128)(2,1)S(1)}, u32[]{:S(2)}, u32[]{:S(2)}) collective-permute-start(bf16[32,4096]{1,0:T(8,128)(2,1)S(1)} %shard_map.120), channel_id=1, source_target_pairs={{0,8},{8,16},{16,24},{24,32},{32,40},{40,48},{48,56},{56,64},{64,7... | collective-permute-start | bytes 786440 | tf_op jit(solution)/shard_map/ppermute | solution.py:26
  60.6 3.2 %collective-permute-start.16 = (bf16[16,128]{1,0:T(8,128)(2,1)S(1)}, bf16[16,128]{1,0:T(8,128)(2,1)S(1)}, u32[]{:S(2)}, u32[]{:S(2)}) collective-permute-start(bf16[16,128]{1,0:T(8,128)(2,1)S(1)} %slice.4), channel_id=1, source_target_pairs={{0,8},{8,0},{16,24},{24,16},{32,40},{40,32},{48,56},{56,48},{64,72... | collective-permute-start | bytes 12296 | tf_op jit(solution)/shard_map/ppermute | solution.py:31
  64.2 8.6 %collective-permute-start.19 = (bf16[32,4096]{1,0:T(8,128)(2,1)S(1)}, bf16[32,4096]{1,0:T(8,128)(2,1)S(1)}, u32[]{:S(2)}, u32[]{:S(2)}) collective-permute-start(bf16[32,4096]{1,0:T(8,128)(2,1)S(1)} %get-tuple-element.99.b3), channel_id=1, source_target_pairs={{0,1},{1,0},{2,3},{3,2},{4,5},{5,4},{6,7},{7,6},{8,9},{9,8},{10,11... | collective-permute-start | bytes 786440 | tf_op jit(solution)/shard_map/ppermute | solution.py:22
  65.9 9.3 %collective-permute-start.18 = (bf16[32,4096]{1,0:T(8,128)(2,1)S(1)}, bf16[32,4096]{1,0:T(8,128)(2,1)S(1)}, u32[]{:S(2)}, u32[]{:S(2)}) collective-permute-start(bf16[32,4096]{1,0:T(8,128)(2,1)S(1)} %get-tuple-element.99.b3), channel_id=1, source_target_pairs={{0,2},{1,3},{2,4},{3,5},{4,6},{5,7},{6,0},{7,1},{8,10},{9,11},{10,... | collective-permute-start | bytes 786440 | tf_op jit(solution)/shard_map/ppermute | solution.py:18
  65.9 9.3 %collective-permute-start.17 = (bf16[32,4096]{1,0:T(8,128)(2,1)S(1)}, bf16[32,4096]{1,0:T(8,128)(2,1)S(1)}, u32[]{:S(2)}, u32[]{:S(2)}) collective-permute-start(bf16[32,4096]{1,0:T(8,128)(2,1)S(1)} %get-tuple-element.99.b3), channel_id=1, source_target_pairs={{0,6},{1,7},{2,0},{3,1},{4,2},{5,3},{6,4},{7,5},{8,14},{9,15},{10,... | collective-permute-start | bytes 786440 | tf_op jit(solution)/shard_map/ppermute | solution.py:18
  75.2 11.6 %collective-permute-start.24 = (bf16[32,4096]{1,0:T(8,128)(2,1)S(1)}, bf16[32,4096]{1,0:T(8,128)(2,1)S(1)}, u32[]{:S(2)}, u32[]{:S(2)}) collective-permute-start(bf16[32,4096]{1,0:T(8,128)(2,1)S(1)} %collective-permute-done.19.b2), channel_id=1, source_target_pairs={{0,4},{1,5},{2,6},{3,7},{4,0},{5,1},{6,2},{7,3},{8,12},{9,13},{10,... | collective-permute-start | bytes 786440 | tf_op jit(solution)/shard_map/ppermute | solution.py:18
  76.7 10.1 %collective-permute-start.20 = (bf16[32,4096]{1,0:T(8,128)(2,1)S(1)}, bf16[32,4096]{1,0:T(8,128)(2,1)S(1)}, u32[]{:S(2)}, u32[]{:S(2)}) collective-permute-start(bf16[32,4096]{1,0:T(8,128)(2,1)S(1)} %collective-permute-done.17.above.b0), channel_id=1, source_target_pairs={{0,1},{1,0},{2,3},{3,2},{4,5},{5,4},{6,7},{7,6},{8,9},{9,8},{10,11... | collective-permute-start | bytes 786440 | tf_op jit(solution)/shard_map/ppermute | solution.py:22
  77.2 12.0 %collective-permute-start.21 = (bf16[32,4096]{1,0:T(8,128)(2,1)S(1)}, bf16[32,4096]{1,0:T(8,128)(2,1)S(1)}, u32[]{:S(2)}, u32[]{:S(2)}) collective-permute-start(bf16[32,4096]{1,0:T(8,128)(2,1)S(1)} %collective-permute-done.18.below.b1), channel_id=1, source_target_pairs={{0,1},{1,0},{2,3},{3,2},{4,5},{5,4},{6,7},{7,6},{8,9},{9,8},{10,11... | collective-permute-start | bytes 786440 | tf_op jit(solution)/shard_map/ppermute | solution.py:22
  78.7 8.0 %collective-permute-start.22 = (bf16[32,2048]{1,0:T(8,128)(2,1)S(1)}, bf16[32,2048]{1,0:T(8,128)(2,1)S(1)}, u32[]{:S(2)}, u32[]{:S(2)}) collective-permute-start(bf16[32,2048]{1,0:T(8,128)(2,1)S(1)} %get-tuple-element.102), channel_id=1, source_target_pairs={{0,6},{1,7},{2,0},{3,1},{4,2},{5,3},{6,4},{7,5},{8,14},{9,15},{10,... | collective-permute-start | bytes 393224 | tf_op jit(solution)/shard_map/ppermute | solution.py:18
  80.3 6.5 %collective-permute-start.23 = (bf16[32,2048]{1,0:T(8,128)(2,1)S(1)}, bf16[32,2048]{1,0:T(8,128)(2,1)S(1)}, u32[]{:S(2)}, u32[]{:S(2)}) collective-permute-start(bf16[32,2048]{1,0:T(8,128)(2,1)S(1)} %get-tuple-element.103), channel_id=1, source_target_pairs={{0,2},{1,3},{2,4},{3,5},{4,6},{5,7},{6,0},{7,1},{8,10},{9,11},{10,... | collective-permute-start | bytes 393224 | tf_op jit(solution)/shard_map/ppermute | solution.py:18
  91.3 11.7 %collective-permute-start.25 = (bf16[64,4096]{1,0:T(8,128)(2,1)S(1)}, bf16[64,4096]{1,0:T(8,128)(2,1)S(1)}, u32[]{:S(2)}, u32[]{:S(2)}) collective-permute-start(bf16[64,4096]{1,0:T(8,128)(2,1)S(1)} %get-tuple-element.118), channel_id=1, source_target_pairs={{0,1},{1,0},{2,3},{3,2},{4,5},{5,4},{6,7},{7,6},{8,9},{9,8},{10,11... | collective-permute-start | bytes 1572872 | tf_op jit(solution)/shard_map/ppermute | solution.py:22
  92.2 10.3 %collective-permute-start.26 = (bf16[32,4096]{1,0:T(8,128)(2,1)S(1)}, bf16[32,4096]{1,0:T(8,128)(2,1)S(1)}, u32[]{:S(2)}, u32[]{:S(2)}) collective-permute-start(bf16[32,4096]{1,0:T(8,128)(2,1)S(1)} %get-tuple-element.119), channel_id=1, source_target_pairs={{0,4},{1,5},{2,6},{3,7},{4,0},{5,1},{6,2},{7,3},{8,12},{9,13},{10,... | collective-permute-start | bytes 786440 | tf_op jit(solution)/shard_map/ppermute | solution.py:18
  94.3 8.2 %collective-permute-start.27 = (bf16[32,2048]{1,0:T(8,128)(2,1)S(1)}, bf16[32,2048]{1,0:T(8,128)(2,1)S(1)}, u32[]{:S(2)}, u32[]{:S(2)}) collective-permute-start(bf16[32,2048]{1,0:T(8,128)(2,1)S(1)} %get-tuple-element.120), channel_id=1, source_target_pairs={{0,2},{1,3},{2,4},{3,5},{4,6},{5,7},{6,0},{7,1},{8,10},{9,11},{10,... | collective-permute-start | bytes 393224 | tf_op jit(solution)/shard_map/ppermute | solution.py:18
  94.5 8.0 %collective-permute-start.28 = (bf16[32,2048]{1,0:T(8,128)(2,1)S(1)}, bf16[32,2048]{1,0:T(8,128)(2,1)S(1)}, u32[]{:S(2)}, u32[]{:S(2)}) collective-permute-start(bf16[32,2048]{1,0:T(8,128)(2,1)S(1)} %get-tuple-element.121), channel_id=1, source_target_pairs={{0,6},{1,7},{2,0},{3,1},{4,2},{5,3},{6,4},{7,5},{8,14},{9,15},{10,... | collective-permute-start | bytes 393224 | tf_op jit(solution)/shard_map/ppermute | solution.py:18
  103.3 7.7 %collective-permute-start.29 = (bf16[32,4096]{1,0:T(8,128)(2,1)S(1)}, bf16[32,4096]{1,0:T(8,128)(2,1)S(1)}, u32[]{:S(2)}, u32[]{:S(2)}) collective-permute-start(bf16[32,4096]{1,0:T(8,128)(2,1)S(1)} %get-tuple-element.122), channel_id=1, source_target_pairs={{0,2},{1,3},{2,4},{3,5},{4,6},{5,7},{6,0},{7,1},{8,10},{9,11},{10,... | collective-permute-start | bytes 786440 | tf_op jit(solution)/shard_map/ppermute | solution.py:18
  105.1 6.4 %collective-permute-start.30 = (bf16[32,4096]{1,0:T(8,128)(2,1)S(1)}, bf16[32,4096]{1,0:T(8,128)(2,1)S(1)}, u32[]{:S(2)}, u32[]{:S(2)}) collective-permute-start(bf16[32,4096]{1,0:T(8,128)(2,1)S(1)} %get-tuple-element.123), channel_id=1, source_target_pairs={{0,6},{1,7},{2,0},{3,1},{4,2},{5,3},{6,4},{7,5},{8,14},{9,15},{10,... | collective-permute-start | bytes 786440 | tf_op jit(solution)/shard_map/ppermute | solution.py:18
  106.6 6.4 %collective-permute-start.31 = (bf16[32,4096]{1,0:T(8,128)(2,1)S(1)}, bf16[32,4096]{1,0:T(8,128)(2,1)S(1)}, u32[]{:S(2)}, u32[]{:S(2)}) collective-permute-start(bf16[32,4096]{1,0:T(8,128)(2,1)S(1)} %get-tuple-element.124), channel_id=1, source_target_pairs={{0,1},{1,0},{2,3},{3,2},{4,5},{5,4},{6,7},{7,6},{8,9},{9,8},{10,11... | collective-permute-start | bytes 786440 | tf_op jit(solution)/shard_map/ppermute | solution.py:22
  (5 other events, 88.4 us)

commit v5 on v4

--- a/solution.py
+++ b/solution.py
@@ -64,7 +64,7 @@
     copies[2].wait()
 
 
-def second_norm_kernel(arrived_ref, in_step_ref, fresh_ref, gain_ref, rows_ref, out_ref):
+def second_norm_kernel(arrived_ref, fresh_ref, gain_ref, rows_ref, out_ref):
     rows = jnp.where(lax.axis_index("section") == 0, fresh_ref[...], arrived_ref[...].astype(jnp.float32))
     rows_ref[0] = rows
     out_ref[...] = normed(rows, gain_ref[...])
@@ -100,8 +100,10 @@
         copy.wait()
 
 
-def halves_kernel(above, below, left, right):
-    width = left.shape[1]
+def halves_kernel(above, below, both, left, right):
+    count, width = left.shape
+    both[:count] = above[...]
+    both[count:] = below[...]
     left[...] = above[:, :width]
     right[...] = below[:, width:]
 
@@ -136,11 +138,11 @@
 
 
 def late_kernel(
-    b0, b1, b2_left, b2_right, b3, wq, wk, wv, wg, early_q, early_k, early_v, early_g, state, decay, lead, w_out,
+    both, b2_left, b2_right, b3, wq, wk, wv, wg, early_q, early_k, early_v, early_g, state, decay, lead, w_out,
     over_z, over_x, half_up, half_down, gated_late, keys, values,
 ):
     b2 = jnp.concatenate([b2_left[...], b2_right[...]], axis=1)
-    late = project((b0, b1, b2, b3), (wq, wk, wv, wg))
+    late = project((both, b2, b3), (wq, wk, wv, wg))
     q, k, v, gate = (
         jnp.concatenate([a, b[...]], axis=0) for a, b in zip(late, (early_q, early_k, early_v, early_g))
     )
@@ -226,10 +228,10 @@
                 limit=42 * MIB,
                     )(log_keep, w_query, w_key, w_value, w_gate, w_out)
         above, below, mate, decay = lax.optimization_barrier((above, below, mate, decay))
-        mate_above, mate_below = swap_z(above), swap_z(below)
-        far_mate = shift_x(mate, 2)
-        left, right = call(halves_kernel, [half_block] * 2, [VMEM] * 2, moved=4 * count * width)(above, below)
-        far = (shift_x(left, -1), shift_x(right, 1))
+        both, left, right = call(
+            halves_kernel, [double, half_block, half_block], [VMEM] * 2, moved=12 * count * width
+        )(above, below)
+        late = (swap_z(both), shift_x(left, -1), shift_x(right, 1), shift_x(mate, 2))
         early = call(
             early_kernel,
             [shape((half, key_size), bf16)] * 2 + [shape((half, value_size), bf16), shape((half, value_size), f32)],
@@ -240,9 +242,9 @@
             late_kernel,
             [double, block, half_block, half_block]
             + [shape((half, value_size), bf16), shape((group, key_size), bf16), shape((group, value_size), bf16)],
-            [VMEM] * 17,
+            [VMEM] * 16,
             **heavy,
-        )(mate_above, mate_below, *far, far_mate, *weights, *early, state, decay, lead, out_weight)
+        )(*late, *weights, *early, state, decay, lead, out_weight)
         via_z, via_x = swap_z(over_z), shift_x(over_x, 2)
         via_up, via_down = shift_x(half_up, 1), shift_x(half_down, -1)
         up, down, to_mate, mine, state = call(
@@ -261,8 +263,8 @@
             result = call(sum_kernel, block, [VMEM] * 5, moved=16 * count * width)(*parts)
             arrived = next_section(result)
             rows, own = call(
-                second_norm_kernel, [shape(inflow.shape, f32), block], [VMEM] * 4, moved=12 * count * width
-            )(arrived, other_core(arrived), fresh, norm_gain)
+                second_norm_kernel, [shape(inflow.shape, f32), block], [VMEM] * 3, moved=12 * count * width
+            )(arrived, fresh, norm_gain)
         else:
             rows = call(sum_kernel, shape(inflow.shape, f32), [VMEM] * 5, moved=16 * count * width)(*parts)
     return (rows, state)

time: 116 us -> 115 us (level)
  starting transfers between devices: 47.3 us -> 44 us
  waiting for transfers between devices: 45.9 us -> 48.4 us
    ppermute x20, waiting for transfers between devices: 25.3 us -> 33.3 us  [shift_x(): lax.ppermute(value, 'tensor', [(t, (t + 2 * steps) % 8) for t in range(8)])]
    ppermute x10 -> x8, waiting for transfers between devices: 13.1 us -> 8.35 us  [swap_z(): return lax.ppermute(value, 'tensor', [(t, t ^ 1) for t in range(8)])]
    ppermute x1 -> x0, starting transfers between devices: 2.4 us -> none  [other_core(): lax.ppermute(value[:16, :128], 'section', [(s, s ^ 1) for s in range(coun...]
    ppermute x10 -> x8, starting transfers between devices: 11.2 us -> 10.3 us  [swap_z(): return lax.ppermute(value, 'tensor', [(t, t ^ 1) for t in range(8)])]
  transfers between devices with their start and end apart: 32 -> 29, of which waited for: 19 -> 18; matrix products, arithmetic and copies ran while one was open for 0% -> 0% of each run, Pallas kernels for 10% -> 10%
where the time goes in v5:
time: 115 us; the launch traced here: 113 us
  waiting for transfers between devices  48.4 us (42%)
  starting transfers between devices  44 us (38%)
  Pallas kernels  19.2 us (17%)
  between operations  1.47 us (1%)
    ppermute x20, waiting for transfers between devices, shift_x(): lax.ppermute(value, 'tensor', [(t, (t + 2 * steps) % 8) for t in range(8)])  33.3 us
    ppermute x20, starting transfers between devices, shift_x(): lax.ppermute(value, 'tensor', [(t, (t + 2 * steps) % 8) for t in range(8)])  31.8 us
    ppermute x8, starting transfers between devices, swap_z(): return lax.ppermute(value, 'tensor', [(t, t ^ 1) for t in range(8)])  10.3 us
    ppermute x8, waiting for transfers between devices, swap_z(): return lax.ppermute(value, 'tensor', [(t, t ^ 1) for t in range(8)])  8.35 us
    ppermute x1, waiting for transfers between devices, next_section(): lax.ppermute(value, 'section', [(s, s + 1) for s in range(lax.axis_size('...  6.76 us
    pallas_call x2, Pallas kernels, body(): call(late_kernel, [double, block, half_block, half_block] + [shape((half,...  4.2 us
    pallas_call x1, Pallas kernels, body(): call(setup_kernel, [shape(a.shape, a.dtype) for a in (w_query, w_key, w_v...  4.14 us
    pallas_call x2, Pallas kernels, body(): call(out_kernel, [block] * 3 + [shape((count, width), f32), shape(state.s...  4.1 us
  transfers between devices with their start and end apart: 29, of which 18 were waited for; matrix products, arithmetic and copies ran while one was open for 0% of the time, Pallas kernels for 10%

profile of v5, /device:TPU:88, one launch (start us, length us, event | category | flops | bytes accessed | tf_op | source)
XLA Modules:
  0.0 113.1 jit_solution(17251101038823126267)
XLA Ops:
  0.6 2.2 %shard_map.113 = (bf16[32,4096]{1,0:T(8,128)(2,1)}, f32[1,1,256,256]{3,2,1,0:T(8,128)}) custom-call(f32[1,32,4096]{2,1,0:T(8,128)} %rows.1, f32[1,4096]{1,0:T(1,128)} %gain_ref.1, f32[1,1,256,256]{3,2,1,0:T(8,128)} %state_hbm.1), custom_call_target="tpu_custom_call" | custom-call | bytes 786432 | tf_op jit(solution)/shard_map/pallas_call | solution.py:209
  2.8 2.0 %collective-permute-start.2 = (bf16[32,4096]{1,0:T(8,128)(2,1)}, bf16[32,4096]{1,0:T(8,128)(2,1)S(1)}, u32[]{:S(2)}, u32[]{:S(2)}) collective-permute-start(bf16[32,4096]{1,0:T(8,128)(2,1)} %get-tuple-element.66.b3), channel_id=1, source_target_pairs={{0,1},{1,0},{2,3},{3,2},{4,5},{5,4},{6,7},{7,6},{8,9},{9,8},{10,11... | collective-permute-start | bytes 786440 | tf_op jit(solution)/shard_map/ppermute | solution.py:22
  4.8 1.5 %collective-permute-start.1 = (bf16[32,4096]{1,0:T(8,128)(2,1)}, bf16[32,4096]{1,0:T(8,128)(2,1)S(1)}, u32[]{:S(2)}, u32[]{:S(2)}) collective-permute-start(bf16[32,4096]{1,0:T(8,128)(2,1)} %get-tuple-element.66.b3), channel_id=1, source_target_pairs={{0,2},{1,3},{2,4},{3,5},{4,6},{5,7},{6,0},{7,1},{8,10},{9,11},{10,... | collective-permute-start | bytes 786440 | tf_op jit(solution)/shard_map/ppermute | solution.py:18
  6.3 1.7 %collective-permute-start = (bf16[32,4096]{1,0:T(8,128)(2,1)}, bf16[32,4096]{1,0:T(8,128)(2,1)S(1)}, u32[]{:S(2)}, u32[]{:S(2)}) collective-permute-start(bf16[32,4096]{1,0:T(8,128)(2,1)} %get-tuple-element.66.b3), channel_id=1, source_target_pairs={{0,6},{1,7},{2,0},{3,1},{4,2},{5,3},{6,4},{7,5},{8,14},{9,15},{10,... | collective-permute-start | bytes 786440 | tf_op jit(solution)/shard_map/ppermute | solution.py:18
  8.7 4.1 %shard_map.114 = (bf16[1,4096,256]{2,1,0:T(8,128)(2,1)S(1)}, bf16[1,4096,256]{2,1,0:T(8,128)(2,1)S(1)}, bf16[1,4096,256]{2,1,0:T(8,128)(2,1)S(1)}, bf16[1,4096,2...) custom-call(f32[1,1]{1,0:T(1,128)S(6)} %log1p.3.log_keep_ref, ...), custom_call_target="tpu_custom_call" | custom-call | bytes 10485760 | tf_op jit(solution)/shard_map/pallas_call | solution.py:221
  14.5 2.7 %collective-permute-start.6 = (bf16[32,4096]{1,0:T(8,128)(2,1)S(1)}, bf16[32,4096]{1,0:T(8,128)(2,1)S(1)}, u32[]{:S(2)}, u32[]{:S(2)}) collective-permute-start(bf16[32,4096]{1,0:T(8,128)(2,1)S(1)} %collective-permute-done.2.b2), channel_id=1, source_target_pairs={{0,4},{1,5},{2,6},{3,7},{4,0},{5,1},{6,2},{7,3},{8,12},{9,13},{10,... | collective-permute-start | bytes 786440 | tf_op jit(solution)/shard_map/ppermute | solution.py:18
  17.2 1.4 %collective-permute-start.4 = (bf16[32,2048]{1,0:T(8,128)(2,1)S(1)}, bf16[32,2048]{1,0:T(8,128)(2,1)S(1)}, u32[]{:S(2)}, u32[]{:S(2)}) collective-permute-start(bf16[32,2048]{1,0:T(8,128)(2,1)S(1)} %get-tuple-element.71), channel_id=1, source_target_pairs={{0,6},{1,7},{2,0},{3,1},{4,2},{5,3},{6,4},{7,5},{8,14},{9,15},{10,... | collective-permute-start | bytes 393224 | tf_op jit(solution)/shard_map/ppermute | solution.py:18
  20.6 5.1 %collective-permute-done.4.b2_left = bf16[32,2048]{1,0:T(8,128)(2,1)S(1)} collective-permute-done((bf16[32,2048]{1,0:T(8,128)(2,1)S(1)}, bf16[32,2048]{1,0:T(8,128)(2,1)S(1)}, u32[]{:S(2)}, u32[]{:S(2)}) %collective-permute-start.4) | collective-permute-done | bytes 131104 | tf_op jit(solution)/shard_map/ppermute | solution.py:18
  26.6 2.1 %shard_map.117 = (bf16[64,4096]{1,0:T(8,128)(2,1)S(1)}, bf16[32,4096]{1,0:T(8,128)(2,1)S(1)}, bf16[32,2048]{1,0:T(8,128)(2,1)S(1)}, bf16[32,2048]{1,0:T(8,128)(2...) custom-call(bf16[64,4096]{1,0:T(8,128)(2,1)S(1)} %collective-permute-done.3.both, ...), custom_call_target="tpu_custom_call" | custom-call | flops 1073741824 | bytes 8388608 | tf_op jit(solution)/shard_map/pallas_call | solution.py:241
  29.5 2.4 %collective-permute-start.8 = (bf16[32,4096]{1,0:T(8,128)(2,1)S(1)}, bf16[32,4096]{1,0:T(8,128)(2,1)S(1)}, u32[]{:S(2)}, u32[]{:S(2)}) collective-permute-start(bf16[32,4096]{1,0:T(8,128)(2,1)S(1)} %get-tuple-element.95), channel_id=1, source_target_pairs={{0,4},{1,5},{2,6},{3,7},{4,0},{5,1},{6,2},{7,3},{8,12},{9,13},{10,... | collective-permute-start | bytes 786440 | tf_op jit(solution)/shard_map/ppermute | solution.py:18
  33.0 2.2 %collective-permute-start.10 = (bf16[32,2048]{1,0:T(8,128)(2,1)S(1)}, bf16[32,2048]{1,0:T(8,128)(2,1)S(1)}, u32[]{:S(2)}, u32[]{:S(2)}) collective-permute-start(bf16[32,2048]{1,0:T(8,128)(2,1)S(1)} %get-tuple-element.97), channel_id=1, source_target_pairs={{0,6},{1,7},{2,0},{3,1},{4,2},{5,3},{6,4},{7,5},{8,14},{9,15},{10,... | collective-permute-start | bytes 393224 | tf_op jit(solution)/shard_map/ppermute | solution.py:18
  35.1 1.7 %shard_map.118 = (bf16[32,4096]{1,0:T(8,128)(2,1)S(1)}, bf16[32,4096]{1,0:T(8,128)(2,1)S(1)}, bf16[32,4096]{1,0:T(8,128)(2,1)S(1)}, f32[32,4096]{1,0:T(8,128)S(1)}, f32[1,1,256,256]{3,2,1,0:T(8,128)S(1)}) custom-call(f32[1,1]{1,0:T(1,128)S(6)} %log1p.3.log_keep_ref, bf16[128,256]{1,0:T(8,128)(2,1)S(1)} %get-tuple-element.86.gated, ...), custom_call_target="tpu_custom_call" | custom-call | flops 268435456 | bytes 2097152 | tf_op jit(solution)/shard_map/pallas_call | solution.py:250
  36.8 3.0 %collective-permute-done.9.via_up = bf16[32,2048]{1,0:T(8,128)(2,1)S(1)} collective-permute-done((bf16[32,2048]{1,0:T(8,128)(2,1)S(1)}, bf16[32,2048]{1,0:T(8,128)(2,1)S(1)}, u32[]{:S(2)}, u32[]{:S(2)}) %collective-permute-start.9) | collective-permute-done | bytes 131104 | tf_op jit(solution)/shard_map/ppermute | solution.py:18
  41.2 1.8 %collective-permute-start.11 = (bf16[32,4096]{1,0:T(8,128)(2,1)S(1)}, bf16[32,4096]{1,0:T(8,128)(2,1)S(1)}, u32[]{:S(2)}, u32[]{:S(2)}) collective-permute-start(bf16[32,4096]{1,0:T(8,128)(2,1)S(1)} %get-tuple-element.98), channel_id=1, source_target_pairs={{0,2},{1,3},{2,4},{3,5},{4,6},{5,7},{6,0},{7,1},{8,10},{9,11},{10,... | collective-permute-start | bytes 786440 | tf_op jit(solution)/shard_map/ppermute | solution.py:18
  43.1 1.5 %collective-permute-start.12 = (bf16[32,4096]{1,0:T(8,128)(2,1)S(1)}, bf16[32,4096]{1,0:T(8,128)(2,1)S(1)}, u32[]{:S(2)}, u32[]{:S(2)}) collective-permute-start(bf16[32,4096]{1,0:T(8,128)(2,1)S(1)} %get-tuple-element.99), channel_id=1, source_target_pairs={{0,6},{1,7},{2,0},{3,1},{4,2},{5,3},{6,4},{7,5},{8,14},{9,15},{10,... | collective-permute-start | bytes 786440 | tf_op jit(solution)/shard_map/ppermute | solution.py:18
  45.6 4.3 %collective-permute-done.11.got_up = bf16[32,4096]{1,0:T(8,128)(2,1)S(1)} collective-permute-done((bf16[32,4096]{1,0:T(8,128)(2,1)S(1)}, bf16[32,4096]{1,0:T(8,128)(2,1)S(1)}, u32[]{:S(2)}, u32[]{:S(2)}) %collective-permute-start.11) | collective-permute-done | bytes 262176 | tf_op jit(solution)/shard_map/ppermute | solution.py:18
  51.6 1.9 %collective-permute-start.14 = (bf16[32,4096]{1,0:T(8,128)(2,1)S(1)}, bf16[32,4096]{1,0:T(8,128)(2,1)S(1)}, u32[]{:S(2)}, u32[]{:S(2)}) collective-permute-start(bf16[32,4096]{1,0:T(8,128)(2,1)S(1)} %shard_map.120), channel_id=1, source_target_pairs={{0,8},{8,16},{16,24},{24,32},{32,40},{40,48},{48,56},{56,64},{64,7... | collective-permute-start | bytes 786440 | tf_op jit(solution)/shard_map/ppermute | solution.py:26
  53.6 6.8 %collective-permute-done.14.arrived_ref = bf16[32,4096]{1,0:T(8,128)(2,1)S(1)} collective-permute-done((bf16[32,4096]{1,0:T(8,128)(2,1)S(1)}, bf16[32,4096]{1,0:T(8,128)(2,1)S(1)}, u32[]{:S(2)}, u32[]{:S(2)}) %collective-permute-start.14) | collective-permute-done | bytes 262176 | tf_op jit(solution)/shard_map/ppermute | solution.py:26
  60.7 3.5 %collective-permute-start.17 = (bf16[32,4096]{1,0:T(8,128)(2,1)S(1)}, bf16[32,4096]{1,0:T(8,128)(2,1)S(1)}, u32[]{:S(2)}, u32[]{:S(2)}) collective-permute-start(bf16[32,4096]{1,0:T(8,128)(2,1)S(1)} %get-tuple-element.102.b3), channel_id=1, source_target_pairs={{0,1},{1,0},{2,3},{3,2},{4,5},{5,4},{6,7},{7,6},{8,9},{9,8},{10,11... | collective-permute-start | bytes 786440 | tf_op jit(solution)/shard_map/ppermute | solution.py:22
  65.3 2.1 %collective-permute-start.15 = (bf16[32,4096]{1,0:T(8,128)(2,1)S(1)}, bf16[32,4096]{1,0:T(8,128)(2,1)S(1)}, u32[]{:S(2)}, u32[]{:S(2)}) collective-permute-start(bf16[32,4096]{1,0:T(8,128)(2,1)S(1)} %get-tuple-element.102.b3), channel_id=1, source_target_pairs={{0,6},{1,7},{2,0},{3,1},{4,2},{5,3},{6,4},{7,5},{8,14},{9,15},{10,... | collective-permute-start | bytes 786440 | tf_op jit(solution)/shard_map/ppermute | solution.py:18
  67.4 3.5 %collective-permute-done.17.b2 = bf16[32,4096]{1,0:T(8,128)(2,1)S(1)} collective-permute-done((bf16[32,4096]{1,0:T(8,128)(2,1)S(1)}, bf16[32,4096]{1,0:T(8,128)(2,1)S(1)}, u32[]{:S(2)}, u32[]{:S(2)}) %collective-permute-start.17) | collective-permute-done | bytes 262176 | tf_op jit(solution)/shard_map/ppermute | solution.py:22
  70.9 2.7 %collective-permute-done.16.below.b1 = bf16[32,4096]{1,0:T(8,128)(2,1)S(1)} collective-permute-done((bf16[32,4096]{1,0:T(8,128)(2,1)S(1)}, bf16[32,4096]{1,0:T(8,128)(2,1)S(1)}, u32[]{:S(2)}, u32[]{:S(2)}) %collective-permute-start.16) | collective-permute-done | bytes 262176 | tf_op jit(solution)/shard_map/ppermute | solution.py:18
  74.1 1.7 %collective-permute-start.21 = (bf16[32,4096]{1,0:T(8,128)(2,1)S(1)}, bf16[32,4096]{1,0:T(8,128)(2,1)S(1)}, u32[]{:S(2)}, u32[]{:S(2)}) collective-permute-start(bf16[32,4096]{1,0:T(8,128)(2,1)S(1)} %collective-permute-done.17.b2), channel_id=1, source_target_pairs={{0,4},{1,5},{2,6},{3,7},{4,0},{5,1},{6,2},{7,3},{8,12},{9,13},{10,... | collective-permute-start | bytes 786440 | tf_op jit(solution)/shard_map/ppermute | solution.py:18
  75.8 1.4 %collective-permute-start.19 = (bf16[32,2048]{1,0:T(8,128)(2,1)S(1)}, bf16[32,2048]{1,0:T(8,128)(2,1)S(1)}, u32[]{:S(2)}, u32[]{:S(2)}) collective-permute-start(bf16[32,2048]{1,0:T(8,128)(2,1)S(1)} %get-tuple-element.106), channel_id=1, source_target_pairs={{0,6},{1,7},{2,0},{3,1},{4,2},{5,3},{6,4},{7,5},{8,14},{9,15},{10,... | collective-permute-start | bytes 393224 | tf_op jit(solution)/shard_map/ppermute | solution.py:18
  79.3 6.6 %collective-permute-done.19.b2_left = bf16[32,2048]{1,0:T(8,128)(2,1)S(1)} collective-permute-done((bf16[32,2048]{1,0:T(8,128)(2,1)S(1)}, bf16[32,2048]{1,0:T(8,128)(2,1)S(1)}, u32[]{:S(2)}, u32[]{:S(2)}) %collective-permute-start.19) | collective-permute-done | bytes 131104 | tf_op jit(solution)/shard_map/ppermute | solution.py:18
  86.7 2.1 %shard_map.124 = (bf16[64,4096]{1,0:T(8,128)(2,1)S(1)}, bf16[32,4096]{1,0:T(8,128)(2,1)S(1)}, bf16[32,2048]{1,0:T(8,128)(2,1)S(1)}, bf16[32,2048]{1,0:T(8,128)(2...) custom-call(bf16[64,4096]{1,0:T(8,128)(2,1)S(1)} %collective-permute-done.18.both,, ...), custom_call_target="tpu_custom_call" | custom-call | flops 1073741824 | bytes 8388608 | tf_op jit(solution)/shard_map/pallas_call | solution.py:241
  91.1 2.3 %collective-permute-start.24 = (bf16[32,2048]{1,0:T(8,128)(2,1)S(1)}, bf16[32,2048]{1,0:T(8,128)(2,1)S(1)}, u32[]{:S(2)}, u32[]{:S(2)}) collective-permute-start(bf16[32,2048]{1,0:T(8,128)(2,1)S(1)} %get-tuple-element.124), channel_id=1, source_target_pairs={{0,2},{1,3},{2,4},{3,5},{4,6},{5,7},{6,0},{7,1},{8,10},{9,11},{10,... | collective-permute-start | bytes 393224 | tf_op jit(solution)/shard_map/ppermute | solution.py:18
  94.3 2.4 %shard_map.125 = (bf16[32,4096]{1,0:T(8,128)(2,1)S(1)}, bf16[32,4096]{1,0:T(8,128)(2,1)S(1)}, bf16[32,4096]{1,0:T(8,128)(2,1)S(1)}, f32[32,4096]{1,0:T(8,128)S(1)}, f32[1,1,256,256]{3,2,1,0:T(8,128)}) custom-call(f32[1,1]{1,0:T(1,128)S(6)} %log1p.3.log_keep_ref, bf16[128,256]{1,0:T(8,128)(2,1)S(1)} %get-tuple-element.115.gated, ...), custom_call_target="tpu_custom_call" | custom-call | flops 268435456 | bytes 2097152 | tf_op jit(solution)/shard_map/pallas_call | solution.py:250
  96.7 4.2 %collective-permute-done.24.via_up = bf16[32,2048]{1,0:T(8,128)(2,1)S(1)} collective-permute-done((bf16[32,2048]{1,0:T(8,128)(2,1)S(1)}, bf16[32,2048]{1,0:T(8,128)(2,1)S(1)}, u32[]{:S(2)}, u32[]{:S(2)}) %collective-permute-start.24) | collective-permute-done | bytes 131104 | tf_op jit(solution)/shard_map/ppermute | solution.py:18
  102.6 2.6 %collective-permute-start.27 = (bf16[32,4096]{1,0:T(8,128)(2,1)S(1)}, bf16[32,4096]{1,0:T(8,128)(2,1)S(1)}, u32[]{:S(2)}, u32[]{:S(2)}) collective-permute-start(bf16[32,4096]{1,0:T(8,128)(2,1)S(1)} %get-tuple-element.127), channel_id=1, source_target_pairs={{0,6},{1,7},{2,0},{3,1},{4,2},{5,3},{6,4},{7,5},{8,14},{9,15},{10,... | collective-permute-start | bytes 786440 | tf_op jit(solution)/shard_map/ppermute | solution.py:18
  106.4 4.3 %collective-permute-done.26.got_up = bf16[32,4096]{1,0:T(8,128)(2,1)S(1)} collective-permute-done((bf16[32,4096]{1,0:T(8,128)(2,1)S(1)}, bf16[32,4096]{1,0:T(8,128)(2,1)S(1)}, u32[]{:S(2)}, u32[]{:S(2)}) %collective-permute-start.26) | collective-permute-done | bytes 262176 | tf_op jit(solution)/shard_map/ppermute | solution.py:18
  110.7 1.5 %collective-permute-done.28.got_mate = bf16[32,4096]{1,0:T(8,128)(2,1)S(1)} collective-permute-done((bf16[32,4096]{1,0:T(8,128)(2,1)S(1)}, bf16[32,4096]{1,0:T(8,128)(2,1)S(1)}, u32[]{:S(2)}, u32[]{:S(2)}) %collective-permute-start.28) | collective-permute-done | bytes 262176 | tf_op jit(solution)/shard_map/ppermute | solution.py:22
  (51 shorter events, 22.3 us)
Async XLA Ops:
  2.8 10.1 %collective-permute-start.2 = (bf16[32,4096]{1,0:T(8,128)(2,1)}, bf16[32,4096]{1,0:T(8,128)(2,1)S(1)}, u32[]{:S(2)}, u32[]{:S(2)}) collective-permute-start(bf16[32,4096]{1,0:T(8,128)(2,1)} %get-tuple-element.66.b3), channel_id=1, source_target_pairs={{0,1},{1,0},{2,3},{3,2},{4,5},{5,4},{6,7},{7,6},{8,9},{9,8},{10,11... | collective-permute-start | bytes 786440 | tf_op jit(solution)/shard_map/ppermute | solution.py:22
  4.8 9.2 %collective-permute-start.1 = (bf16[32,4096]{1,0:T(8,128)(2,1)}, bf16[32,4096]{1,0:T(8,128)(2,1)S(1)}, u32[]{:S(2)}, u32[]{:S(2)}) collective-permute-start(bf16[32,4096]{1,0:T(8,128)(2,1)} %get-tuple-element.66.b3), channel_id=1, source_target_pairs={{0,2},{1,3},{2,4},{3,5},{4,6},{5,7},{6,0},{7,1},{8,10},{9,11},{10,... | collective-permute-start | bytes 786440 | tf_op jit(solution)/shard_map/ppermute | solution.py:18
  6.3 7.7 %collective-permute-start = (bf16[32,4096]{1,0:T(8,128)(2,1)}, bf16[32,4096]{1,0:T(8,128)(2,1)S(1)}, u32[]{:S(2)}, u32[]{:S(2)}) collective-permute-start(bf16[32,4096]{1,0:T(8,128)(2,1)} %get-tuple-element.66.b3), channel_id=1, source_target_pairs={{0,6},{1,7},{2,0},{3,1},{4,2},{5,3},{6,4},{7,5},{8,14},{9,15},{10,... | collective-permute-start | bytes 786440 | tf_op jit(solution)/shard_map/ppermute | solution.py:18
  14.0 12.6 %collective-permute-start.3 = (bf16[64,4096]{1,0:T(8,128)(2,1)S(1)}, bf16[64,4096]{1,0:T(8,128)(2,1)S(1)}, u32[]{:S(2)}, u32[]{:S(2)}) collective-permute-start(bf16[64,4096]{1,0:T(8,128)(2,1)S(1)} %get-tuple-element.70), channel_id=1, source_target_pairs={{0,1},{1,0},{2,3},{3,2},{4,5},{5,4},{6,7},{7,6},{8,9},{9,8},{10,11... | collective-permute-start | bytes 1572872 | tf_op jit(solution)/shard_map/ppermute | solution.py:22
  14.5 11.2 %collective-permute-start.6 = (bf16[32,4096]{1,0:T(8,128)(2,1)S(1)}, bf16[32,4096]{1,0:T(8,128)(2,1)S(1)}, u32[]{:S(2)}, u32[]{:S(2)}) collective-permute-start(bf16[32,4096]{1,0:T(8,128)(2,1)S(1)} %collective-permute-done.2.b2), channel_id=1, source_target_pairs={{0,4},{1,5},{2,6},{3,7},{4,0},{5,1},{6,2},{7,3},{8,12},{9,13},{10,... | collective-permute-start | bytes 786440 | tf_op jit(solution)/shard_map/ppermute | solution.py:18
  17.2 8.5 %collective-permute-start.4 = (bf16[32,2048]{1,0:T(8,128)(2,1)S(1)}, bf16[32,2048]{1,0:T(8,128)(2,1)S(1)}, u32[]{:S(2)}, u32[]{:S(2)}) collective-permute-start(bf16[32,2048]{1,0:T(8,128)(2,1)S(1)} %get-tuple-element.71), channel_id=1, source_target_pairs={{0,6},{1,7},{2,0},{3,1},{4,2},{5,3},{6,4},{7,5},{8,14},{9,15},{10,... | collective-permute-start | bytes 393224 | tf_op jit(solution)/shard_map/ppermute | solution.py:18
  18.7 7.0 %collective-permute-start.5 = (bf16[32,2048]{1,0:T(8,128)(2,1)S(1)}, bf16[32,2048]{1,0:T(8,128)(2,1)S(1)}, u32[]{:S(2)}, u32[]{:S(2)}) collective-permute-start(bf16[32,2048]{1,0:T(8,128)(2,1)S(1)} %get-tuple-element.72), channel_id=1, source_target_pairs={{0,2},{1,3},{2,4},{3,5},{4,6},{5,7},{6,0},{7,1},{8,10},{9,11},{10,... | collective-permute-start | bytes 393224 | tf_op jit(solution)/shard_map/ppermute | solution.py:18
  28.7 12.3 %collective-permute-start.7 = (bf16[64,4096]{1,0:T(8,128)(2,1)S(1)}, bf16[64,4096]{1,0:T(8,128)(2,1)S(1)}, u32[]{:S(2)}, u32[]{:S(2)}) collective-permute-start(bf16[64,4096]{1,0:T(8,128)(2,1)S(1)} %get-tuple-element.94), channel_id=1, source_target_pairs={{0,1},{1,0},{2,3},{3,2},{4,5},{5,4},{6,7},{7,6},{8,9},{9,8},{10,11... | collective-permute-start | bytes 1572872 | tf_op jit(solution)/shard_map/ppermute | solution.py:22
  29.5 11.5 %collective-permute-start.8 = (bf16[32,4096]{1,0:T(8,128)(2,1)S(1)}, bf16[32,4096]{1,0:T(8,128)(2,1)S(1)}, u32[]{:S(2)}, u32[]{:S(2)}) collective-permute-start(bf16[32,4096]{1,0:T(8,128)(2,1)S(1)} %get-tuple-element.95), channel_id=1, source_target_pairs={{0,4},{1,5},{2,6},{3,7},{4,0},{5,1},{6,2},{7,3},{8,12},{9,13},{10,... | collective-permute-start | bytes 786440 | tf_op jit(solution)/shard_map/ppermute | solution.py:18
  31.9 7.9 %collective-permute-start.9 = (bf16[32,2048]{1,0:T(8,128)(2,1)S(1)}, bf16[32,2048]{1,0:T(8,128)(2,1)S(1)}, u32[]{:S(2)}, u32[]{:S(2)}) collective-permute-start(bf16[32,2048]{1,0:T(8,128)(2,1)S(1)} %get-tuple-element.96), channel_id=1, source_target_pairs={{0,2},{1,3},{2,4},{3,5},{4,6},{5,7},{6,0},{7,1},{8,10},{9,11},{10,... | collective-permute-start | bytes 393224 | tf_op jit(solution)/shard_map/ppermute | solution.py:18
  33.0 8.0 %collective-permute-start.10 = (bf16[32,2048]{1,0:T(8,128)(2,1)S(1)}, bf16[32,2048]{1,0:T(8,128)(2,1)S(1)}, u32[]{:S(2)}, u32[]{:S(2)}) collective-permute-start(bf16[32,2048]{1,0:T(8,128)(2,1)S(1)} %get-tuple-element.97), channel_id=1, source_target_pairs={{0,6},{1,7},{2,0},{3,1},{4,2},{5,3},{6,4},{7,5},{8,14},{9,15},{10,... | collective-permute-start | bytes 393224 | tf_op jit(solution)/shard_map/ppermute | solution.py:18
  35.1 16.4 %copy-start = (f32[1,32,4096]{2,1,0:T(8,128)S(1)}, f32[1,32,4096]{2,1,0:T(8,128)}, u32[]{:S(2)}) copy-start(f32[1,32,4096]{2,1,0:T(8,128)} %rows.1) | copy-start | bytes 1572868
  36.8 23.5 %copy-start.2 = (f32[32,4096]{1,0:T(8,128)S(1)}, f32[32,4096]{1,0:T(8,128)}, u32[]{:S(2)}) copy-start(f32[32,4096]{1,0:T(8,128)} %fresh_ref.1) | copy-start | bytes 1572868
  36.8 23.5 %copy-start.4 = (f32[1,4096]{1,0:T(1,128)S(1)}, f32[1,4096]{1,0:T(1,128)}, u32[]{:S(2)}) copy-start(f32[1,4096]{1,0:T(1,128)} %gain_ref.1) | copy-start | bytes 49156
  41.2 8.7 %collective-permute-start.11 = (bf16[32,4096]{1,0:T(8,128)(2,1)S(1)}, bf16[32,4096]{1,0:T(8,128)(2,1)S(1)}, u32[]{:S(2)}, u32[]{:S(2)}) collective-permute-start(bf16[32,4096]{1,0:T(8,128)(2,1)S(1)} %get-tuple-element.98), channel_id=1, source_target_pairs={{0,2},{1,3},{2,4},{3,5},{4,6},{5,7},{6,0},{7,1},{8,10},{9,11},{10,... | collective-permute-start | bytes 786440 | tf_op jit(solution)/shard_map/ppermute | solution.py:18
  43.1 7.4 %collective-permute-start.12 = (bf16[32,4096]{1,0:T(8,128)(2,1)S(1)}, bf16[32,4096]{1,0:T(8,128)(2,1)S(1)}, u32[]{:S(2)}, u32[]{:S(2)}) collective-permute-start(bf16[32,4096]{1,0:T(8,128)(2,1)S(1)} %get-tuple-element.99), channel_id=1, source_target_pairs={{0,6},{1,7},{2,0},{3,1},{4,2},{5,3},{6,4},{7,5},{8,14},{9,15},{10,... | collective-permute-start | bytes 786440 | tf_op jit(solution)/shard_map/ppermute | solution.py:18
  44.6 6.9 %collective-permute-start.13 = (bf16[32,4096]{1,0:T(8,128)(2,1)S(1)}, bf16[32,4096]{1,0:T(8,128)(2,1)S(1)}, u32[]{:S(2)}, u32[]{:S(2)}) collective-permute-start(bf16[32,4096]{1,0:T(8,128)(2,1)S(1)} %get-tuple-element.100), channel_id=1, source_target_pairs={{0,1},{1,0},{2,3},{3,2},{4,5},{5,4},{6,7},{7,6},{8,9},{9,8},{10,11... | collective-permute-start | bytes 786440 | tf_op jit(solution)/shard_map/ppermute | solution.py:22
  51.6 8.7 %collective-permute-start.14 = (bf16[32,4096]{1,0:T(8,128)(2,1)S(1)}, bf16[32,4096]{1,0:T(8,128)(2,1)S(1)}, u32[]{:S(2)}, u32[]{:S(2)}) collective-permute-start(bf16[32,4096]{1,0:T(8,128)(2,1)S(1)} %shard_map.120), channel_id=1, source_target_pairs={{0,8},{8,16},{16,24},{24,32},{32,40},{40,48},{48,56},{56,64},{64,7... | collective-permute-start | bytes 786440 | tf_op jit(solution)/shard_map/ppermute | solution.py:26
  60.7 10.2 %collective-permute-start.17 = (bf16[32,4096]{1,0:T(8,128)(2,1)S(1)}, bf16[32,4096]{1,0:T(8,128)(2,1)S(1)}, u32[]{:S(2)}, u32[]{:S(2)}) collective-permute-start(bf16[32,4096]{1,0:T(8,128)(2,1)S(1)} %get-tuple-element.102.b3), channel_id=1, source_target_pairs={{0,1},{1,0},{2,3},{3,2},{4,5},{5,4},{6,7},{7,6},{8,9},{9,8},{10,11... | collective-permute-start | bytes 786440 | tf_op jit(solution)/shard_map/ppermute | solution.py:22
  64.2 9.4 %collective-permute-start.16 = (bf16[32,4096]{1,0:T(8,128)(2,1)S(1)}, bf16[32,4096]{1,0:T(8,128)(2,1)S(1)}, u32[]{:S(2)}, u32[]{:S(2)}) collective-permute-start(bf16[32,4096]{1,0:T(8,128)(2,1)S(1)} %get-tuple-element.102.b3), channel_id=1, source_target_pairs={{0,2},{1,3},{2,4},{3,5},{4,6},{5,7},{6,0},{7,1},{8,10},{9,11},{10,... | collective-permute-start | bytes 786440 | tf_op jit(solution)/shard_map/ppermute | solution.py:18
  65.3 8.3 %collective-permute-start.15 = (bf16[32,4096]{1,0:T(8,128)(2,1)S(1)}, bf16[32,4096]{1,0:T(8,128)(2,1)S(1)}, u32[]{:S(2)}, u32[]{:S(2)}) collective-permute-start(bf16[32,4096]{1,0:T(8,128)(2,1)S(1)} %get-tuple-element.102.b3), channel_id=1, source_target_pairs={{0,6},{1,7},{2,0},{3,1},{4,2},{5,3},{6,4},{7,5},{8,14},{9,15},{10,... | collective-permute-start | bytes 786440 | tf_op jit(solution)/shard_map/ppermute | solution.py:18
  73.7 13.1 %collective-permute-start.18 = (bf16[64,4096]{1,0:T(8,128)(2,1)S(1)}, bf16[64,4096]{1,0:T(8,128)(2,1)S(1)}, u32[]{:S(2)}, u32[]{:S(2)}) collective-permute-start(bf16[64,4096]{1,0:T(8,128)(2,1)S(1)} %get-tuple-element.105), channel_id=1, source_target_pairs={{0,1},{1,0},{2,3},{3,2},{4,5},{5,4},{6,7},{7,6},{8,9},{9,8},{10,11... | collective-permute-start | bytes 1572872 | tf_op jit(solution)/shard_map/ppermute | solution.py:22
  74.1 11.7 %collective-permute-start.21 = (bf16[32,4096]{1,0:T(8,128)(2,1)S(1)}, bf16[32,4096]{1,0:T(8,128)(2,1)S(1)}, u32[]{:S(2)}, u32[]{:S(2)}) collective-permute-start(bf16[32,4096]{1,0:T(8,128)(2,1)S(1)} %collective-permute-done.17.b2), channel_id=1, source_target_pairs={{0,4},{1,5},{2,6},{3,7},{4,0},{5,1},{6,2},{7,3},{8,12},{9,13},{10,... | collective-permute-start | bytes 786440 | tf_op jit(solution)/shard_map/ppermute | solution.py:18
  75.8 10.0 %collective-permute-start.19 = (bf16[32,2048]{1,0:T(8,128)(2,1)S(1)}, bf16[32,2048]{1,0:T(8,128)(2,1)S(1)}, u32[]{:S(2)}, u32[]{:S(2)}) collective-permute-start(bf16[32,2048]{1,0:T(8,128)(2,1)S(1)} %get-tuple-element.106), channel_id=1, source_target_pairs={{0,6},{1,7},{2,0},{3,1},{4,2},{5,3},{6,4},{7,5},{8,14},{9,15},{10,... | collective-permute-start | bytes 393224 | tf_op jit(solution)/shard_map/ppermute | solution.py:18
  77.2 8.6 %collective-permute-start.20 = (bf16[32,2048]{1,0:T(8,128)(2,1)S(1)}, bf16[32,2048]{1,0:T(8,128)(2,1)S(1)}, u32[]{:S(2)}, u32[]{:S(2)}) collective-permute-start(bf16[32,2048]{1,0:T(8,128)(2,1)S(1)} %get-tuple-element.107), channel_id=1, source_target_pairs={{0,2},{1,3},{2,4},{3,5},{4,6},{5,7},{6,0},{7,1},{8,10},{9,11},{10,... | collective-permute-start | bytes 393224 | tf_op jit(solution)/shard_map/ppermute | solution.py:18
  88.8 12.9 %collective-permute-start.22 = (bf16[64,4096]{1,0:T(8,128)(2,1)S(1)}, bf16[64,4096]{1,0:T(8,128)(2,1)S(1)}, u32[]{:S(2)}, u32[]{:S(2)}) collective-permute-start(bf16[64,4096]{1,0:T(8,128)(2,1)S(1)} %get-tuple-element.122), channel_id=1, source_target_pairs={{0,1},{1,0},{2,3},{3,2},{4,5},{5,4},{6,7},{7,6},{8,9},{9,8},{10,11... | collective-permute-start | bytes 1572872 | tf_op jit(solution)/shard_map/ppermute | solution.py:22
  89.8 11.4 %collective-permute-start.23 = (bf16[32,4096]{1,0:T(8,128)(2,1)S(1)}, bf16[32,4096]{1,0:T(8,128)(2,1)S(1)}, u32[]{:S(2)}, u32[]{:S(2)}) collective-permute-start(bf16[32,4096]{1,0:T(8,128)(2,1)S(1)} %get-tuple-element.123), channel_id=1, source_target_pairs={{0,4},{1,5},{2,6},{3,7},{4,0},{5,1},{6,2},{7,3},{8,12},{9,13},{10,... | collective-permute-start | bytes 786440 | tf_op jit(solution)/shard_map/ppermute | solution.py:18
  91.1 9.9 %collective-permute-start.24 = (bf16[32,2048]{1,0:T(8,128)(2,1)S(1)}, bf16[32,2048]{1,0:T(8,128)(2,1)S(1)}, u32[]{:S(2)}, u32[]{:S(2)}) collective-permute-start(bf16[32,2048]{1,0:T(8,128)(2,1)S(1)} %get-tuple-element.124), channel_id=1, source_target_pairs={{0,2},{1,3},{2,4},{3,5},{4,6},{5,7},{6,0},{7,1},{8,10},{9,11},{10,... | collective-permute-start | bytes 393224 | tf_op jit(solution)/shard_map/ppermute | solution.py:18
  93.3 7.9 %collective-permute-start.25 = (bf16[32,2048]{1,0:T(8,128)(2,1)S(1)}, bf16[32,2048]{1,0:T(8,128)(2,1)S(1)}, u32[]{:S(2)}, u32[]{:S(2)}) collective-permute-start(bf16[32,2048]{1,0:T(8,128)(2,1)S(1)} %get-tuple-element.125), channel_id=1, source_target_pairs={{0,6},{1,7},{2,0},{3,1},{4,2},{5,3},{6,4},{7,5},{8,14},{9,15},{10,... | collective-permute-start | bytes 393224 | tf_op jit(solution)/shard_map/ppermute | solution.py:18
  102.0 8.7 %collective-permute-start.26 = (bf16[32,4096]{1,0:T(8,128)(2,1)S(1)}, bf16[32,4096]{1,0:T(8,128)(2,1)S(1)}, u32[]{:S(2)}, u32[]{:S(2)}) collective-permute-start(bf16[32,4096]{1,0:T(8,128)(2,1)S(1)} %get-tuple-element.126), channel_id=1, source_target_pairs={{0,2},{1,3},{2,4},{3,5},{4,6},{5,7},{6,0},{7,1},{8,10},{9,11},{10,... | collective-permute-start | bytes 786440 | tf_op jit(solution)/shard_map/ppermute | solution.py:18
  102.6 8.0 %collective-permute-start.27 = (bf16[32,4096]{1,0:T(8,128)(2,1)S(1)}, bf16[32,4096]{1,0:T(8,128)(2,1)S(1)}, u32[]{:S(2)}, u32[]{:S(2)}) collective-permute-start(bf16[32,4096]{1,0:T(8,128)(2,1)S(1)} %get-tuple-element.127), channel_id=1, source_target_pairs={{0,6},{1,7},{2,0},{3,1},{4,2},{5,3},{6,4},{7,5},{8,14},{9,15},{10,... | collective-permute-start | bytes 786440 | tf_op jit(solution)/shard_map/ppermute | solution.py:18
  105.3 6.9 %collective-permute-start.28 = (bf16[32,4096]{1,0:T(8,128)(2,1)S(1)}, bf16[32,4096]{1,0:T(8,128)(2,1)S(1)}, u32[]{:S(2)}, u32[]{:S(2)}) collective-permute-start(bf16[32,4096]{1,0:T(8,128)(2,1)S(1)} %get-tuple-element.128), channel_id=1, source_target_pairs={{0,1},{1,0},{2,3},{3,2},{4,5},{5,4},{6,7},{7,6},{8,9},{9,8},{10,11... | collective-permute-start | bytes 786440 | tf_op jit(solution)/shard_map/ppermute | solution.py:22
  (2 other events, 17.9 us)

commit v6 on v5

--- a/solution.py
+++ b/solution.py
@@ -176,7 +176,11 @@
     new_state[0, 0] = keep * state[0, 0] + added
 
 
-def relay_kernel(up, down, to_mate, via_z, via_x, via_up, via_down, up_sum, down_sum, mate_sum):
+def relay_mate_kernel(to_mate, via_x, mate_sum):
+    mate_sum[...] = (to_mate[...].astype(jnp.float32) + via_x[...].astype(jnp.float32)).astype(mate_sum.dtype)
+
+
+def relay_kernel(up, down, via_z, via_up, via_down, up_sum, down_sum):
     f32 = jnp.float32
     count, width = via_up.shape
     up_total = up[...].astype(f32) + via_z[:count].astype(f32)
@@ -185,7 +189,6 @@
     up_sum[:, width:] = up_total[:, width:].astype(up_sum.dtype)
     down_sum[:, :width] = down_total[:, :width].astype(down_sum.dtype)
     down_sum[:, width:] = (down_total[:, width:] + via_down[...].astype(f32)).astype(down_sum.dtype)
-    mate_sum[...] = (to_mate[...].astype(f32) + via_x[...].astype(f32)).astype(mate_sum.dtype)
 
 
 def sum_kernel(rows, own, got_up, got_down, got_mate, out):
@@ -254,10 +257,10 @@
             flops=2 * half * value_size * width,
             moved=2 * value_size * width,
         )(log_keep, gated_late, out_weight, keys, values, tail, state)
-        up, down, to_mate = call(relay_kernel, [block] * 3, [VMEM] * 7, moved=8 * count * width)(
-            up, down, to_mate, via_z, via_x, via_up, via_down
-        )
-        got_up, got_down, got_mate = shift_x(up, 1), shift_x(down, -1), swap_z(to_mate)
+        to_mate = call(relay_mate_kernel, block, [VMEM] * 2, moved=6 * count * width)(to_mate, via_x)
+        got_mate = swap_z(to_mate)
+        up, down = call(relay_kernel, [block] * 2, [VMEM] * 5, moved=8 * count * width)(up, down, via_z, via_up, via_down)
+        got_up, got_down = shift_x(up, 1), shift_x(down, -1)
         parts = (rows, mine, got_up, got_down, got_mate)
         if turn_index == 0:
             result = call(sum_kernel, block, [VMEM] * 5, moved=16 * count * width)(*parts)

time: 115 us -> 114 us (level); the launches traced: 113 us -> 113 us
  starting transfers between devices: 44 us -> 46.3 us
  waiting for transfers between devices: 48.4 us -> 46.5 us
    ppermute x20, waiting for transfers between devices: 33.3 us -> 29.8 us  [shift_x(): lax.ppermute(value, 'tensor', [(t, (t + 2 * steps) % 8) for t in range(8)])]
    ppermute x20, starting transfers between devices: 31.8 us -> 34 us  [shift_x(): lax.ppermute(value, 'tensor', [(t, (t + 2 * steps) % 8) for t in range(8)])]
    ppermute x8, waiting for transfers between devices: 8.35 us -> 9.91 us  [swap_z(): return lax.ppermute(value, 'tensor', [(t, t ^ 1) for t in range(8)])]
  transfers between devices with their start and end apart: 29 -> 29, of which waited for: 18 -> 19; matrix products, arithmetic and copies ran while one was open for 0% -> 0% of each run, Pallas kernels for 10% -> 10%
where the time goes in v6:
time: 114 us; the launch traced here: 113 us
  waiting for transfers between devices  46.5 us (41%)
  starting transfers between devices  46.3 us (41%)
  Pallas kernels  19.3 us (17%)
  between operations  1.46 us (1%)
    ppermute x20, starting transfers between devices, shift_x(): lax.ppermute(value, 'tensor', [(t, (t + 2 * steps) % 8) for t in range(8)])  34 us
    ppermute x20, waiting for transfers between devices, shift_x(): lax.ppermute(value, 'tensor', [(t, (t + 2 * steps) % 8) for t in range(8)])  29.8 us
    ppermute x8, starting transfers between devices, swap_z(): return lax.ppermute(value, 'tensor', [(t, t ^ 1) for t in range(8)])  10.4 us
    ppermute x8, waiting for transfers between devices, swap_z(): return lax.ppermute(value, 'tensor', [(t, t ^ 1) for t in range(8)])  9.91 us
    ppermute x1, waiting for transfers between devices, next_section(): lax.ppermute(value, 'section', [(s, s + 1) for s in range(lax.axis_size('...  6.76 us
    pallas_call x2, Pallas kernels, body(): call(late_kernel, [double, block, half_block, half_block] + [shape((half,...  4.2 us
    pallas_call x1, Pallas kernels, body(): call(setup_kernel, [shape(a.shape, a.dtype) for a in (w_query, w_key, w_v...  4.14 us
    pallas_call x2, Pallas kernels, body(): call(out_kernel, [block] * 3 + [shape((count, width), f32), shape(state.s...  4.1 us
  transfers between devices with their start and end apart: 29, of which 19 were waited for; matrix products, arithmetic and copies ran while one was open for 0% of the time, Pallas kernels for 10%

profile of v6, /device:TPU:88, one launch (start us, length us, event | category | flops | bytes accessed | tf_op | source)
XLA Modules:
  0.0 113.5 jit_solution(18053603326618514333)
XLA Ops:
  0.6 2.2 %shard_map.113 = (bf16[32,4096]{1,0:T(8,128)(2,1)}, f32[1,1,256,256]{3,2,1,0:T(8,128)}) custom-call(f32[1,32,4096]{2,1,0:T(8,128)} %rows.1, f32[1,4096]{1,0:T(1,128)} %gain_ref.1, f32[1,1,256,256]{3,2,1,0:T(8,128)} %state_hbm.1), custom_call_target="tpu_custom_call" | custom-call | bytes 786432 | tf_op jit(solution)/shard_map/pallas_call | solution.py:212
  2.8 2.0 %collective-permute-start.2 = (bf16[32,4096]{1,0:T(8,128)(2,1)}, bf16[32,4096]{1,0:T(8,128)(2,1)S(1)}, u32[]{:S(2)}, u32[]{:S(2)}) collective-permute-start(bf16[32,4096]{1,0:T(8,128)(2,1)} %get-tuple-element.64.b3), channel_id=1, source_target_pairs={{0,1},{1,0},{2,3},{3,2},{4,5},{5,4},{6,7},{7,6},{8,9},{9,8},{10,11... | collective-permute-start | bytes 786440 | tf_op jit(solution)/shard_map/ppermute | solution.py:22
  4.8 1.5 %collective-permute-start.1 = (bf16[32,4096]{1,0:T(8,128)(2,1)}, bf16[32,4096]{1,0:T(8,128)(2,1)S(1)}, u32[]{:S(2)}, u32[]{:S(2)}) collective-permute-start(bf16[32,4096]{1,0:T(8,128)(2,1)} %get-tuple-element.64.b3), channel_id=1, source_target_pairs={{0,2},{1,3},{2,4},{3,5},{4,6},{5,7},{6,0},{7,1},{8,10},{9,11},{10,... | collective-permute-start | bytes 786440 | tf_op jit(solution)/shard_map/ppermute | solution.py:18
  6.3 1.7 %collective-permute-start = (bf16[32,4096]{1,0:T(8,128)(2,1)}, bf16[32,4096]{1,0:T(8,128)(2,1)S(1)}, u32[]{:S(2)}, u32[]{:S(2)}) collective-permute-start(bf16[32,4096]{1,0:T(8,128)(2,1)} %get-tuple-element.64.b3), channel_id=1, source_target_pairs={{0,6},{1,7},{2,0},{3,1},{4,2},{5,3},{6,4},{7,5},{8,14},{9,15},{10,... | collective-permute-start | bytes 786440 | tf_op jit(solution)/shard_map/ppermute | solution.py:18
  8.7 4.1 %shard_map.114 = (bf16[1,4096,256]{2,1,0:T(8,128)(2,1)S(1)}, bf16[1,4096,256]{2,1,0:T(8,128)(2,1)S(1)}, bf16[1,4096,256]{2,1,0:T(8,128)(2,1)S(1)}, bf16[1,4096,2...) custom-call(f32[1,1]{1,0:T(1,128)S(6)} %log1p.3.log_keep_ref, ...), custom_call_target="tpu_custom_call" | custom-call | bytes 10485760 | tf_op jit(solution)/shard_map/pallas_call | solution.py:224
  14.5 2.7 %collective-permute-start.6 = (bf16[32,4096]{1,0:T(8,128)(2,1)S(1)}, bf16[32,4096]{1,0:T(8,128)(2,1)S(1)}, u32[]{:S(2)}, u32[]{:S(2)}) collective-permute-start(bf16[32,4096]{1,0:T(8,128)(2,1)S(1)} %collective-permute-done.2.b2), channel_id=1, source_target_pairs={{0,4},{1,5},{2,6},{3,7},{4,0},{5,1},{6,2},{7,3},{8,12},{9,13},{10,... | collective-permute-start | bytes 786440 | tf_op jit(solution)/shard_map/ppermute | solution.py:18
  20.6 5.1 %collective-permute-done.4.b2_left = bf16[32,2048]{1,0:T(8,128)(2,1)S(1)} collective-permute-done((bf16[32,2048]{1,0:T(8,128)(2,1)S(1)}, bf16[32,2048]{1,0:T(8,128)(2,1)S(1)}, u32[]{:S(2)}, u32[]{:S(2)}) %collective-permute-start.4) | collective-permute-done | bytes 131104 | tf_op jit(solution)/shard_map/ppermute | solution.py:18
  26.6 2.1 %shard_map.117 = (bf16[64,4096]{1,0:T(8,128)(2,1)S(1)}, bf16[32,4096]{1,0:T(8,128)(2,1)S(1)}, bf16[32,2048]{1,0:T(8,128)(2,1)S(1)}, bf16[32,2048]{1,0:T(8,128)(2...) custom-call(bf16[64,4096]{1,0:T(8,128)(2,1)S(1)} %collective-permute-done.3.both, ...), custom_call_target="tpu_custom_call" | custom-call | flops 1073741824 | bytes 8388608 | tf_op jit(solution)/shard_map/pallas_call | solution.py:244
  29.5 2.4 %collective-permute-start.12 = (bf16[32,4096]{1,0:T(8,128)(2,1)S(1)}, bf16[32,4096]{1,0:T(8,128)(2,1)S(1)}, u32[]{:S(2)}, u32[]{:S(2)}) collective-permute-start(bf16[32,4096]{1,0:T(8,128)(2,1)S(1)} %get-tuple-element.97), channel_id=1, source_target_pairs={{0,4},{1,5},{2,6},{3,7},{4,0},{5,1},{6,2},{7,3},{8,12},{9,13},{10,... | collective-permute-start | bytes 786440 | tf_op jit(solution)/shard_map/ppermute | solution.py:18
  33.0 2.2 %collective-permute-start.9 = (bf16[32,2048]{1,0:T(8,128)(2,1)S(1)}, bf16[32,2048]{1,0:T(8,128)(2,1)S(1)}, u32[]{:S(2)}, u32[]{:S(2)}) collective-permute-start(bf16[32,2048]{1,0:T(8,128)(2,1)S(1)} %get-tuple-element.93), channel_id=1, source_target_pairs={{0,6},{1,7},{2,0},{3,1},{4,2},{5,3},{6,4},{7,5},{8,14},{9,15},{10,... | collective-permute-start | bytes 393224 | tf_op jit(solution)/shard_map/ppermute | solution.py:18
  35.1 1.7 %shard_map.118 = (bf16[32,4096]{1,0:T(8,128)(2,1)S(1)}, bf16[32,4096]{1,0:T(8,128)(2,1)S(1)}, bf16[32,4096]{1,0:T(8,128)(2,1)S(1)}, f32[32,4096]{1,0:T(8,128)S(1)}, f32[1,1,256,256]{3,2,1,0:T(8,128)S(1)}) custom-call(f32[1,1]{1,0:T(1,128)S(6)} %log1p.3.log_keep_ref, bf16[128,256]{1,0:T(8,128)(2,1)S(1)} %get-tuple-element.84.gated, ...), custom_call_target="tpu_custom_call" | custom-call | flops 268435456 | bytes 2097152 | tf_op jit(solution)/shard_map/pallas_call | solution.py:253
  36.8 1.7 %collective-permute-done.12.via_x = bf16[32,4096]{1,0:T(8,128)(2,1)S(1)} collective-permute-done((bf16[32,4096]{1,0:T(8,128)(2,1)S(1)}, bf16[32,4096]{1,0:T(8,128)(2,1)S(1)}, u32[]{:S(2)}, u32[]{:S(2)}) %collective-permute-start.12) | collective-permute-done | bytes 262176 | tf_op jit(solution)/shard_map/ppermute | solution.py:18
  41.0 2.2 %collective-permute-done.7.via_z = bf16[64,4096]{1,0:T(8,128)(2,1)S(1)} collective-permute-done((bf16[64,4096]{1,0:T(8,128)(2,1)S(1)}, bf16[64,4096]{1,0:T(8,128)(2,1)S(1)}, u32[]{:S(2)}, u32[]{:S(2)}) %collective-permute-start.7) | collective-permute-done | bytes 524320 | tf_op jit(solution)/shard_map/ppermute | solution.py:22
  43.3 1.8 %collective-permute-start.10 = (bf16[32,4096]{1,0:T(8,128)(2,1)S(1)}, bf16[32,4096]{1,0:T(8,128)(2,1)S(1)}, u32[]{:S(2)}, u32[]{:S(2)}) collective-permute-start(bf16[32,4096]{1,0:T(8,128)(2,1)S(1)} %get-tuple-element.94), channel_id=1, source_target_pairs={{0,2},{1,3},{2,4},{3,5},{4,6},{5,7},{6,0},{7,1},{8,10},{9,11},{10,... | collective-permute-start | bytes 786440 | tf_op jit(solution)/shard_map/ppermute | solution.py:18
  45.1 1.6 %collective-permute-start.11 = (bf16[32,4096]{1,0:T(8,128)(2,1)S(1)}, bf16[32,4096]{1,0:T(8,128)(2,1)S(1)}, u32[]{:S(2)}, u32[]{:S(2)}) collective-permute-start(bf16[32,4096]{1,0:T(8,128)(2,1)S(1)} %get-tuple-element.95), channel_id=1, source_target_pairs={{0,6},{1,7},{2,0},{3,1},{4,2},{5,3},{6,4},{7,5},{8,14},{9,15},{10,... | collective-permute-start | bytes 786440 | tf_op jit(solution)/shard_map/ppermute | solution.py:18
  46.7 4.3 %collective-permute-done.10.got_up = bf16[32,4096]{1,0:T(8,128)(2,1)S(1)} collective-permute-done((bf16[32,4096]{1,0:T(8,128)(2,1)S(1)}, bf16[32,4096]{1,0:T(8,128)(2,1)S(1)}, u32[]{:S(2)}, u32[]{:S(2)}) %collective-permute-start.10) | collective-permute-done | bytes 262176 | tf_op jit(solution)/shard_map/ppermute | solution.py:18
  51.7 1.9 %collective-permute-start.14 = (bf16[32,4096]{1,0:T(8,128)(2,1)S(1)}, bf16[32,4096]{1,0:T(8,128)(2,1)S(1)}, u32[]{:S(2)}, u32[]{:S(2)}) collective-permute-start(bf16[32,4096]{1,0:T(8,128)(2,1)S(1)} %shard_map.121), channel_id=1, source_target_pairs={{0,8},{8,16},{16,24},{24,32},{32,40},{40,48},{48,56},{56,64},{64,7... | collective-permute-start | bytes 786440 | tf_op jit(solution)/shard_map/ppermute | solution.py:26
  53.6 6.8 %collective-permute-done.14.arrived_ref = bf16[32,4096]{1,0:T(8,128)(2,1)S(1)} collective-permute-done((bf16[32,4096]{1,0:T(8,128)(2,1)S(1)}, bf16[32,4096]{1,0:T(8,128)(2,1)S(1)}, u32[]{:S(2)}, u32[]{:S(2)}) %collective-permute-start.14) | collective-permute-done | bytes 262176 | tf_op jit(solution)/shard_map/ppermute | solution.py:26
  60.7 3.5 %collective-permute-start.17 = (bf16[32,4096]{1,0:T(8,128)(2,1)S(1)}, bf16[32,4096]{1,0:T(8,128)(2,1)S(1)}, u32[]{:S(2)}, u32[]{:S(2)}) collective-permute-start(bf16[32,4096]{1,0:T(8,128)(2,1)S(1)} %get-tuple-element.99.b3), channel_id=1, source_target_pairs={{0,1},{1,0},{2,3},{3,2},{4,5},{5,4},{6,7},{7,6},{8,9},{9,8},{10,11... | collective-permute-start | bytes 786440 | tf_op jit(solution)/shard_map/ppermute | solution.py:22
  65.4 2.0 %collective-permute-start.15 = (bf16[32,4096]{1,0:T(8,128)(2,1)S(1)}, bf16[32,4096]{1,0:T(8,128)(2,1)S(1)}, u32[]{:S(2)}, u32[]{:S(2)}) collective-permute-start(bf16[32,4096]{1,0:T(8,128)(2,1)S(1)} %get-tuple-element.99.b3), channel_id=1, source_target_pairs={{0,6},{1,7},{2,0},{3,1},{4,2},{5,3},{6,4},{7,5},{8,14},{9,15},{10,... | collective-permute-start | bytes 786440 | tf_op jit(solution)/shard_map/ppermute | solution.py:18
  67.5 3.8 %collective-permute-done.17.b2 = bf16[32,4096]{1,0:T(8,128)(2,1)S(1)} collective-permute-done((bf16[32,4096]{1,0:T(8,128)(2,1)S(1)}, bf16[32,4096]{1,0:T(8,128)(2,1)S(1)}, u32[]{:S(2)}, u32[]{:S(2)}) %collective-permute-start.17) | collective-permute-done | bytes 262176 | tf_op jit(solution)/shard_map/ppermute | solution.py:22
  71.3 2.7 %collective-permute-done.16.below.b1 = bf16[32,4096]{1,0:T(8,128)(2,1)S(1)} collective-permute-done((bf16[32,4096]{1,0:T(8,128)(2,1)S(1)}, bf16[32,4096]{1,0:T(8,128)(2,1)S(1)}, u32[]{:S(2)}, u32[]{:S(2)}) %collective-permute-start.16) | collective-permute-done | bytes 262176 | tf_op jit(solution)/shard_map/ppermute | solution.py:18
  74.5 2.9 %collective-permute-start.21 = (bf16[32,4096]{1,0:T(8,128)(2,1)S(1)}, bf16[32,4096]{1,0:T(8,128)(2,1)S(1)}, u32[]{:S(2)}, u32[]{:S(2)}) collective-permute-start(bf16[32,4096]{1,0:T(8,128)(2,1)S(1)} %collective-permute-done.17.b2), channel_id=1, source_target_pairs={{0,4},{1,5},{2,6},{3,7},{4,0},{5,1},{6,2},{7,3},{8,12},{9,13},{10,... | collective-permute-start | bytes 786440 | tf_op jit(solution)/shard_map/ppermute | solution.py:18
  80.7 5.8 %collective-permute-done.19.b2_left = bf16[32,2048]{1,0:T(8,128)(2,1)S(1)} collective-permute-done((bf16[32,2048]{1,0:T(8,128)(2,1)S(1)}, bf16[32,2048]{1,0:T(8,128)(2,1)S(1)}, u32[]{:S(2)}, u32[]{:S(2)}) %collective-permute-start.19) | collective-permute-done | bytes 131104 | tf_op jit(solution)/shard_map/ppermute | solution.py:18
  87.4 2.1 %shard_map.125 = (bf16[64,4096]{1,0:T(8,128)(2,1)S(1)}, bf16[32,4096]{1,0:T(8,128)(2,1)S(1)}, bf16[32,2048]{1,0:T(8,128)(2,1)S(1)}, bf16[32,2048]{1,0:T(8,128)(2...) custom-call(bf16[64,4096]{1,0:T(8,128)(2,1)S(1)} %collective-permute-done.18.both,, ...), custom_call_target="tpu_custom_call" | custom-call | flops 1073741824 | bytes 8388608 | tf_op jit(solution)/shard_map/pallas_call | solution.py:244
  90.5 2.3 %collective-permute-start.27 = (bf16[32,4096]{1,0:T(8,128)(2,1)S(1)}, bf16[32,4096]{1,0:T(8,128)(2,1)S(1)}, u32[]{:S(2)}, u32[]{:S(2)}) collective-permute-start(bf16[32,4096]{1,0:T(8,128)(2,1)S(1)} %get-tuple-element.124), channel_id=1, source_target_pairs={{0,4},{1,5},{2,6},{3,7},{4,0},{5,1},{6,2},{7,3},{8,12},{9,13},{10,... | collective-permute-start | bytes 786440 | tf_op jit(solution)/shard_map/ppermute | solution.py:18
  94.0 2.1 %collective-permute-start.24 = (bf16[32,2048]{1,0:T(8,128)(2,1)S(1)}, bf16[32,2048]{1,0:T(8,128)(2,1)S(1)}, u32[]{:S(2)}, u32[]{:S(2)}) collective-permute-start(bf16[32,2048]{1,0:T(8,128)(2,1)S(1)} %get-tuple-element.120), channel_id=1, source_target_pairs={{0,6},{1,7},{2,0},{3,1},{4,2},{5,3},{6,4},{7,5},{8,14},{9,15},{10,... | collective-permute-start | bytes 393224 | tf_op jit(solution)/shard_map/ppermute | solution.py:18
  96.1 2.4 %shard_map.126 = (bf16[32,4096]{1,0:T(8,128)(2,1)S(1)}, bf16[32,4096]{1,0:T(8,128)(2,1)S(1)}, bf16[32,4096]{1,0:T(8,128)(2,1)S(1)}, f32[32,4096]{1,0:T(8,128)S(1)}, f32[1,1,256,256]{3,2,1,0:T(8,128)}) custom-call(f32[1,1]{1,0:T(1,128)S(6)} %log1p.3.log_keep_ref, bf16[128,256]{1,0:T(8,128)(2,1)S(1)} %get-tuple-element.112.gated, ...), custom_call_target="tpu_custom_call" | custom-call | flops 268435456 | bytes 2097152 | tf_op jit(solution)/shard_map/pallas_call | solution.py:253
  98.5 1.9 %collective-permute-done.27.via_x = bf16[32,4096]{1,0:T(8,128)(2,1)S(1)} collective-permute-done((bf16[32,4096]{1,0:T(8,128)(2,1)S(1)}, bf16[32,4096]{1,0:T(8,128)(2,1)S(1)}, u32[]{:S(2)}, u32[]{:S(2)}) %collective-permute-start.27) | collective-permute-done | bytes 262176 | tf_op jit(solution)/shard_map/ppermute | solution.py:18
  102.6 2.1 %collective-permute-done.22.via_z = bf16[64,4096]{1,0:T(8,128)(2,1)S(1)} collective-permute-done((bf16[64,4096]{1,0:T(8,128)(2,1)S(1)}, bf16[64,4096]{1,0:T(8,128)(2,1)S(1)}, u32[]{:S(2)}, u32[]{:S(2)}) %collective-permute-start.22) | collective-permute-done | bytes 524320 | tf_op jit(solution)/shard_map/ppermute | solution.py:22
  105.8 2.4 %collective-permute-start.26 = (bf16[32,4096]{1,0:T(8,128)(2,1)S(1)}, bf16[32,4096]{1,0:T(8,128)(2,1)S(1)}, u32[]{:S(2)}, u32[]{:S(2)}) collective-permute-start(bf16[32,4096]{1,0:T(8,128)(2,1)S(1)} %get-tuple-element.122), channel_id=1, source_target_pairs={{0,6},{1,7},{2,0},{3,1},{4,2},{5,3},{6,4},{7,5},{8,14},{9,15},{10,... | collective-permute-start | bytes 786440 | tf_op jit(solution)/shard_map/ppermute | solution.py:18
  108.2 4.3 %collective-permute-done.25.got_up = bf16[32,4096]{1,0:T(8,128)(2,1)S(1)} collective-permute-done((bf16[32,4096]{1,0:T(8,128)(2,1)S(1)}, bf16[32,4096]{1,0:T(8,128)(2,1)S(1)}, u32[]{:S(2)}, u32[]{:S(2)}) %collective-permute-start.25) | collective-permute-done | bytes 262176 | tf_op jit(solution)/shard_map/ppermute | solution.py:18
  (53 shorter events, 23.7 us)
Async XLA Ops:
  2.8 10.1 %collective-permute-start.2 = (bf16[32,4096]{1,0:T(8,128)(2,1)}, bf16[32,4096]{1,0:T(8,128)(2,1)S(1)}, u32[]{:S(2)}, u32[]{:S(2)}) collective-permute-start(bf16[32,4096]{1,0:T(8,128)(2,1)} %get-tuple-element.64.b3), channel_id=1, source_target_pairs={{0,1},{1,0},{2,3},{3,2},{4,5},{5,4},{6,7},{7,6},{8,9},{9,8},{10,11... | collective-permute-start | bytes 786440 | tf_op jit(solution)/shard_map/ppermute | solution.py:22
  4.8 9.2 %collective-permute-start.1 = (bf16[32,4096]{1,0:T(8,128)(2,1)}, bf16[32,4096]{1,0:T(8,128)(2,1)S(1)}, u32[]{:S(2)}, u32[]{:S(2)}) collective-permute-start(bf16[32,4096]{1,0:T(8,128)(2,1)} %get-tuple-element.64.b3), channel_id=1, source_target_pairs={{0,2},{1,3},{2,4},{3,5},{4,6},{5,7},{6,0},{7,1},{8,10},{9,11},{10,... | collective-permute-start | bytes 786440 | tf_op jit(solution)/shard_map/ppermute | solution.py:18
  6.3 7.7 %collective-permute-start = (bf16[32,4096]{1,0:T(8,128)(2,1)}, bf16[32,4096]{1,0:T(8,128)(2,1)S(1)}, u32[]{:S(2)}, u32[]{:S(2)}) collective-permute-start(bf16[32,4096]{1,0:T(8,128)(2,1)} %get-tuple-element.64.b3), channel_id=1, source_target_pairs={{0,6},{1,7},{2,0},{3,1},{4,2},{5,3},{6,4},{7,5},{8,14},{9,15},{10,... | collective-permute-start | bytes 786440 | tf_op jit(solution)/shard_map/ppermute | solution.py:18
  14.0 12.6 %collective-permute-start.3 = (bf16[64,4096]{1,0:T(8,128)(2,1)S(1)}, bf16[64,4096]{1,0:T(8,128)(2,1)S(1)}, u32[]{:S(2)}, u32[]{:S(2)}) collective-permute-start(bf16[64,4096]{1,0:T(8,128)(2,1)S(1)} %get-tuple-element.68), channel_id=1, source_target_pairs={{0,1},{1,0},{2,3},{3,2},{4,5},{5,4},{6,7},{7,6},{8,9},{9,8},{10,11... | collective-permute-start | bytes 1572872 | tf_op jit(solution)/shard_map/ppermute | solution.py:22
  14.5 11.2 %collective-permute-start.6 = (bf16[32,4096]{1,0:T(8,128)(2,1)S(1)}, bf16[32,4096]{1,0:T(8,128)(2,1)S(1)}, u32[]{:S(2)}, u32[]{:S(2)}) collective-permute-start(bf16[32,4096]{1,0:T(8,128)(2,1)S(1)} %collective-permute-done.2.b2), channel_id=1, source_target_pairs={{0,4},{1,5},{2,6},{3,7},{4,0},{5,1},{6,2},{7,3},{8,12},{9,13},{10,... | collective-permute-start | bytes 786440 | tf_op jit(solution)/shard_map/ppermute | solution.py:18
  17.2 8.5 %collective-permute-start.4 = (bf16[32,2048]{1,0:T(8,128)(2,1)S(1)}, bf16[32,2048]{1,0:T(8,128)(2,1)S(1)}, u32[]{:S(2)}, u32[]{:S(2)}) collective-permute-start(bf16[32,2048]{1,0:T(8,128)(2,1)S(1)} %get-tuple-element.69), channel_id=1, source_target_pairs={{0,6},{1,7},{2,0},{3,1},{4,2},{5,3},{6,4},{7,5},{8,14},{9,15},{10,... | collective-permute-start | bytes 393224 | tf_op jit(solution)/shard_map/ppermute | solution.py:18
  18.7 7.0 %collective-permute-start.5 = (bf16[32,2048]{1,0:T(8,128)(2,1)S(1)}, bf16[32,2048]{1,0:T(8,128)(2,1)S(1)}, u32[]{:S(2)}, u32[]{:S(2)}) collective-permute-start(bf16[32,2048]{1,0:T(8,128)(2,1)S(1)} %get-tuple-element.70), channel_id=1, source_target_pairs={{0,2},{1,3},{2,4},{3,5},{4,6},{5,7},{6,0},{7,1},{8,10},{9,11},{10,... | collective-permute-start | bytes 393224 | tf_op jit(solution)/shard_map/ppermute | solution.py:18
  28.7 14.4 %collective-permute-start.7 = (bf16[64,4096]{1,0:T(8,128)(2,1)S(1)}, bf16[64,4096]{1,0:T(8,128)(2,1)S(1)}, u32[]{:S(2)}, u32[]{:S(2)}) collective-permute-start(bf16[64,4096]{1,0:T(8,128)(2,1)S(1)} %get-tuple-element.91), channel_id=1, source_target_pairs={{0,1},{1,0},{2,3},{3,2},{4,5},{5,4},{6,7},{7,6},{8,9},{9,8},{10,11... | collective-permute-start | bytes 1572872 | tf_op jit(solution)/shard_map/ppermute | solution.py:22
  29.5 9.0 %collective-permute-start.12 = (bf16[32,4096]{1,0:T(8,128)(2,1)S(1)}, bf16[32,4096]{1,0:T(8,128)(2,1)S(1)}, u32[]{:S(2)}, u32[]{:S(2)}) collective-permute-start(bf16[32,4096]{1,0:T(8,128)(2,1)S(1)} %get-tuple-element.97), channel_id=1, source_target_pairs={{0,4},{1,5},{2,6},{3,7},{4,0},{5,1},{6,2},{7,3},{8,12},{9,13},{10,... | collective-permute-start | bytes 786440 | tf_op jit(solution)/shard_map/ppermute | solution.py:18
  31.9 7.9 %collective-permute-start.8 = (bf16[32,2048]{1,0:T(8,128)(2,1)S(1)}, bf16[32,2048]{1,0:T(8,128)(2,1)S(1)}, u32[]{:S(2)}, u32[]{:S(2)}) collective-permute-start(bf16[32,2048]{1,0:T(8,128)(2,1)S(1)} %get-tuple-element.92), channel_id=1, source_target_pairs={{0,2},{1,3},{2,4},{3,5},{4,6},{5,7},{6,0},{7,1},{8,10},{9,11},{10,... | collective-permute-start | bytes 393224 | tf_op jit(solution)/shard_map/ppermute | solution.py:18
  33.0 8.0 %collective-permute-start.9 = (bf16[32,2048]{1,0:T(8,128)(2,1)S(1)}, bf16[32,2048]{1,0:T(8,128)(2,1)S(1)}, u32[]{:S(2)}, u32[]{:S(2)}) collective-permute-start(bf16[32,2048]{1,0:T(8,128)(2,1)S(1)} %get-tuple-element.93), channel_id=1, source_target_pairs={{0,6},{1,7},{2,0},{3,1},{4,2},{5,3},{6,4},{7,5},{8,14},{9,15},{10,... | collective-permute-start | bytes 393224 | tf_op jit(solution)/shard_map/ppermute | solution.py:18
  35.1 16.4 %copy-start = (f32[1,32,4096]{2,1,0:T(8,128)S(1)}, f32[1,32,4096]{2,1,0:T(8,128)}, u32[]{:S(2)}) copy-start(f32[1,32,4096]{2,1,0:T(8,128)} %rows.1) | copy-start | bytes 1572868
  38.5 21.9 %copy-start.2 = (f32[32,4096]{1,0:T(8,128)S(1)}, f32[32,4096]{1,0:T(8,128)}, u32[]{:S(2)}) copy-start(f32[32,4096]{1,0:T(8,128)} %fresh_ref.1) | copy-start | bytes 1572868
  38.5 21.9 %copy-start.4 = (f32[1,4096]{1,0:T(1,128)S(1)}, f32[1,4096]{1,0:T(1,128)}, u32[]{:S(2)}) copy-start(f32[1,4096]{1,0:T(1,128)} %gain_ref.1) | copy-start | bytes 49156
  38.5 8.1 %collective-permute-start.13 = (bf16[32,4096]{1,0:T(8,128)(2,1)S(1)}, bf16[32,4096]{1,0:T(8,128)(2,1)S(1)}, u32[]{:S(2)}, u32[]{:S(2)}) collective-permute-start(bf16[32,4096]{1,0:T(8,128)(2,1)S(1)} %shard_map.120), channel_id=1, source_target_pairs={{0,1},{1,0},{2,3},{3,2},{4,5},{5,4},{6,7},{7,6},{8,9},{9,8},{10,11... | collective-permute-start | bytes 786440 | tf_op jit(solution)/shard_map/ppermute | solution.py:22
  43.3 7.7 %collective-permute-start.10 = (bf16[32,4096]{1,0:T(8,128)(2,1)S(1)}, bf16[32,4096]{1,0:T(8,128)(2,1)S(1)}, u32[]{:S(2)}, u32[]{:S(2)}) collective-permute-start(bf16[32,4096]{1,0:T(8,128)(2,1)S(1)} %get-tuple-element.94), channel_id=1, source_target_pairs={{0,2},{1,3},{2,4},{3,5},{4,6},{5,7},{6,0},{7,1},{8,10},{9,11},{10,... | collective-permute-start | bytes 786440 | tf_op jit(solution)/shard_map/ppermute | solution.py:18
  45.1 6.4 %collective-permute-start.11 = (bf16[32,4096]{1,0:T(8,128)(2,1)S(1)}, bf16[32,4096]{1,0:T(8,128)(2,1)S(1)}, u32[]{:S(2)}, u32[]{:S(2)}) collective-permute-start(bf16[32,4096]{1,0:T(8,128)(2,1)S(1)} %get-tuple-element.95), channel_id=1, source_target_pairs={{0,6},{1,7},{2,0},{3,1},{4,2},{5,3},{6,4},{7,5},{8,14},{9,15},{10,... | collective-permute-start | bytes 786440 | tf_op jit(solution)/shard_map/ppermute | solution.py:18
  51.7 8.7 %collective-permute-start.14 = (bf16[32,4096]{1,0:T(8,128)(2,1)S(1)}, bf16[32,4096]{1,0:T(8,128)(2,1)S(1)}, u32[]{:S(2)}, u32[]{:S(2)}) collective-permute-start(bf16[32,4096]{1,0:T(8,128)(2,1)S(1)} %shard_map.121), channel_id=1, source_target_pairs={{0,8},{8,16},{16,24},{24,32},{32,40},{40,48},{48,56},{56,64},{64,7... | collective-permute-start | bytes 786440 | tf_op jit(solution)/shard_map/ppermute | solution.py:26
  60.7 10.6 %collective-permute-start.17 = (bf16[32,4096]{1,0:T(8,128)(2,1)S(1)}, bf16[32,4096]{1,0:T(8,128)(2,1)S(1)}, u32[]{:S(2)}, u32[]{:S(2)}) collective-permute-start(bf16[32,4096]{1,0:T(8,128)(2,1)S(1)} %get-tuple-element.99.b3), channel_id=1, source_target_pairs={{0,1},{1,0},{2,3},{3,2},{4,5},{5,4},{6,7},{7,6},{8,9},{9,8},{10,11... | collective-permute-start | bytes 786440 | tf_op jit(solution)/shard_map/ppermute | solution.py:22
  64.2 9.7 %collective-permute-start.16 = (bf16[32,4096]{1,0:T(8,128)(2,1)S(1)}, bf16[32,4096]{1,0:T(8,128)(2,1)S(1)}, u32[]{:S(2)}, u32[]{:S(2)}) collective-permute-start(bf16[32,4096]{1,0:T(8,128)(2,1)S(1)} %get-tuple-element.99.b3), channel_id=1, source_target_pairs={{0,2},{1,3},{2,4},{3,5},{4,6},{5,7},{6,0},{7,1},{8,10},{9,11},{10,... | collective-permute-start | bytes 786440 | tf_op jit(solution)/shard_map/ppermute | solution.py:18
  65.4 8.5 %collective-permute-start.15 = (bf16[32,4096]{1,0:T(8,128)(2,1)S(1)}, bf16[32,4096]{1,0:T(8,128)(2,1)S(1)}, u32[]{:S(2)}, u32[]{:S(2)}) collective-permute-start(bf16[32,4096]{1,0:T(8,128)(2,1)S(1)} %get-tuple-element.99.b3), channel_id=1, source_target_pairs={{0,6},{1,7},{2,0},{3,1},{4,2},{5,3},{6,4},{7,5},{8,14},{9,15},{10,... | collective-permute-start | bytes 786440 | tf_op jit(solution)/shard_map/ppermute | solution.py:18
  74.0 13.4 %collective-permute-start.18 = (bf16[64,4096]{1,0:T(8,128)(2,1)S(1)}, bf16[64,4096]{1,0:T(8,128)(2,1)S(1)}, u32[]{:S(2)}, u32[]{:S(2)}) collective-permute-start(bf16[64,4096]{1,0:T(8,128)(2,1)S(1)} %get-tuple-element.102), channel_id=1, source_target_pairs={{0,1},{1,0},{2,3},{3,2},{4,5},{5,4},{6,7},{7,6},{8,9},{9,8},{10,11... | collective-permute-start | bytes 1572872 | tf_op jit(solution)/shard_map/ppermute | solution.py:22
  74.5 12.1 %collective-permute-start.21 = (bf16[32,4096]{1,0:T(8,128)(2,1)S(1)}, bf16[32,4096]{1,0:T(8,128)(2,1)S(1)}, u32[]{:S(2)}, u32[]{:S(2)}) collective-permute-start(bf16[32,4096]{1,0:T(8,128)(2,1)S(1)} %collective-permute-done.17.b2), channel_id=1, source_target_pairs={{0,4},{1,5},{2,6},{3,7},{4,0},{5,1},{6,2},{7,3},{8,12},{9,13},{10,... | collective-permute-start | bytes 786440 | tf_op jit(solution)/shard_map/ppermute | solution.py:18
  77.4 9.2 %collective-permute-start.19 = (bf16[32,2048]{1,0:T(8,128)(2,1)S(1)}, bf16[32,2048]{1,0:T(8,128)(2,1)S(1)}, u32[]{:S(2)}, u32[]{:S(2)}) collective-permute-start(bf16[32,2048]{1,0:T(8,128)(2,1)S(1)} %get-tuple-element.103), channel_id=1, source_target_pairs={{0,6},{1,7},{2,0},{3,1},{4,2},{5,3},{6,4},{7,5},{8,14},{9,15},{10,... | collective-permute-start | bytes 393224 | tf_op jit(solution)/shard_map/ppermute | solution.py:18
  78.5 8.0 %collective-permute-start.20 = (bf16[32,2048]{1,0:T(8,128)(2,1)S(1)}, bf16[32,2048]{1,0:T(8,128)(2,1)S(1)}, u32[]{:S(2)}, u32[]{:S(2)}) collective-permute-start(bf16[32,2048]{1,0:T(8,128)(2,1)S(1)} %get-tuple-element.104), channel_id=1, source_target_pairs={{0,2},{1,3},{2,4},{3,5},{4,6},{5,7},{6,0},{7,1},{8,10},{9,11},{10,... | collective-permute-start | bytes 393224 | tf_op jit(solution)/shard_map/ppermute | solution.py:18
  89.5 15.2 %collective-permute-start.22 = (bf16[64,4096]{1,0:T(8,128)(2,1)S(1)}, bf16[64,4096]{1,0:T(8,128)(2,1)S(1)}, u32[]{:S(2)}, u32[]{:S(2)}) collective-permute-start(bf16[64,4096]{1,0:T(8,128)(2,1)S(1)} %get-tuple-element.118), channel_id=1, source_target_pairs={{0,1},{1,0},{2,3},{3,2},{4,5},{5,4},{6,7},{7,6},{8,9},{9,8},{10,11... | collective-permute-start | bytes 1572872 | tf_op jit(solution)/shard_map/ppermute | solution.py:22
  90.5 9.8 %collective-permute-start.27 = (bf16[32,4096]{1,0:T(8,128)(2,1)S(1)}, bf16[32,4096]{1,0:T(8,128)(2,1)S(1)}, u32[]{:S(2)}, u32[]{:S(2)}) collective-permute-start(bf16[32,4096]{1,0:T(8,128)(2,1)S(1)} %get-tuple-element.124), channel_id=1, source_target_pairs={{0,4},{1,5},{2,6},{3,7},{4,0},{5,1},{6,2},{7,3},{8,12},{9,13},{10,... | collective-permute-start | bytes 786440 | tf_op jit(solution)/shard_map/ppermute | solution.py:18
  92.9 8.9 %collective-permute-start.23 = (bf16[32,2048]{1,0:T(8,128)(2,1)S(1)}, bf16[32,2048]{1,0:T(8,128)(2,1)S(1)}, u32[]{:S(2)}, u32[]{:S(2)}) collective-permute-start(bf16[32,2048]{1,0:T(8,128)(2,1)S(1)} %get-tuple-element.119), channel_id=1, source_target_pairs={{0,2},{1,3},{2,4},{3,5},{4,6},{5,7},{6,0},{7,1},{8,10},{9,11},{10,... | collective-permute-start | bytes 393224 | tf_op jit(solution)/shard_map/ppermute | solution.py:18
  94.0 8.6 %collective-permute-start.24 = (bf16[32,2048]{1,0:T(8,128)(2,1)S(1)}, bf16[32,2048]{1,0:T(8,128)(2,1)S(1)}, u32[]{:S(2)}, u32[]{:S(2)}) collective-permute-start(bf16[32,2048]{1,0:T(8,128)(2,1)S(1)} %get-tuple-element.120), channel_id=1, source_target_pairs={{0,6},{1,7},{2,0},{3,1},{4,2},{5,3},{6,4},{7,5},{8,14},{9,15},{10,... | collective-permute-start | bytes 393224 | tf_op jit(solution)/shard_map/ppermute | solution.py:18
  100.4 7.7 %collective-permute-start.28 = (bf16[32,4096]{1,0:T(8,128)(2,1)S(1)}, bf16[32,4096]{1,0:T(8,128)(2,1)S(1)}, u32[]{:S(2)}, u32[]{:S(2)}) collective-permute-start(bf16[32,4096]{1,0:T(8,128)(2,1)S(1)} %shard_map.128), channel_id=1, source_target_pairs={{0,1},{1,0},{2,3},{3,2},{4,5},{5,4},{6,7},{7,6},{8,9},{9,8},{10,11... | collective-permute-start | bytes 786440 | tf_op jit(solution)/shard_map/ppermute | solution.py:22
  104.9 7.7 %collective-permute-start.25 = (bf16[32,4096]{1,0:T(8,128)(2,1)S(1)}, bf16[32,4096]{1,0:T(8,128)(2,1)S(1)}, u32[]{:S(2)}, u32[]{:S(2)}) collective-permute-start(bf16[32,4096]{1,0:T(8,128)(2,1)S(1)} %get-tuple-element.121), channel_id=1, source_target_pairs={{0,2},{1,3},{2,4},{3,5},{4,6},{5,7},{6,0},{7,1},{8,10},{9,11},{10,... | collective-permute-start | bytes 786440 | tf_op jit(solution)/shard_map/ppermute | solution.py:18
  105.8 6.8 %collective-permute-start.26 = (bf16[32,4096]{1,0:T(8,128)(2,1)S(1)}, bf16[32,4096]{1,0:T(8,128)(2,1)S(1)}, u32[]{:S(2)}, u32[]{:S(2)}) collective-permute-start(bf16[32,4096]{1,0:T(8,128)(2,1)S(1)} %get-tuple-element.122), channel_id=1, source_target_pairs={{0,6},{1,7},{2,0},{3,1},{4,2},{5,3},{6,4},{7,5},{8,14},{9,15},{10,... | collective-permute-start | bytes 786440 | tf_op jit(solution)/shard_map/ppermute | solution.py:18
  (2 other events, 17.9 us)
